TPU v7x, 32 devices: a whole 2x2x4 slice. The times are simulated.
32 devices in a mesh: grp: 4 (over x, core), row: 8 (over z, y).
Axes of the slice: x: 2, y: 2, z: 4, core: 2. Of those that a mesh axis runs over, the one named last changes fastest.
Arguments:
- pixels: bfloat16 [4, 8, 128, 202, 256], P('grp', 'row'), may hold values from -6 to 6
- wave_table: float32 [256], replicated, may hold values from 0.4 to 2.5
- wave_weight: bfloat16 [128, 128], replicated, may hold values from -0.5 to 0.5
- wave_bias: float32 [128], replicated, may hold values from -3 to 3
- gen_weight: bfloat16 [32768, 768], P('row'), may hold values from -0.01171875 to 0.01171875
- patch_bias: float32 [768], replicated, may hold values from -2 to 2
- norm1_gain: float32 [768], replicated, may hold values from 0.5 to 1.5
- norm1_bias: float32 [768], replicated, may hold values from -2 to 2
- qkv_weight: bfloat16 [768, 2304], P('row'), may hold values from -0.21875 to 0.21875
- query_bias: float32 [768], replicated, may hold values from -2 to 2
- value_bias: float32 [768], replicated, may hold values from -2 to 2
- out_weight: bfloat16 [768, 768], P('row'), may hold values from -0.875 to 0.875
- out_bias: float32 [768], replicated, may hold values from -2 to 2
- norm2_gain: float32 [768], replicated, may hold values from 0.5 to 1.5
- norm2_bias: float32 [768], replicated, may hold values from -2 to 2
- fc1_weight: bfloat16 [768, 3072], P('row'), may hold values from -0.21875 to 0.21875
- fc1_bias: float32 [3072], replicated, may hold values from -2 to 2
- fc2_weight: bfloat16 [3072, 768], P('row'), may hold values from -0.109375 to 0.109375
- fc2_bias: float32 [768], replicated, may hold values from -2 to 2
- band_count: int32 [4], P('grp'), may hold values from 2 to 202, as said below
- band_table: int32 [4, 202], P('grp'), may hold values from 0 to 255
- cotangent: bfloat16 [4, 8, 128, 768], P('grp', 'row'), may hold values from -6 to 6
Outputs:
- block_out: bfloat16 [4, 8, 128, 768], P('grp', 'row')
- pixel_grad: bfloat16 [4, 8, 128, 202, 256], P('grp', 'row')
- wave_weight_grad: float32 [128, 128], replicated
- wave_bias_grad: float32 [128], replicated
- gen_weight_grad: float32 [32768, 768], P('row')
- patch_bias_grad: float32 [768], replicated
- norm1_gain_grad: float32 [768], replicated
- norm1_bias_grad: float32 [768], replicated
- qkv_weight_grad: float32 [768, 2304], P('row')
- query_bias_grad: float32 [768], replicated
- value_bias_grad: float32 [768], replicated
- out_weight_grad: float32 [768, 768], P('row')
- out_bias_grad: float32 [768], replicated
- norm2_gain_grad: float32 [768], replicated
- norm2_bias_grad: float32 [768], replicated
- fc1_weight_grad: float32 [768, 3072], P('row')
- fc1_bias_grad: float32 [3072], replicated
- fc2_weight_grad: float32 [3072, 768], P('row')
- fc2_bias_grad: float32 [768], replicated
Inputs may be any that keep to these rules, and one draw needn't show every extreme that they name: `band_count`: each group's number of live band slots; some group uses all 202. `band_table`: entries of wave_table.
All inputs are finite; a program needn't handle non-finite values.
Results may differ from a plain program's by a relative error of at most 0.019.
Values may be sent and summed in bfloat16 or wider, within the bound.
No kernel may reach another device: no remote copies, remote signals or barrier semaphores. Data moves between devices by JAX's collectives and lax.ppermute only.
A program may use at most 384 MiB of HBM per device.

v0:
```python
import jax
import jax.numpy as jnp
from jax import lax
from jax.sharding import PartitionSpec as P

HEADS = 12


highest = lax.Precision.HIGHEST
epsilon = 1e-06


def sincos(angles_in, out_width):
    half_width = out_width // 2
    freqs = 1.0 / 10000.0 ** (jnp.arange(half_width).astype(angles_in.dtype) * (2.0 / out_width))
    angles = angles_in[:, None] * freqs[None, :]
    return jnp.concatenate([jnp.sin(angles), jnp.cos(angles)], axis=1)


def layer_norm(inputs, gain, shift):
    center = inputs - jnp.mean(inputs, axis=-1, keepdims=True)
    spread = jnp.mean(center * center, axis=-1, keepdims=True)
    return center * lax.rsqrt(spread + epsilon) * gain + shift


def dense_dot(left, right):
    return jnp.dot(left, right, preferred_element_type=jnp.float32)


def left_dot(left, right):
    return lax.dot_general(
        left, right, (((0,), (0,)), ((), ())), preferred_element_type=jnp.float32
    )


def right_dot(left, right):
    return lax.dot_general(
        left, right, (((1,), (1,)), ((), ())), preferred_element_type=jnp.float32
    )


def row_total(values):
    return jnp.sum(values.astype(jnp.float32), axis=0)


def body(
    pixels,
    wave_table,
    wave_weight,
    wave_bias,
    gen_weight,
    patch_bias,
    norm1_gain,
    norm1_bias,
    qkv_weight,
    query_bias,
    value_bias,
    out_weight,
    out_bias,
    norm2_gain,
    norm2_bias,
    fc1_weight,
    fc1_bias,
    fc2_weight,
    fc2_bias,
    band_count,
    band_table,
    cotangent,
):
    tile_count, seq_len, band_slots, pixel_count = pixels.shape[1:]
    model_width = gen_weight.shape[1]
    wave_width = wave_weight.shape[0]
    head_size = model_width // HEADS
    score_scale = head_size ** (-0.5)
    row_count = tile_count * seq_len
    head_shape = (tile_count, seq_len, HEADS, head_size)
    pixel_rows = pixels.reshape(row_count, band_slots, pixel_count)
    onehot = (band_table[0][:, None] == jnp.arange(wave_table.shape[0])[None, :]).astype(
        jnp.float32
    )
    wavelength = jnp.dot(onehot, wave_table, precision=highest)
    wave_embed = sincos(wavelength * 1000.0, wave_width)
    live = (jnp.arange(band_slots) < band_count[0]).astype(jnp.float32)[:, None]

    def hyper_fn(weight, bias):
        return jax.nn.gelu(jnp.dot(wave_embed, weight, precision=highest) + bias) * live

    hyper, hyper_back = jax.vjp(hyper_fn, wave_weight.astype(jnp.float32), wave_bias)
    hyper_low = hyper.astype(jnp.bfloat16)
    patches = jnp.einsum("bk,rbp->rkp", hyper_low, pixel_rows, preferred_element_type=jnp.float32)
    patches = patches.astype(jnp.bfloat16).reshape(row_count, wave_width * pixel_count)
    position = sincos(jnp.arange(seq_len).astype(jnp.float32), model_width)
    columns = patches
    projected = dense_dot(columns, lax.all_gather(gen_weight, "row", axis=0, tiled=True))
    embedded = (projected + patch_bias).reshape(tile_count, seq_len, model_width) + position
    embedded = embedded.reshape(row_count, model_width)
    w_qkv, w_out, w_fc1, w_fc2 = (
        lax.all_gather(qkv_weight, "row", axis=0, tiled=True),
        lax.all_gather(out_weight, "row", axis=0, tiled=True),
        lax.all_gather(fc1_weight, "row", axis=0, tiled=True),
        lax.all_gather(fc2_weight, "row", axis=0, tiled=True),
    )

    def front(inputs):
        normed = layer_norm(inputs, norm1_gain, norm1_bias).astype(jnp.bfloat16)
        mixed = dense_dot(normed, w_qkv)
        queries = (mixed[:, :model_width] + query_bias).astype(jnp.bfloat16).reshape(head_shape)
        key_rows = mixed[:, model_width : 2 * model_width].astype(jnp.bfloat16).reshape(head_shape)
        value_rows = (
            (mixed[:, 2 * model_width :] + value_bias).astype(jnp.bfloat16).reshape(head_shape)
        )
        return (normed, queries, key_rows, value_rows)

    def scores_of(queries, key_rows):
        return (
            jnp.einsum("tqhd,tkhd->thqk", queries, key_rows, preferred_element_type=jnp.float32)
            * score_scale
        )

    def attend(probs, value_rows):
        mixed_heads = jnp.einsum(
            "thqk,tkhd->tqhd", probs, value_rows, preferred_element_type=jnp.float32
        )
        return mixed_heads.astype(jnp.bfloat16).reshape(row_count, model_width)

    def back_half(inputs, attended):
        middle = inputs + dense_dot(attended, w_out) + out_bias
        normed_two = layer_norm(middle, norm2_gain, norm2_bias).astype(jnp.bfloat16)
        fc_pre = dense_dot(normed_two, w_fc1) + fc1_bias
        hidden = jax.nn.gelu(fc_pre).astype(jnp.bfloat16)
        return (middle, normed_two, fc_pre, hidden)

    normed, queries, key_rows, value_rows = front(embedded)
    scores = scores_of(queries, key_rows)
    log_total = jax.nn.logsumexp(scores, axis=-1, keepdims=True)
    attended = attend(jnp.exp(scores - log_total).astype(jnp.bfloat16), value_rows)
    middle, normed_two, fc_pre, hidden = back_half(embedded, attended)
    block_out = middle + dense_dot(hidden, w_fc2) + fc2_bias
    grad_out = cotangent.reshape(row_count, model_width)
    normed, queries, key_rows, value_rows = front(embedded)
    probs_full = jnp.exp(scores_of(queries, key_rows) - log_total)
    probs = probs_full.astype(jnp.bfloat16)
    attended = attend(probs, value_rows)
    middle, normed_two, fc_pre, hidden = back_half(embedded, attended)
    fc2_bias_part = row_total(grad_out)
    fc2_grad = left_dot(hidden, grad_out)
    grad_hidden = right_dot(grad_out, w_fc2)
    grad_pre = jax.vjp(jax.nn.gelu, fc_pre)[1](grad_hidden)[0].astype(jnp.bfloat16)
    fc1_bias_part = row_total(grad_pre)
    fc1_grad = left_dot(normed_two, grad_pre)
    grad_normed_two = right_dot(grad_pre, w_fc1)
    norm_two_back = jax.vjp(layer_norm, middle, norm2_gain, norm2_bias)[1]
    grad_middle, norm2_gain_part, norm2_bias_part = norm_two_back(grad_normed_two)
    grad_middle = grad_middle + grad_out.astype(jnp.float32)
    grad_branch = grad_middle.astype(jnp.bfloat16)
    out_bias_part = row_total(grad_branch)
    out_grad = left_dot(attended, grad_branch)
    grad_attended = right_dot(grad_branch, w_out).astype(jnp.bfloat16).reshape(head_shape)
    grad_probs = jnp.einsum(
        "tqhd,tkhd->thqk", grad_attended, value_rows, preferred_element_type=jnp.float32
    )
    grad_scores = probs_full * (
        grad_probs - jnp.sum(probs_full * grad_probs, axis=-1, keepdims=True)
    )
    grad_scores = grad_scores.astype(jnp.bfloat16)
    grad_queries = (
        jnp.einsum("thqk,tkhd->tqhd", grad_scores, key_rows, preferred_element_type=jnp.float32)
        * score_scale
    ).astype(jnp.bfloat16)
    grad_keys = (
        jnp.einsum("thqk,tqhd->tkhd", grad_scores, queries, preferred_element_type=jnp.float32)
        * score_scale
    ).astype(jnp.bfloat16)
    grad_values = jnp.einsum(
        "thqk,tqhd->tkhd", probs, grad_attended, preferred_element_type=jnp.float32
    ).astype(jnp.bfloat16)
    grad_queries = grad_queries.reshape(row_count, model_width)
    grad_values = grad_values.reshape(row_count, model_width)
    grad_mixed = jnp.concatenate(
        [grad_queries, grad_keys.reshape(row_count, model_width), grad_values], axis=1
    )
    query_bias_part = row_total(grad_queries)
    value_bias_part = row_total(grad_values)
    qkv_grad = left_dot(normed, grad_mixed)
    grad_normed = right_dot(grad_mixed, w_qkv)
    norm_one_back = jax.vjp(layer_norm, embedded, norm1_gain, norm1_bias)[1]
    grad_from_norm, norm1_gain_part, norm1_bias_part = norm_one_back(grad_normed)
    grad_embedded = (grad_middle + grad_from_norm).astype(jnp.bfloat16)
    patch_bias_part = row_total(grad_embedded)
    grad_patches = right_dot(
        grad_embedded, lax.all_gather(gen_weight, "row", axis=0, tiled=True)
    ).astype(jnp.bfloat16)
    grad_cube = grad_patches.reshape(row_count, wave_width, pixel_count)
    pixel_grad = jnp.einsum(
        "rkp,bk->rbp", grad_cube, hyper_low, preferred_element_type=jnp.float32
    ).astype(jnp.bfloat16)
    grad_hyper = jnp.einsum(
        "rkp,rbp->bk", grad_cube, pixel_rows, preferred_element_type=jnp.float32
    )
    wave_weight_part, wave_bias_part = hyper_back(grad_hyper)
    columns = patches
    gen_part = lax.psum_scatter(
        left_dot(columns, grad_embedded), "row", scatter_dimension=0, tiled=True
    )
    qkv_share, out_share, fc1_share, fc2_share = (
        lax.psum_scatter(qkv_grad, "row", scatter_dimension=0, tiled=True),
        lax.psum_scatter(out_grad, "row", scatter_dimension=0, tiled=True),
        lax.psum_scatter(fc1_grad, "row", scatter_dimension=0, tiled=True),
        lax.psum_scatter(fc2_grad, "row", scatter_dimension=0, tiled=True),
    )
    gen_total, qkv_total, out_total, fc1_total, fc2_total = (
        lax.psum(gen_part.astype(jnp.bfloat16), "grp").astype(jnp.float32),
        lax.psum(qkv_share.astype(jnp.bfloat16), "grp").astype(jnp.float32),
        lax.psum(out_share.astype(jnp.bfloat16), "grp").astype(jnp.float32),
        lax.psum(fc1_share.astype(jnp.bfloat16), "grp").astype(jnp.float32),
        lax.psum(fc2_share.astype(jnp.bfloat16), "grp").astype(jnp.float32),
    )
    small_totals = lax.psum(
        (
            wave_weight_part,
            wave_bias_part,
            patch_bias_part,
            norm1_gain_part,
            norm1_bias_part,
            query_bias_part,
            value_bias_part,
            out_bias_part,
            norm2_gain_part,
            norm2_bias_part,
            fc1_bias_part,
            fc2_bias_part,
        ),
        ("grp", "row"),
    )
    (
        wave_weight_total,
        wave_bias_total,
        patch_bias_total,
        norm1_gain_total,
        norm1_bias_total,
        query_bias_total,
        value_bias_total,
        out_bias_total,
        norm2_gain_total,
        norm2_bias_total,
        fc1_bias_total,
        fc2_bias_total,
    ) = small_totals
    block_result = block_out.astype(jnp.bfloat16).reshape(1, tile_count, seq_len, model_width)
    pixel_result = pixel_grad.reshape(1, tile_count, seq_len, band_slots, pixel_count)
    return (
        block_result,
        pixel_result,
        wave_weight_total,
        wave_bias_total,
        gen_total,
        patch_bias_total,
        norm1_gain_total,
        norm1_bias_total,
        qkv_total,
        query_bias_total,
        value_bias_total,
        out_total,
        out_bias_total,
        norm2_gain_total,
        norm2_bias_total,
        fc1_total,
        fc1_bias_total,
        fc2_total,
        fc2_bias_total,
    )


def solution(mesh):
    return jax.shard_map(
        body,
        mesh=mesh,
        in_specs=(
            P("grp", "row", None, None, None),
            P(),
            P(),
            P(),
            P("row", None),
            P(),
            P(),
            P(),
            P("row", None),
            P(),
            P(),
            P("row", None),
            P(),
            P(),
            P(),
            P("row", None),
            P(),
            P("row", None),
            P(),
            P("grp"),
            P("grp", None),
            P("grp", "row", None, None),
        ),
        out_specs=(
            P("grp", "row", None, None),
            P("grp", "row", None, None, None),
            P(),
            P(),
            P("row", None),
            P(),
            P(),
            P(),
            P("row", None),
            P(),
            P(),
            P("row", None),
            P(),
            P(),
            P(),
            P("row", None),
            P(),
            P("row", None),
            P(),
        ),
        check_vma=False,
    )
```

profile of v0, /device:TPU:0, one launch (start us, length us, event | category | flops | bytes accessed | tf_op | source)
XLA Modules:
  0.0 3608.7 jit_solution(8098353346987439397)
XLA Ops:
  13.1 17.1 fusion.4
  30.2 12.7 copy.84
  43.7 921.0 %all-gather.6.cloned.1.call-done = bf16[32768,768]{1,0:T(8,128)(2,1)} async-done(((bf16[4096,768]{1,0:T(8,128)(2,1)}), bf16[32768,768]{1,0:T(8,128)(2,1)}) %all-gather.6.cloned.1.call-update) | async-done | bytes 50331664 | tf_op jit(solution)/shard_map/all_gather | solution.py:94
  964.6 21.0 fusion.68
  985.8 46.2 %all-gather.8.cloned.1.call-done = bf16[768,2304]{1,0:T(8,128)(2,1)} async-done(((bf16[96,2304]{1,0:T(8,128)(2,1)}), bf16[768,2304]{1,0:T(8,128)(2,1)}) %all-gather.8.cloned.1.call-update) | async-done | bytes 3538960 | tf_op jit(solution)/shard_map/all_gather | solution.py:98
  1032.0 2.7 fusion.63
  1036.2 37.6 %all-gather.10.cloned.1.call-done = bf16[768,768]{1,0:T(8,128)(2,1)} async-done(((bf16[96,768]{1,0:T(8,128)(2,1)}), bf16[768,768]{1,0:T(8,128)(2,1)}) %all-gather.10.cloned.1.call-update) | async-done | bytes 1179664 | tf_op jit(solution)/shard_map/all_gather | solution.py:99
  1073.8 1.7 fusion.70
  1075.7 78.8 %all-gather.12.cloned.1.call-done = bf16[768,3072]{1,0:T(8,128)(2,1)} async-done(((bf16[96,3072]{1,0:T(8,128)(2,1)}), bf16[768,3072]{1,0:T(8,128)(2,1)}) %all-gather.12.cloned.1.call-update) | async-done | bytes 4718608 | tf_op jit(solution)/shard_map/all_gather | solution.py:100
  1154.5 3.2 convolution_add_fusion
  1157.7 76.9 %all-gather.14.cloned.1.call-done = bf16[3072,768]{1,0:T(8,128)(2,1)} async-done(((bf16[384,768]{1,0:T(8,128)(2,1)}), bf16[3072,768]{1,0:T(8,128)(2,1)}) %all-gather.14.cloned.1.call-update) | async-done | bytes 4718608 | tf_op jit(solution)/shard_map/all_gather | solution.py:101
  1234.6 4.4 convert_reduce_fusion
  1239.1 1.8 multiply_reduce_fusion.1
  1242.7 1.9 fusion.73
  1244.7 2.6 convolution_convert_fusion.2
  1247.3 1.7 copy.74
  1249.0 1.4 multiply_reduce_fusion
  1252.9 4.2 fusion.34
  1257.3 5.3 fusion.37
  1262.7 1.1 copy-done.6
  1263.8 5.2 fusion.64
  1270.0 3.6 multiply_reduce_fusion.2
  1274.0 37.4 %fusion.72 = f32[32768,768]{1,0:T(8,128)} fusion(bf16[128,32768]{1,0:T(8,128)(2,1)} %bitcast.111, bf16[128,768]{1,0:T(8,128)(2,1)S(1)} %get-tuple-element.101), kind=kOutput, calls=%fused_computation.123 | convolution fusion | flops 6442450944 | bytes 109248512 | tf_op jit(solution)/shard_map/dot_general | solution.py:31
  1311.9 1.6 convert_element_type.228
  1313.6 130.1 %reduce-scatter.8.cloned.1.call-done = f32[96,2304]{1,0:T(8,128)} async-done(((f32[768,2304]{1,0:T(8,128)}), f32[96,2304]{1,0:T(8,128)}) %reduce-scatter.8.cloned.1.call-update) | async-done | bytes 884752 | tf_op jit(solution)/shard_map/reduce_scatter | solution.py:206
  1443.7 2.0 convert_element_type.224
  1445.6 165.2 %reduce-scatter.14.cloned.1.call-done = f32[384,768]{1,0:T(8,128)} async-done(((f32[3072,768]{1,0:T(8,128)}), f32[384,768]{1,0:T(8,128)}) %reduce-scatter.14.cloned.1.call-update) | async-done | bytes 1179664 | tf_op jit(solution)/shard_map/reduce_scatter | solution.py:209
  1610.8 2.1 convert_element_type.234
  1613.0 165.0 %reduce-scatter.12.cloned.1.call-done = f32[96,3072]{1,0:T(8,128)} async-done(((f32[768,3072]{1,0:T(8,128)}), f32[96,3072]{1,0:T(8,128)}) %reduce-scatter.12.cloned.1.call-update) | async-done | bytes 1179664 | tf_op jit(solution)/shard_map/reduce_scatter | solution.py:208
  1778.0 2.2 convert_element_type.231
  1780.1 1538.6 %reduce-scatter.16.cloned.1.call-done = f32[4096,768]{1,0:T(8,128)} async-done(((f32[32768,768]{1,0:T(8,128)}), f32[4096,768]{1,0:T(8,128)}) %reduce-scatter.16.cloned.1.call-update) | async-done | bytes 12582928
  3318.7 7.7 convert_element_type.221
  3326.5 24.3 convolution_convert_fusion
  3350.8 9.4 copy.85
  3360.2 27.6 fusion.71
  3387.8 1.1 fusion.56
  3388.9 10.6 convert_bitcast_fusion
  3399.5 4.1 fusion.20
  3403.7 21.0 copy.79
  3424.7 41.4 %all-reduce.1 = (f32[128]{0:T(128)}, f32[768]{0:T(1024)}, f32[768]{0:T(1024)}, f32[768]{0:T(1024)}, f32[768]{0:T(1024)}, /*index=5*/f32[768]{0:T(1024)}, f32[768...) all-reduce(f32[128]{0:T(128)S(1)} %get-tuple-element.123, ...), channel_id=1, replica_groups=mesh['grp'=4,'row'=8] {'grp','row'}, use_global_device_ids=true, to_apply=%region_13.0 | all-reduce | flops 10112 | bytes 80896 | tf_op jit(solution)/shard_map/psum | solution.py:218
  3466.2 10.0 all-reduce.8.cloned.1.call-done
  3476.2 1.7 convert_element_type.229
  3477.9 2.0 convert_element_type.225
  3480.0 1.1 convert_element_type.232
  3481.1 1.1 convert_element_type.235
  3482.2 8.6 convert_element_type.222
  3490.7 109.2 %all-reduce.6.cloned.1.call-done = f32[128,128]{1,0:T(8,128)} async-done(((f32[128,128]{1,0:T(8,128)}), f32[128,128]{1,0:T(8,128)}) %all-reduce.6.cloned.1.call-update) | async-done | bytes 65552 | tf_op jit(solution)/shard_map/psum | solution.py:218
  3599.9 1.5 copy.109
  (153 shorter events, 14.2 us)
Async XLA Ops:
  7.2 5.6 copy-start
  7.2 957.4 %all-gather.6.cloned.1.call-start = ((), (), s32[]{:S(2)}) async-start(), calls=%async_computation.5 | async-start | bytes 56623104 | tf_op jit(solution)/shard_map/all_gather | solution.py:94
  7.9 3.4 copy-start.43
  8.0 3.4 copy-start.44
  8.0 4.8 copy-start.41
  8.0 1024.0 %all-gather.8.cloned.1.call-start = ((), (), s32[]{:S(2)}) async-start(), calls=%async_computation.6 | async-start | bytes 3981312 | tf_op jit(solution)/shard_map/all_gather | solution.py:98
  8.7 1065.0 %all-gather.10.cloned.1.call-start = ((), (), s32[]{:S(2)}) async-start(), calls=%async_computation.7 | async-start | bytes 1327104 | tf_op jit(solution)/shard_map/all_gather | solution.py:99
  9.5 1145.0 %all-gather.12.cloned.1.call-start = ((), (), s32[]{:S(2)}) async-start(), calls=%async_computation.8 | async-start | bytes 5308416 | tf_op jit(solution)/shard_map/all_gather | solution.py:100
  10.0 1224.6 %all-gather.14.cloned.1.call-start = ((), (), s32[]{:S(2)}) async-start(), calls=%async_computation.9 | async-start | bytes 5308416 | tf_op jit(solution)/shard_map/all_gather | solution.py:101
  10.6 1301.3 %reduce-scatter.10.cloned.1.call-start = ((), (), s32[]{:S(2)}) async-start(), calls=%async_computation.12 | async-start | bytes 2654208 | tf_op jit(solution)/shard_map/reduce_scatter | solution.py:207
  11.3 18.8 copy-start.39
  13.1 17.1 copy-start.17
  30.2 934.5 %copy-start.35 = (f32[768]{0:T(1024)S(1)}, f32[768]{0:T(1024)}, u32[]{:S(2)}) copy-start(f32[768]{0:T(1024)} %param.27) | copy-start | bytes 9220
  964.6 67.4 %copy-start.31 = (f32[768]{0:T(1024)S(1)}, f32[768]{0:T(1024)}, u32[]{:S(2)}) copy-start(f32[768]{0:T(1024)} %param.28) | copy-start | bytes 9220
  964.6 67.4 %copy-start.33 = (f32[768]{0:T(1024)S(1)}, f32[768]{0:T(1024)}, u32[]{:S(2)}) copy-start(f32[768]{0:T(1024)} %param.29) | copy-start | bytes 9220
  985.8 48.9 %copy-start.36 = (f32[768]{0:T(1024)S(1)}, f32[768]{0:T(1024)}, u32[]{:S(2)}) copy-start(f32[768]{0:T(1024)} %param.31) | copy-start | bytes 9220
  985.8 48.9 %copy-start.37 = (f32[768]{0:T(1024)S(1)}, f32[768]{0:T(1024)}, u32[]{:S(2)}) copy-start(f32[768]{0:T(1024)} %param.32) | copy-start | bytes 9220
  1035.0 1.1 copy-start.10
  1035.1 1.0 copy-start.8
  1035.3 38.4 %copy-start.38 = (f32[768]{0:T(1024)S(1)}, f32[768]{0:T(1024)}, u32[]{:S(2)}) copy-start(f32[768]{0:T(1024)} %param.34) | copy-start | bytes 9220
  1036.1 39.6 %copy-start.12 = (bf16[12,64,128]{2,1,0:T(8,128)(2,1)}, bf16[12,64,128]{2,1,0:T(8,128)(2,1)S(1)}, u32[]{:S(2)}) copy-start(bf16[12,64,128]{2,1,0:T(8,128)(2,1)S(1)} %convolution_convert_fusion.3) | copy-start | bytes 589828
  1036.1 118.4 %copy-start.30 = (f32[768]{0:T(1024)S(1)}, f32[768]{0:T(1024)}, u32[]{:S(2)}) copy-start(f32[768]{0:T(1024)} %param.35) | copy-start | bytes 9220
  1036.1 118.4 %copy-start.32 = (f32[768]{0:T(1024)S(1)}, f32[768]{0:T(1024)}, u32[]{:S(2)}) copy-start(f32[768]{0:T(1024)} %param.36) | copy-start | bytes 9220
  1036.2 118.3 %copy-start.34 = (f32[3072]{0:T(1024)S(1)}, f32[3072]{0:T(1024)}, u32[]{:S(2)}) copy-start(f32[3072]{0:T(1024)} %param.38) | copy-start | bytes 36868
  1075.7 158.9 %copy-start.7 = (bf16[1,1,128,768]{3,2,1,0:T(8,128)(2,1)S(1)}, bf16[1,1,128,768]{3,2,1,0:T(8,128)(2,1)}, u32[]{:S(2)}) copy-start(bf16[1,1,128,768]{3,2,1,0:T(8,128)(2,1)} %param.43) | copy-start | bytes 589828
  1234.6 4.5 copy-start.2
  1239.0 1.8 copy-start.5
  1240.9 1.8 copy-start.13
  1244.6 199.0 %reduce-scatter.8.cloned.1.call-start = ((), (), s32[]{:S(2)}) async-start(), calls=%async_computation.11 | async-start | bytes 7962624 | tf_op jit(solution)/shard_map/reduce_scatter | solution.py:206
  1249.0 1.7 copy-start.11
  1250.5 0.9 copy-start.9
  1250.5 1.3 copy-start.15
  1257.1 353.7 %reduce-scatter.14.cloned.1.call-start = ((), (), s32[]{:S(2)}) async-start(), calls=%async_computation.14 | async-start | bytes 10616832 | tf_op jit(solution)/shard_map/reduce_scatter | solution.py:209
  1262.6 1.2 copy-start.6
  1262.6 515.3 %reduce-scatter.12.cloned.1.call-start = ((), (), s32[]{:S(2)}) async-start(), calls=%async_computation.13 | async-start | bytes 10616832 | tf_op jit(solution)/shard_map/reduce_scatter | solution.py:208
  1269.0 1.0 copy-start.26
  1269.0 4.8 copy-start.4
  1269.1 2049.6 %reduce-scatter.16.cloned.1.call-start = ((), (), s32[]{:S(2)}) async-start(), calls=%async_computation.15 | async-start | bytes 113246208
  1311.5 2164.7 %all-reduce.8.cloned.1.call-start = ((), (), s32[]{:S(2)}) async-start(), calls=%async_computation.16 | async-start | bytes 16121856 | tf_op jit(solution)/shard_map/psum | solution.py:212
  3326.5 273.4 %all-reduce.6.cloned.1.call-start = ((), (), s32[]{:S(2)}) async-start(), calls=%async_computation.10 | async-start | bytes 131072 | tf_op jit(solution)/shard_map/psum | solution.py:218
  3350.8 9.4 copy-start.18
  3350.8 9.4 copy-start.40
  3360.2 27.6 copy-start.20
  3360.2 27.6 copy-start.22
  3388.9 10.6 copy-start.42
  3476.2 3.8 copy-start.29
  3477.9 3.2 copy-start.28
  3482.2 119.2 %copy-start.1 = (bf16[128,128]{1,0:T(8,128)(2,1)S(1)}, bf16[128,128]{1,0:T(8,128)(2,1)}, u32[]{:S(2)}) copy-start(bf16[128,128]{1,0:T(8,128)(2,1)} %param.24) | copy-start | bytes 98308
  (9 other events, 6.9 us)
Sparse Core Ops, SparseCore 0:
  9.6 955.0 all-gather.5
  966.8 65.1 all-gather.7
  1034.2 39.5 all-gather.9
  1075.8 78.6 all-gather.11
  1156.5 78.0 all-gather.13
  1244.7 67.1 reduce-scatter.9
  1315.6 128.0 reduce-scatter.7
  1448.3 162.5 reduce-scatter.13
  1615.4 162.5 reduce-scatter.11
  1782.2 1536.4 reduce-scatter.15
  3326.6 149.5 all-reduce.7
  3482.2 117.6 all-reduce.5
where the time goes:
time: 3620 us; the launch traced here: 3610 us
  waiting for transfers between devices  3280 us (91%)
  matrix products  183 us (5%)
  local copies, waits for them, and re-layouts  52.2 us (1%)
  blocking collectives  41.4 us (1%)
    unnamed x13, waiting for transfers between devices  1540 us
    all_gather x1, waiting for transfers between devices, body(): lax.all_gather(gen_weight, 'row', axis=0, tiled=True)  921 us
    reduce_scatter x1, waiting for transfers between devices, body(): lax.psum_scatter(fc2_grad, 'row', scatter_dimension=0, tiled=True)  165 us
    reduce_scatter x1, waiting for transfers between devices, body(): lax.psum_scatter(fc1_grad, 'row', scatter_dimension=0, tiled=True)  165 us
    reduce_scatter x1, waiting for transfers between devices, body(): lax.psum_scatter(qkv_grad, 'row', scatter_dimension=0, tiled=True)  130 us
    psum x1, waiting for transfers between devices, body(): lax.psum((wave_weight_part, wave_bias_part, patch_bias_part, norm1_gain_p...  109 us
    all_gather x1, waiting for transfers between devices, body(): lax.all_gather(fc1_weight, 'row', axis=0, tiled=True)  78.8 us
    all_gather x1, waiting for transfers between devices, body(): lax.all_gather(fc2_weight, 'row', axis=0, tiled=True)  76.9 us
  transfers between devices with their start and end apart: 12, of which 12 were waited for; matrix products, arithmetic and copies ran while one was open for 7% of the time, Pallas kernels for 0%

commit v1 on v0

v1 whole, which is shorter than its diff:
```python
import jax
import jax.numpy as jnp
from jax import lax
from jax.experimental import pallas as pl
from jax.experimental.pallas import tpu as pltpu
from jax.sharding import Mesh
from jax.sharding import PartitionSpec as P

HEADS = 12

bf16 = jnp.bfloat16
f32 = jnp.float32
highest = lax.Precision.HIGHEST
epsilon = 1e-06

AXES = ("x", "c", "z", "y")
VMEM_LIMIT = 48 * 1024 * 1024
MIX_ROWS = 16
GEN_STEP = 4


def sincos(angles_in, out_width):
    half_width = out_width // 2
    freqs = 1.0 / 10000.0 ** (jnp.arange(half_width).astype(angles_in.dtype) * (2.0 / out_width))
    angles = angles_in[:, None] * freqs[None, :]
    return jnp.concatenate([jnp.sin(angles), jnp.cos(angles)], axis=1)


def layer_norm(inputs, gain, shift):
    center = inputs - jnp.mean(inputs, axis=-1, keepdims=True)
    spread = jnp.mean(center * center, axis=-1, keepdims=True)
    return center * lax.rsqrt(spread + epsilon) * gain + shift


def dense_dot(left, right):
    return jnp.dot(left, right, preferred_element_type=f32)


def left_dot(left, right):
    return lax.dot_general(left, right, (((0,), (0,)), ((), ())), preferred_element_type=f32)


def right_dot(left, right):
    return lax.dot_general(left, right, (((1,), (1,)), ((), ())), preferred_element_type=f32)


def row_total(values):
    return jnp.sum(values.astype(f32), axis=0)


def mix_kernel(hyper_ref, pix_ref, out_a, out_b, out_c, out_d, scratch):
    rows = pix_ref.shape[0]
    entries = hyper_ref.shape[0]
    half = pix_ref.shape[2] // 2
    for r in range(rows):
        mixed = dense_dot(hyper_ref[...], pix_ref[r])
        for h in range(2):
            scratch[h, pl.ds(r, entries, stride=rows), :] = mixed[:, h * half : (h + 1) * half]
    for j, out in enumerate((out_a, out_b, out_c, out_d)):
        share = out.shape[0]
        for h in range(2):
            part = scratch[h, j * share * rows : (j + 1) * share * rows, :]
            out[:, :, h * half : (h + 1) * half] = part.reshape(share, rows, half).astype(bf16)


def mix_pixels(hyper_t, pixel_rows):
    entries = hyper_t.shape[0]
    row_count, slots, pixel_count = pixel_rows.shape
    share = entries // 4
    out = jax.ShapeDtypeStruct((share, row_count, pixel_count), bf16)
    return pl.pallas_call(
        mix_kernel,
        grid=(row_count // MIX_ROWS,),
        in_specs=[
            pl.BlockSpec((entries, slots), lambda i: (0, 0)),
            pl.BlockSpec((MIX_ROWS, slots, pixel_count), lambda i: (i, 0, 0)),
        ],
        out_specs=[pl.BlockSpec((share, MIX_ROWS, pixel_count), lambda i: (0, i, 0))] * 4,
        out_shape=[out] * 4,
        scratch_shapes=[pltpu.VMEM((2, entries * MIX_ROWS, pixel_count // 2), f32)],
        compiler_params=pltpu.CompilerParams(vmem_limit_bytes=VMEM_LIMIT),
        cost_estimate=pl.CostEstimate(
            flops=2 * row_count * slots * pixel_count * entries,
            bytes_accessed=2 * row_count * pixel_count * (slots + entries),
            transcendentals=0,
        ),
        name="mix_pixels",
    )(hyper_t, pixel_rows)


def halves(steps):
    first = lambda i: (jnp.minimum(i, steps - 1), 0, 0)
    second = lambda i: (jnp.maximum(i - steps, 0), 0, 0)
    return first, second


def project_kernel(a0, a1, a2, a3, w0, w1, out):
    i = pl.program_id(0)
    steps = pl.num_programs(0) // 2
    rows = a0.shape[1]

    @pl.when(i == 0)
    def _():
        out[...] = jnp.zeros_like(out)

    def add(w):
        for k in range(w.shape[0]):
            left = jnp.concatenate([a[k] for a in (a0, a1, a2, a3)], axis=0)
            out[...] += dense_dot(left, w[k])

    @pl.when(i < steps)
    def _():
        add(w0)

    @pl.when(i >= steps)
    def _():
        add(w1)


def project(parts, near, far):
    share, rows, pixel_count = parts[0].shape
    width = near.shape[2]
    steps = share // 2 // GEN_STEP
    first, second = halves(steps)
    return pl.pallas_call(
        project_kernel,
        grid=(2 * steps,),
        in_specs=[pl.BlockSpec((GEN_STEP, rows, pixel_count), lambda i: (i, 0, 0))] * 4
        + [
            pl.BlockSpec((GEN_STEP, pixel_count, width), first),
            pl.BlockSpec((GEN_STEP, pixel_count, width), second),
        ],
        out_specs=pl.BlockSpec((4 * rows, width), lambda i: (0, 0)),
        out_shape=jax.ShapeDtypeStruct((4 * rows, width), f32),
        compiler_params=pltpu.CompilerParams(vmem_limit_bytes=VMEM_LIMIT),
        cost_estimate=pl.CostEstimate(
            flops=8 * share * rows * pixel_count * width,
            bytes_accessed=2 * share * pixel_count * (4 * rows + width),
            transcendentals=0,
        ),
        name="project",
    )(*parts, near, far)


def back_kernel(g, w0, w1, o0, o1, o2, o3):
    i = pl.program_id(0)
    steps = pl.num_programs(0) // 2
    rows = o0.shape[1]

    def work(w):
        for k in range(w.shape[0]):
            res = right_dot(g[...], w[k]).astype(bf16)
            for j, out in enumerate((o0, o1, o2, o3)):
                out[k] = res[j * rows : (j + 1) * rows]

    @pl.when(i < steps)
    def _():
        work(w0)

    @pl.when(i >= steps)
    def _():
        work(w1)


def back_patches(grads, near, far):
    share, pixel_count, width = 2 * near.shape[0], near.shape[1], near.shape[2]
    rows = grads.shape[0] // 4
    steps = share // 2 // GEN_STEP
    first, second = halves(steps)
    out = jax.ShapeDtypeStruct((share, rows, pixel_count), bf16)
    return pl.pallas_call(
        back_kernel,
        grid=(2 * steps,),
        in_specs=[
            pl.BlockSpec((4 * rows, width), lambda i: (0, 0)),
            pl.BlockSpec((GEN_STEP, pixel_count, width), first),
            pl.BlockSpec((GEN_STEP, pixel_count, width), second),
        ],
        out_specs=[pl.BlockSpec((GEN_STEP, rows, pixel_count), lambda i: (i, 0, 0))] * 4,
        out_shape=[out] * 4,
        compiler_params=pltpu.CompilerParams(vmem_limit_bytes=VMEM_LIMIT),
        cost_estimate=pl.CostEstimate(
            flops=8 * share * rows * pixel_count * width,
            bytes_accessed=2 * share * pixel_count * (4 * rows + width),
            transcendentals=0,
        ),
        name="back_patches",
    )(grads, near, far)


def gen_grad_kernel(a0, a1, a2, a3, g, out):
    for k in range(out.shape[0]):
        left = jnp.concatenate([a[k] for a in (a0, a1, a2, a3)], axis=0)
        out[k] = left_dot(left, g[...]).astype(bf16)


def gen_grad(parts, grads, which):
    share, rows, pixel_count = parts[0].shape
    width = grads.shape[1]
    steps = share // 2 // GEN_STEP
    return pl.pallas_call(
        gen_grad_kernel,
        grid=(steps,),
        in_specs=[pl.BlockSpec((GEN_STEP, rows, pixel_count), lambda i: (i + which * steps, 0, 0))] * 4
        + [pl.BlockSpec((4 * rows, width), lambda i: (0, 0))],
        out_specs=pl.BlockSpec((GEN_STEP, pixel_count, width), lambda i: (i, 0, 0)),
        out_shape=jax.ShapeDtypeStruct((share // 2, pixel_count, width), bf16),
        compiler_params=pltpu.CompilerParams(vmem_limit_bytes=VMEM_LIMIT),
        cost_estimate=pl.CostEstimate(
            flops=4 * share * rows * pixel_count * width,
            bytes_accessed=share * pixel_count * (4 * rows + width),
            transcendentals=0,
        ),
        name="gen_grad",
    )(*parts, grads)


def pixel_kernel(hyper_ref, pix_ref, g0, g1, g2, g3, grad_ref, total_ref, scratch):
    rows = pix_ref.shape[0]
    entries = hyper_ref.shape[1]
    half = pix_ref.shape[2] // 2

    @pl.when(pl.program_id(0) == 0)
    def _():
        total_ref[...] = jnp.zeros_like(total_ref)

    for j, g in enumerate((g0, g1, g2, g3)):
        share = g.shape[0]
        for h in range(2):
            part = g[:, :, h * half : (h + 1) * half].astype(f32)
            scratch[h, j * share * rows : (j + 1) * share * rows, :] = part.reshape(share * rows, half)
    total = total_ref[...]
    for r in range(rows):
        grad = jnp.concatenate(
            [scratch[h, pl.ds(r, entries, stride=rows), :] for h in range(2)], axis=1
        ).astype(bf16)
        grad_ref[r] = dense_dot(hyper_ref[...], grad).astype(bf16)
        total = total + right_dot(pix_ref[r], grad)
    total_ref[...] = total


def pixel_back(hyper, pixel_rows, parts):
    slots, entries = hyper.shape
    row_count, _, pixel_count = pixel_rows.shape
    share = entries // 4
    return pl.pallas_call(
        pixel_kernel,
        grid=(row_count // MIX_ROWS,),
        in_specs=[
            pl.BlockSpec((slots, entries), lambda i: (0, 0)),
            pl.BlockSpec((MIX_ROWS, slots, pixel_count), lambda i: (i, 0, 0)),
        ]
        + [pl.BlockSpec((share, MIX_ROWS, pixel_count), lambda i: (0, i, 0))] * 4,
        out_specs=[
            pl.BlockSpec((MIX_ROWS, slots, pixel_count), lambda i: (i, 0, 0)),
            pl.BlockSpec((slots, entries), lambda i: (0, 0)),
        ],
        out_shape=[
            jax.ShapeDtypeStruct((row_count, slots, pixel_count), bf16),
            jax.ShapeDtypeStruct((slots, entries), f32),
        ],
        scratch_shapes=[pltpu.VMEM((2, entries * MIX_ROWS, pixel_count // 2), f32)],
        compiler_params=pltpu.CompilerParams(vmem_limit_bytes=VMEM_LIMIT),
        cost_estimate=pl.CostEstimate(
            flops=4 * row_count * slots * pixel_count * entries,
            bytes_accessed=2 * row_count * pixel_count * (2 * slots + entries),
            transcendentals=0,
        ),
        name="pixel_back",
    )(hyper, pixel_rows, *parts)


PAIR = [(0, 1), (1, 0)]
CORNER = [(i, i ^ 3) for i in range(4)]


def swap_core(value):
    return lax.ppermute(value, "c", PAIR)


def swap_x(value):
    return lax.ppermute(value, "x", PAIR)


def swap_plane(values):
    return [
        values[0],
        lax.ppermute(values[1], "y", PAIR),
        lax.ppermute(values[2], "x", PAIR),
        lax.ppermute(values[3], ("x", "y"), CORNER),
    ]


def body(
    pixels,
    wave_table,
    wave_weight,
    wave_bias,
    gen_weight,
    patch_bias,
    norm1_gain,
    norm1_bias,
    qkv_weight,
    query_bias,
    value_bias,
    out_weight,
    out_bias,
    norm2_gain,
    norm2_bias,
    fc1_weight,
    fc1_bias,
    fc2_weight,
    fc2_bias,
    band_count,
    band_table,
    cotangent,
):
    tile_count, seq_len, band_slots, pixel_count = pixels.shape[1:]
    model_width = gen_weight.shape[1]
    wave_width = wave_weight.shape[0]
    hidden_width = fc1_weight.shape[1]
    head_size = model_width // HEADS
    score_scale = head_size ** (-0.5)
    row_count = tile_count * seq_len
    head_shape = (tile_count, seq_len, HEADS, head_size)
    z_size = lax.axis_size("z")
    row_size = 2 * z_size
    at_x, at_c, at_y = lax.axis_index("x"), lax.axis_index("c"), lax.axis_index("y")
    quarter = 2 * at_x + at_c
    shard = qkv_weight.shape[0]
    unit = hidden_width // row_size // 4

    gen_rows = gen_weight.shape[0] // 4
    own_rows = lax.dynamic_slice_in_dim(gen_weight, quarter * gen_rows, gen_rows, 0)

    attn_pieces = jnp.stack(
        [qkv_weight[:, j * model_width : (j + 1) * model_width] for j in range(3)] + [out_weight]
    )
    fc1_pieces = fc1_weight.reshape(shard, row_size, 4, unit).transpose(2, 0, 1, 3)
    fc1_pieces = fc1_pieces.reshape(4, shard, row_size * unit)
    fc2_pieces = fc2_weight.reshape(4, unit, model_width)
    own_pieces = jnp.stack(
        [
            lax.dynamic_index_in_dim(pieces, quarter, 0, keepdims=False)
            for pieces in (attn_pieces, fc1_pieces, fc2_pieces)
        ]
    )
    gathered = lax.all_gather(own_pieces, ("z", "y"), axis=0, tiled=False)
    gathered = gathered.transpose(1, 0, 2, 3).reshape(3, model_width, model_width)
    other_core = swap_core(gathered)
    blocks = [gathered, other_core, swap_x(gathered), swap_x(other_core)]
    attn_blocks = jnp.stack([block[0] for block in blocks])
    w_query, w_key, w_value, w_out = (
        lax.dynamic_index_in_dim(attn_blocks, j ^ quarter, 0, keepdims=False) for j in range(4)
    )
    w_qkv = jnp.concatenate([w_query, w_key, w_value], axis=1)
    w_fc1 = jnp.concatenate([block[1] for block in blocks], axis=1)
    w_fc2 = jnp.concatenate([block[2] for block in blocks], axis=0)
    near = lax.all_gather(own_rows, "z", axis=0, tiled=True)
    far = swap_core(near)
    near = near.reshape(-1, pixel_count, model_width)
    far = far.reshape(-1, pixel_count, model_width)

    unit_order = fc1_bias.reshape(row_size, 4, unit).transpose(1, 0, 2).reshape(4, row_size * unit)
    bias_fc1 = jnp.concatenate(
        [lax.dynamic_index_in_dim(unit_order, quarter ^ d, 0, keepdims=False) for d in range(4)]
    )

    onehot = (band_table[0][:, None] == jnp.arange(wave_table.shape[0])[None, :]).astype(f32)
    wavelength = jnp.dot(onehot, wave_table, precision=highest)
    wave_embed = sincos(wavelength * 1000.0, wave_width)
    live = (jnp.arange(band_slots) < band_count[0]).astype(f32)[:, None]

    def hyper_fn(weight, bias):
        return jax.nn.gelu(jnp.dot(wave_embed, weight, precision=highest) + bias) * live

    hyper, hyper_back = jax.vjp(hyper_fn, wave_weight.astype(f32), wave_bias)
    per_row = wave_width // row_size
    place = jnp.arange(wave_width)
    kk = place % (per_row // 4)
    place = place // (per_row // 4)
    entry_z = place % z_size
    place = place // z_size
    entry_c, entry_y, entry_x = (place % 2) ^ at_c, (place // 2 % 2) ^ at_y, (place // 4) ^ at_x
    entry = per_row * (2 * entry_z + entry_y) + per_row // 4 * (2 * entry_x + entry_c) + kk
    order = (jnp.arange(wave_width)[:, None] == entry[None, :]).astype(bf16)
    hyper_low = dense_dot(hyper.astype(bf16), order).astype(bf16)

    pixel_rows = pixels.reshape(row_count, band_slots, pixel_count)
    patches = swap_plane(mix_pixels(hyper_low.T, pixel_rows))
    partial = project(patches, near, far)
    partial = swap_plane([partial[j * row_count : (j + 1) * row_count] for j in range(4)])
    projected = (partial[0] + partial[1]) + (partial[2] + partial[3])
    position = sincos(jnp.arange(seq_len).astype(f32), model_width)
    embedded = (projected + patch_bias).reshape(tile_count, seq_len, model_width) + position
    embedded = embedded.reshape(row_count, model_width)

    normed = layer_norm(embedded, norm1_gain, norm1_bias).astype(bf16)
    mixed = dense_dot(normed, w_qkv)
    queries = (mixed[:, :model_width] + query_bias).astype(bf16).reshape(head_shape)
    key_rows = mixed[:, model_width : 2 * model_width].astype(bf16).reshape(head_shape)
    value_rows = (mixed[:, 2 * model_width :] + value_bias).astype(bf16).reshape(head_shape)
    scores = (
        jnp.einsum("tqhd,tkhd->thqk", queries, key_rows, preferred_element_type=f32) * score_scale
    )
    probs_full = jax.nn.softmax(scores, axis=-1)
    probs = probs_full.astype(bf16)
    attended = (
        jnp.einsum("thqk,tkhd->tqhd", probs, value_rows, preferred_element_type=f32)
        .astype(bf16)
        .reshape(row_count, model_width)
    )
    middle = embedded + dense_dot(attended, w_out) + out_bias
    normed_two = layer_norm(middle, norm2_gain, norm2_bias).astype(bf16)
    fc_pre = dense_dot(normed_two, w_fc1) + bias_fc1
    hidden, gelu_back = jax.vjp(jax.nn.gelu, fc_pre)
    hidden = hidden.astype(bf16)
    block_out = middle + dense_dot(hidden, w_fc2) + fc2_bias

    grad_out = cotangent.reshape(row_count, model_width)
    fc2_bias_part = row_total(grad_out)
    fc2_grad = left_dot(hidden, grad_out)
    grad_hidden = right_dot(grad_out, w_fc2)
    grad_pre = gelu_back(grad_hidden)[0].astype(bf16)
    fc1_bias_part = row_total(grad_pre).reshape(4, row_size * unit)
    fc1_bias_part = jnp.stack(
        [lax.dynamic_index_in_dim(fc1_bias_part, quarter ^ j, 0, keepdims=False) for j in range(4)]
    )
    fc1_bias_part = fc1_bias_part.reshape(4, row_size, unit).transpose(1, 0, 2).reshape(-1)
    fc1_grad = left_dot(normed_two, grad_pre)
    grad_normed_two = right_dot(grad_pre, w_fc1)
    norm_two_back = jax.vjp(layer_norm, middle, norm2_gain, norm2_bias)[1]
    grad_middle, norm2_gain_part, norm2_bias_part = norm_two_back(grad_normed_two)
    grad_middle = grad_middle + grad_out.astype(f32)
    grad_branch = grad_middle.astype(bf16)
    out_bias_part = row_total(grad_branch)
    out_grad = left_dot(attended, grad_branch)
    grad_attended = right_dot(grad_branch, w_out).astype(bf16).reshape(head_shape)
    grad_probs = jnp.einsum(
        "tqhd,tkhd->thqk", grad_attended, value_rows, preferred_element_type=f32
    )
    grad_scores = probs_full * (
        grad_probs - jnp.sum(probs_full * grad_probs, axis=-1, keepdims=True)
    )
    grad_scores = grad_scores.astype(bf16)
    grad_queries = (
        jnp.einsum("thqk,tkhd->tqhd", grad_scores, key_rows, preferred_element_type=f32)
        * score_scale
    ).astype(bf16)
    grad_keys = (
        jnp.einsum("thqk,tqhd->tkhd", grad_scores, queries, preferred_element_type=f32)
        * score_scale
    ).astype(bf16)
    grad_values = jnp.einsum(
        "thqk,tqhd->tkhd", probs, grad_attended, preferred_element_type=f32
    ).astype(bf16)
    grad_queries = grad_queries.reshape(row_count, model_width)
    grad_values = grad_values.reshape(row_count, model_width)
    grad_mixed = jnp.concatenate(
        [grad_queries, grad_keys.reshape(row_count, model_width), grad_values], axis=1
    )
    query_bias_part = row_total(grad_queries)
    value_bias_part = row_total(grad_values)
    qkv_grad = left_dot(normed, grad_mixed)
    grad_normed = right_dot(grad_mixed, w_qkv)
    norm_one_back = jax.vjp(layer_norm, embedded, norm1_gain, norm1_bias)[1]
    grad_from_norm, norm1_gain_part, norm1_bias_part = norm_one_back(grad_normed)
    grad_embedded = (grad_middle + grad_from_norm).astype(bf16)
    patch_bias_part = row_total(grad_embedded)

    grads = jnp.concatenate(swap_plane([grad_embedded] * 4), axis=0)
    far_grad = swap_core(gen_grad(patches, grads, 1))
    back = swap_plane(back_patches(grads, near, far))
    near_grad = gen_grad(patches, grads, 0)
    gen_half = (near_grad.astype(f32) + far_grad.astype(f32)).astype(bf16)
    gen_half = gen_half.reshape(-1, model_width)
    gen_part = lax.psum_scatter(gen_half, "z", scatter_dimension=0, tiled=True)
    gen_total = lax.all_gather(gen_part, ("x", "c"), axis=0, tiled=True).astype(f32)

    attn_grads = jnp.stack(
        [qkv_grad[:, j * model_width : (j + 1) * model_width].astype(bf16) for j in range(3)]
        + [out_grad.astype(bf16)]
    )
    block_grads = []
    for d in range(4):
        cut = slice(d * model_width, (d + 1) * model_width)
        block_grads.append(
            jnp.stack(
                [
                    lax.dynamic_index_in_dim(attn_grads, quarter ^ d, 0, keepdims=False),
                    fc1_grad[:, cut].astype(bf16),
                    fc2_grad[cut].astype(bf16),
                ]
            )
        )
    received = swap_core(jnp.stack([block_grads[1], block_grads[3]]))
    kept = jnp.stack([block_grads[0], block_grads[2]])
    halves_sum = (kept.astype(f32) + received.astype(f32)).astype(bf16)
    received = swap_x(halves_sum[1])
    quarter_sum = (halves_sum[0].astype(f32) + received.astype(f32)).astype(bf16)
    pieces = lax.psum_scatter(quarter_sum, ("z", "y"), scatter_dimension=1, tiled=True)
    pieces = lax.all_gather(pieces, ("x", "c"), axis=0, tiled=False).astype(f32)
    qkv_total = jnp.concatenate([pieces[0, 0], pieces[1, 0], pieces[2, 0]], axis=1)
    out_total = pieces[3, 0]
    fc1_total = pieces[:, 1].reshape(4, shard, row_size, unit).transpose(1, 2, 0, 3)
    fc1_total = fc1_total.reshape(shard, hidden_width)
    fc2_total = pieces[:, 2].reshape(4 * unit, model_width)

    pixel_grad, grad_hyper = pixel_back(hyper_low, pixel_rows, back)
    grad_hyper = lax.dot_general(
        grad_hyper, order.astype(f32), (((1,), (1,)), ((), ())), precision=highest
    )
    wave_weight_part, wave_bias_part = hyper_back(grad_hyper)
    axes = ("x", "c", "z", "y")
    early = (
        patch_bias_part,
        norm1_gain_part,
        norm1_bias_part,
        query_bias_part,
        value_bias_part,
        out_bias_part,
        norm2_gain_part,
        norm2_bias_part,
        fc2_bias_part,
        fc1_bias_part,
    )
    early_total = lax.psum(jnp.concatenate(early), axes)
    early_total = [early_total[j * model_width : (j + 1) * model_width] for j in range(9)] + [
        early_total[9 * model_width :]
    ]
    (
        patch_bias_total,
        norm1_gain_total,
        norm1_bias_total,
        query_bias_total,
        value_bias_total,
        out_bias_total,
        norm2_gain_total,
        norm2_bias_total,
        fc2_bias_total,
        fc1_bias_total,
    ) = early_total
    late_total = lax.psum(jnp.concatenate([wave_weight_part, wave_bias_part[None]], axis=0), axes)
    wave_weight_total, wave_bias_total = late_total[:wave_width], late_total[wave_width]
    block_result = block_out.astype(bf16).reshape(1, tile_count, seq_len, model_width)
    pixel_result = pixel_grad.reshape(1, tile_count, seq_len, band_slots, pixel_count)
    return (
        block_result,
        pixel_result,
        wave_weight_total,
        wave_bias_total,
        gen_total,
        patch_bias_total,
        norm1_gain_total,
        norm1_bias_total,
        qkv_total,
        query_bias_total,
        value_bias_total,
        out_total,
        out_bias_total,
        norm2_gain_total,
        norm2_bias_total,
        fc1_total,
        fc1_bias_total,
        fc2_total,
        fc2_bias_total,
    )


def solution(mesh):
    grp_size, row_size = mesh.devices.shape
    split = Mesh(mesh.devices.reshape(grp_size // 2, 2, row_size // 2, 2), AXES)
    grp, row = ("x", "c"), ("z", "y")
    return jax.shard_map(
        body,
        mesh=split,
        in_specs=(
            P(grp, row, None, None, None),
            P(),
            P(),
            P(),
            P(row, None),
            P(),
            P(),
            P(),
            P(row, None),
            P(),
            P(),
            P(row, None),
            P(),
            P(),
            P(),
            P(row, None),
            P(),
            P(row, None),
            P(),
            P(grp),
            P(grp, None),
            P(grp, row, None, None),
        ),
        out_specs=(
            P(grp, row, None, None),
            P(grp, row, None, None, None),
            P(),
            P(),
            P(row, None),
            P(),
            P(),
            P(),
            P(row, None),
            P(),
            P(),
            P(row, None),
            P(),
            P(),
            P(),
            P(row, None),
            P(),
            P(row, None),
            P(),
        ),
        check_vma=False,
    )
```

time: 3620 us -> 1050 us (0.29)
  waiting for transfers between devices: 3280 us -> 731 us
  matrix products: 183 us -> 43.5 us
  Pallas kernels: 0 us -> 70.3 us
    unnamed x13 -> x7, waiting for transfers between devices: 1540 us -> 0.6 us
    all_gather x5 -> x4, waiting for transfers between devices: 1160 us -> 234 us  [the longest x1 112 us: body(): near = lax.all_gather(own_rows, 'z', axis=0, tiled=True)]
    reduce_scatter x4 -> x2, waiting for transfers between devices: 461 us -> 34.8 us  [the longest x1 34.8 us: body(): gen_part = lax.psum_scatter(gen_half, 'z', scatter_dimension=0, tiled=True)]
    ppermute x0 -> x19, waiting for transfers between devices: none -> 397 us  [the longest x4 128 us: swap_plane(): lax.ppermute(values[3], ('x', 'y'), CORNER)]
    dot_general x10 -> x7, matrix products: 88.4 us -> 13.7 us  [the longest x5 12.8 us: dense_dot(): return jnp.dot(left, right, preferred_element_type=f32)]
    pallas_call x0 -> x6, Pallas kernels: none -> 70.3 us  [the longest x1 17.5 us: pixel_back(): pl.pallas_call(pixel_kernel, grid=(row_count // MIX_ROWS,), in_specs=[pl....]
    psum x2 -> x1, waiting for transfers between devices: 119 us -> 64.2 us  [body(): lax.psum(jnp.concatenate([wave_weight_part, wave_bias_part[None]], axis=0...]
    dot_general x5 -> x4, matrix products: 54 us -> 4.83 us  [left_dot(): lax.dot_general(left, right, (((0,), (0,)), ((), ())), preferred_element_...]
  transfers between devices with their start and end apart: 12 -> 26, of which waited for: 12 -> 18; matrix products, arithmetic and copies ran while one was open for 7% -> 9% of each run, Pallas kernels for 0% -> 6%
where the time goes in v1:
time: 1050 us
  waiting for transfers between devices  731 us (70%)
  local copies, waits for them, and re-layouts  73.9 us (7%)
  Pallas kernels  70.3 us (7%)
  other arithmetic  52.4 us (5%)
  matrix products  43.5 us (4%)
  blocking collectives  41.2 us (4%)
  starting transfers between devices  20 us (2%)
  between operations  16.6 us (2%)
    ppermute x4, waiting for transfers between devices, swap_plane(): lax.ppermute(values[3], ('x', 'y'), CORNER)  128 us
    all_gather x1, waiting for transfers between devices, body(): near = lax.all_gather(own_rows, 'z', axis=0, tiled=True)  112 us
    ppermute x3, waiting for transfers between devices, swap_x(): return lax.ppermute(value, 'x', PAIR)  109 us
    ppermute x4, waiting for transfers between devices, swap_plane(): lax.ppermute(values[1], 'y', PAIR)  100 us
    all_gather x1, waiting for transfers between devices, body(): gathered = lax.all_gather(own_pieces, ('z', 'y'), axis=0, tiled=False)  65.2 us
    psum x1, waiting for transfers between devices, body(): lax.psum(jnp.concatenate([wave_weight_part, wave_bias_part[None]], axis=0...  64.2 us
    ppermute x4, waiting for transfers between devices, swap_plane(): lax.ppermute(values[2], 'x', PAIR)  49.5 us
    psum x1, blocking collectives, body(): early_total = lax.psum(jnp.concatenate(early), axes)  41.2 us
  transfers between devices with their start and end apart: 26, of which 18 were waited for; matrix products, arithmetic and copies ran while one was open for 9% of the time, Pallas kernels for 6%

profile of v1, /device:TPU:0, one launch (start us, length us, event | category | flops | bytes accessed | tf_op | source)
XLA Modules:
  0.0 1048.7 jit_solution(16080181750466785181)
XLA Ops:
  13.5 2.7 constant_dynamic-slice_fusion.14
  16.2 65.2 %all-gather.11.cloned.1.call-done = bf16[24,96,768]{2,1,0:T(8,128)(2,1)} async-done(((bf16[3,96,768]{2,1,0:T(8,128)(2,1)}), bf16[24,96,768]{2,1,0:T(8,128)(2,1)}) %all-gather.11.cloned.1.call-update) | async-done | bytes 3538960 | tf_op jit(solution)/shard_map/all_gather | solution.py:348
  81.5 4.1 copy.90
  85.5 111.9 %all-gather.7.cloned.1.call-done = bf16[4096,768]{1,0:T(8,128)(2,1)} async-done(((bf16[1024,768]{1,0:T(8,128)(2,1)}), bf16[4096,768]{1,0:T(8,128)(2,1)}) %all-gather.7.cloned.1.call-update) | async-done | bytes 6291472 | tf_op jit(solution)/shard_map/all_gather | solution.py:359
  202.2 11.3 %copy.110 = bf16[1,1,128,202,256]{4,3,2,1,0:T(8,128)(2,1)} copy(bf16[1,1,128,202,256]{4,2,3,1,0:T(8,128)(2,1)} %param.22) | data formatting | bytes 26476544 | tf_op args[0]
  213.4 13.1 %mix_pixels.1 = (bf16[32,128,256]{2,1,0:T(8,128)(2,1)S(1)}, bf16[32,128,256]{2,1,0:T(8,128)(2,1)}, bf16[32,128,256]{2,1,0:T(8,128)(2,1)}, bf16[32,128,256]{2,1,0:T(8,128)(2,1)}) custom-call(bf16[128,202]{1,0:T(8,128)(2,1)S(1)} %copy.88.hyper_ref, bf16[128,202,256]{2,1,0:T(8,128)(2,1)} %bitcast.189), custom_call_target="tpu_custom_call" | custom-call | flops 1694498816 | bytes 21626880 | tf_op jit(solution)/shard_map/mix_pixels/pallas_call | solution.py:71
  229.5 47.7 %collective-permute-done.8 = bf16[3,768,768]{2,1,0:T(8,128)(2,1)} collective-permute-done((bf16[3,768,768]{2,1,0:T(8,128)(2,1)}, bf16[3,768,768]{2,1,0:T(8,128)(2,1)}, u32[]{:S(2)}, u32[]{:S(2)}) %collective-permute-start.8) | collective-permute-done | bytes 3538976 | tf_op jit(solution)/shard_map/ppermute | solution.py:282
  277.2 2.4 collective-permute-start.2
  280.6 3.6 fusion.88
  284.2 3.6 slice_bitcast_fusion.18
  287.8 3.6 slice_bitcast_fusion.17
  291.4 61.6 %collective-permute-done.9 = bf16[3,768,768]{2,1,0:T(8,128)(2,1)} collective-permute-done((bf16[3,768,768]{2,1,0:T(8,128)(2,1)}, bf16[3,768,768]{2,1,0:T(8,128)(2,1)}, u32[]{:S(2)}, u32[]{:S(2)}) %collective-permute-start.9) | collective-permute-done | bytes 3538976 | tf_op jit(solution)/shard_map/ppermute | solution.py:282
  353.0 3.6 slice_bitcast_fusion.16
  356.6 41.3 %collective-permute-done.1.a2 = bf16[32,128,256]{2,1,0:T(8,128)(2,1)} collective-permute-done((bf16[32,128,256]{2,1,0:T(8,128)(2,1)}, bf16[32,128,256]{2,1,0:T(8,128)(2,1)}, u32[]{:S(2)}, u32[]{:S(2)}) %collective-permute-start.1) | collective-permute-done | bytes 2097184 | tf_op jit(solution)/shard_map/ppermute | solution.py:289
  398.0 45.4 %collective-permute-done.2.a3 = bf16[32,128,256]{2,1,0:T(8,128)(2,1)} collective-permute-done((bf16[32,128,256]{2,1,0:T(8,128)(2,1)}, bf16[32,128,256]{2,1,0:T(8,128)(2,1)}, u32[]{:S(2)}, u32[]{:S(2)}) %collective-permute-start.2) | collective-permute-done | bytes 2097184 | tf_op jit(solution)/shard_map/ppermute | solution.py:290
  443.4 12.5 %project.1 = f32[512,768]{1,0:T(8,128)S(1)} custom-call(bf16[32,128,256]{2,1,0:T(8,128)(2,1)S(1)} %get-tuple-element.29.a0, bf16[32,128,256]{2,1,0:T(8,128)(2,1)} %collective-permute-done.a1, bf16[32,128,256]{2,1,0:T(8,128)(2,1)} %collective-permute-done.1.a2, bf16[32,128,256]{2,1,0:T(8,128)(2,1)} %collective-permute-done.2.a3, ...), custom_call_target="tpu_custom_call" | custom-call | flops 6442450944 | bytes 20971520 | tf_op jit(solution)/shard_map/project/pallas_call | solution.py:125
  462.4 5.7 collective-permute-done.5
  468.1 7.2 collective-permute-done.6
  482.7 3.5 convolution_add_fusion
  486.4 9.1 convert_reduce_fusion
  498.8 2.5 fusion.20
  503.1 3.0 convert_reduce_fusion.3
  519.6 3.6 pad_maximum_fusion
  523.2 3.3 maximum_bitcast_fusion.1
  528.7 6.1 collective-permute-done.17
  534.8 9.7 add_convert_fusion
  544.5 2.4 slice_bitcast_fusion
  548.5 3.3 multiply_reduce_fusion.2
  555.8 75.7 %collective-permute-done.12 = bf16[128,768]{1,0:T(8,128)(2,1)S(1)} collective-permute-done((bf16[128,768]{1,0:T(8,128)(2,1)S(1)}, bf16[128,768]{1,0:T(8,128)(2,1)S(1)}, u32[]{:S(2)}, u32[]{:S(2)}) %collective-permute-start.12) | collective-permute-done | bytes 196640 | tf_op jit(solution)/shard_map/ppermute | solution.py:290
  631.5 2.5 collective-permute-done.11
  634.1 2.8 fusion.1
  637.0 7.1 gen_grad.3
  644.1 7.1 gen_grad.2
  651.2 3.4 collective-permute-done.16
  654.6 9.5 add_convert_fusion.1
  664.1 12.9 %back_patches.1 = (bf16[32,128,256]{2,1,0:T(8,128)(2,1)S(1)}, bf16[32,128,256]{2,1,0:T(8,128)(2,1)S(1)}, bf16[32,128,256]{2,1,0:T(8,128)(2,1)}, bf16[32,128,256]{2,1,0:T(8,128)(2,1)}) custom-call(bf16[512,768]{1,0:T(8,128)(2,1)S(1)} %pad_maximum_fusion.13.g, bf16[16,256,768]{2,1,0:T(8,128)(2,1)} %bitcast.234, bf16[16,256,768]{2,1,0:T(8,128)(2,1)} %bitcast.7.w1), custom_call_target="tpu_custom_call" | custom-call | flops 6442450944 | bytes 20971520 | tf_op jit(solution)/shard_map/back_patches/pallas_call | solution.py:171
  680.6 98.7 %collective-permute-done.13.g1 = bf16[32,128,256]{2,1,0:T(8,128)(2,1)S(1)} collective-permute-done((bf16[32,128,256]{2,1,0:T(8,128)(2,1)S(1)}, bf16[32,128,256]{2,1,0:T(8,128)(2,1)S(1)}, u32[]{:S(2)}, u32[]{:S(2)}) %collective-permute-start.13) | collective-permute-done | bytes 2097184 | tf_op jit(solution)/shard_map/ppermute | solution.py:288
  781.4 17.5 %pixel_back.1 = (bf16[128,202,256]{2,1,0:T(8,128)(2,1)}, f32[202,128]{1,0:T(8,128)S(1)}) custom-call(bf16[202,128]{1,0:T(8,128)(2,1)S(1)} %convolution_convert_fusion.6.hyper_ref, bf16[128,202,256]{2,1,0:T(8,128)(2,1)} %bitcast.190, bf16[32,128,256]{2,1,0:T(8,128)(2,1)S(1)} %get-tuple-element.33.g0, bf16[32,128,256]{2,1,0:T(8,128)(2,1)S(1)} %collective-permute-done.13.g1, ...), custom_call_target="tpu_custom_call" | custom-call | flops 3388997632 | bytes 34865152 | tf_op jit(solution)/shard_map/pixel_back/pallas_call | solution.py:246
  801.3 34.8 %reduce-scatter.3.cloned.1.call-done = bf16[1024,768]{1,0:T(8,128)(2,1)} async-done(((bf16[4096,768]{1,0:T(8,128)(2,1)}), bf16[1024,768]{1,0:T(8,128)(2,1)}) %reduce-scatter.3.cloned.1.call-update) | async-done | bytes 1572880 | tf_op jit(solution)/shard_map/reduce_scatter | solution.py:477
  836.7 41.2 %psum.15 = f32[9984]{0:T(1024)S(1)} all-reduce(f32[9984]{0:T(1024)S(1)} %constant_dynamic-update-slice_fusion), channel_id=1, replica_groups=mesh['x'=2,'c'=2,'z'=4,'y'=2] {'x','c','z','y'}, use_global_device_ids=true, to_apply=%region_24.25 | all-reduce | flops 9984 | bytes 79872 | tf_op jit(solution)/shard_map/psum | solution.py:527
  879.2 6.5 fusion.25
  885.7 10.8 %copy.102 = bf16[1,1,128,202,256]{4,2,3,1,0:T(8,128)(2,1)} copy(bf16[1,1,128,202,256]{4,3,2,1,0:T(8,128)(2,1)S(1)} %bitcast.196) | data formatting | bytes 26476544
  896.4 64.2 %all-reduce.2.cloned.1.call-done = f32[129,128]{1,0:T(8,128)} async-done(((f32[129,128]{1,0:T(8,128)}), f32[129,128]{1,0:T(8,128)}) %all-reduce.2.cloned.1.call-update) | async-done | bytes 66064 | tf_op jit(solution)/shard_map/psum | solution.py:543
  963.3 21.8 %all-gather.13.cloned.1.call-done = bf16[12,96,768]{2,1,0:T(8,128)(2,1)} async-done(((bf16[3,96,768]{2,1,0:T(8,128)(2,1)}), bf16[12,96,768]{2,1,0:T(8,128)(2,1)}) %all-gather.13.cloned.1.call-update) | async-done | bytes 1769488 | tf_op jit(solution)/shard_map/all_gather | solution.py:502
  985.0 3.7 convert.25
  991.7 2.7 reshape.418
  997.5 35.5 %all-gather.9.cloned.1.call-done = bf16[4096,768]{1,0:T(8,128)(2,1)} async-done(((bf16[1024,768]{1,0:T(8,128)(2,1)}), bf16[4096,768]{1,0:T(8,128)(2,1)}) %all-gather.9.cloned.1.call-update) | async-done | bytes 6291472 | tf_op jit(solution)/shard_map/all_gather | solution.py:478
  1033.0 8.6 convert_element_type.225
  (319 shorter events, 72.1 us)
Async XLA Ops:
  7.2 193.9 %copy-start = (bf16[128,128]{1,0:T(8,128)(2,1)S(1)}, bf16[128,128]{1,0:T(8,128)(2,1)}, u32[]{:S(2)}) copy-start(bf16[128,128]{1,0:T(8,128)(2,1)} %param.24) | copy-start | bytes 98308
  7.2 74.3 %all-gather.11.cloned.1.call-start = ((), (), s32[]{:S(2)}) async-start(), calls=%async_computation.7 | async-start | bytes 3981312 | tf_op jit(solution)/shard_map/all_gather | solution.py:348
  13.4 184.1 %all-gather.7.cloned.1.call-start = ((), (), s32[]{:S(2)}) async-start(), calls=%async_computation.2 | async-start | bytes 7864320 | tf_op jit(solution)/shard_map/all_gather | solution.py:359
  16.2 784.3 %reduce-scatter.5.cloned.1.call-start = ((), (), s32[]{:S(2)}) async-start(), calls=%async_computation.6 | async-start | bytes 3981312 | tf_op jit(solution)/shard_map/reduce_scatter | solution.py:501
  81.5 118.8 %copy-start.82 = (f32[256]{0:T(256)S(1)}, f32[256]{0:T(256)}, u32[]{:S(2)}) copy-start(f32[256]{0:T(256)} %param.23) | copy-start | bytes 3076
  81.5 118.8 %copy-start.83 = (s32[1,202]{1,0:T(1,128)S(1)}, s32[1,202]{1,0:T(1,128)}, u32[]{:S(2)}) copy-start(s32[1,202]{1,0:T(1,128)} %param.42) | copy-start | bytes 2428
  81.5 119.6 %copy-start.76 = (f32[128]{0:T(128)S(1)}, f32[128]{0:T(128)}, u32[]{:S(2)}) copy-start(f32[128]{0:T(128)} %param.25) | copy-start | bytes 1540
  85.5 113.5 %collective-permute-start.7 = (bf16[3,768,768]{2,1,0:T(8,128)(2,1)}, bf16[3,768,768]{2,1,0:T(8,128)(2,1)}, u32[]{:S(2)}, u32[]{:S(2)}) collective-permute-start(bf16[3,768,768]{2,1,0:T(8,128)(2,1)} %bitcast.18), channel_id=1, source_target_pairs={{0,8},{8,0},{1,9},{9,1},{2,10},{10,2},{3,11},{11,3},{4,12},{12,4},... | collective-permute-start | bytes 10616840 | tf_op jit(solution)/shard_map/ppermute | solution.py:278
  197.5 245.9 %collective-permute-start.3 = (bf16[4096,768]{1,0:T(8,128)(2,1)}, bf16[4096,768]{1,0:T(8,128)(2,1)}, u32[]{:S(2)}, u32[]{:S(2)}) collective-permute-start(bf16[4096,768]{1,0:T(8,128)(2,1)} %all-gather.7.cloned.1.call-done), channel_id=1, source_target_pairs={{0,8},{8,0},{1,9},{9,1},{2,10},{10,2},{3,11},{11,3},{4,12},{12,4},... | collective-permute-start | bytes 18874376 | tf_op jit(solution)/shard_map/ppermute | solution.py:278
  197.5 79.6 %collective-permute-start.8 = (bf16[3,768,768]{2,1,0:T(8,128)(2,1)}, bf16[3,768,768]{2,1,0:T(8,128)(2,1)}, u32[]{:S(2)}, u32[]{:S(2)}) collective-permute-start(bf16[3,768,768]{2,1,0:T(8,128)(2,1)} %bitcast.18), channel_id=1, source_target_pairs={{0,16},{16,0},{1,17},{17,1},{2,18},{18,2},{3,19},{19,3},{4,20},{20... | collective-permute-start | bytes 10616840 | tf_op jit(solution)/shard_map/ppermute | solution.py:282
  199.0 154.0 %collective-permute-start.9 = (bf16[3,768,768]{2,1,0:T(8,128)(2,1)}, bf16[3,768,768]{2,1,0:T(8,128)(2,1)}, u32[]{:S(2)}, u32[]{:S(2)}) collective-permute-start(bf16[3,768,768]{2,1,0:T(8,128)(2,1)} %collective-permute-done.7), channel_id=1, source_target_pairs={{0,16},{16,0},{1,17},{17,1},{2,18},{18,2},{3,19},{19,3},{4,20},{20... | collective-permute-start | bytes 10616840 | tf_op jit(solution)/shard_map/ppermute | solution.py:282
  213.4 66.2 %copy-start.55 = (f32[3072]{0:T(1024)S(1)}, f32[3072]{0:T(1024)}, u32[]{:S(2)}) copy-start(f32[3072]{0:T(1024)} %param.38) | copy-start | bytes 36868
  226.6 130.1 %collective-permute-start = (bf16[32,128,256]{2,1,0:T(8,128)(2,1)}, bf16[32,128,256]{2,1,0:T(8,128)(2,1)}, u32[]{:S(2)}, u32[]{:S(2)}) collective-permute-start(bf16[32,128,256]{2,1,0:T(8,128)(2,1)} %get-tuple-element.30), channel_id=1, source_target_pairs={{0,1},{1,0},{2,3},{3,2},{4,5},{5,4},{6,7},{7,6},{8,9},{9,8},{10,11... | collective-permute-start | bytes 6291464 | tf_op jit(solution)/shard_map/ppermute | solution.py:288
  228.0 170.0 %collective-permute-start.1 = (bf16[32,128,256]{2,1,0:T(8,128)(2,1)}, bf16[32,128,256]{2,1,0:T(8,128)(2,1)}, u32[]{:S(2)}, u32[]{:S(2)}) collective-permute-start(bf16[32,128,256]{2,1,0:T(8,128)(2,1)} %get-tuple-element.31), channel_id=1, source_target_pairs={{0,16},{16,0},{1,17},{17,1},{2,18},{18,2},{3,19},{19,3},{4,20},{20... | collective-permute-start | bytes 6291464 | tf_op jit(solution)/shard_map/ppermute | solution.py:289
  277.2 166.2 %collective-permute-start.2 = (bf16[32,128,256]{2,1,0:T(8,128)(2,1)}, bf16[32,128,256]{2,1,0:T(8,128)(2,1)}, u32[]{:S(2)}, u32[]{:S(2)}) collective-permute-start(bf16[32,128,256]{2,1,0:T(8,128)(2,1)} %get-tuple-element.32), channel_id=1, source_target_pairs={{0,17},{1,16},{16,1},{17,0},{2,19},{3,18},{18,3},{19,2},{4,21},{5,... | collective-permute-start | bytes 6291464 | tf_op jit(solution)/shard_map/ppermute | solution.py:290
  456.0 12.1 %collective-permute-start.5 = (f32[128,768]{1,0:T(8,128)S(1)}, f32[128,768]{1,0:T(8,128)S(1)}, u32[]{:S(2)}, u32[]{:S(2)}) collective-permute-start(f32[128,768]{1,0:T(8,128)S(1)} %get-tuple-element.173), channel_id=1, source_target_pairs={{0,16},{16,0},{1,17},{17,1},{2,18},{18,2},{3,19},{19,3},{4,20},{20... | collective-permute-start | bytes 1179656 | tf_op jit(solution)/shard_map/ppermute | solution.py:289
  457.6 17.7 %collective-permute-start.6 = (f32[128,768]{1,0:T(8,128)S(1)}, f32[128,768]{1,0:T(8,128)S(1)}, u32[]{:S(2)}, u32[]{:S(2)}) collective-permute-start(f32[128,768]{1,0:T(8,128)S(1)} %get-tuple-element.172), channel_id=1, source_target_pairs={{0,17},{1,16},{16,1},{17,0},{2,19},{3,18},{18,3},{19,2},{4,21},{5,... | collective-permute-start | bytes 1179656 | tf_op jit(solution)/shard_map/ppermute | solution.py:290
  458.1 18.6 %collective-permute-start.4 = (f32[128,768]{1,0:T(8,128)S(1)}, f32[128,768]{1,0:T(8,128)S(1)}, u32[]{:S(2)}, u32[]{:S(2)}) collective-permute-start(f32[128,768]{1,0:T(8,128)S(1)} %get-tuple-element.171), channel_id=1, source_target_pairs={{0,1},{1,0},{2,3},{3,2},{4,5},{5,4},{6,7},{7,6},{8,9},{9,8},{10,11... | collective-permute-start | bytes 1179656 | tf_op jit(solution)/shard_map/ppermute | solution.py:288
  460.2 16.5 %copy-start.73 = (f32[768]{0:T(1024)S(1)}, f32[768]{0:T(1024)}, u32[]{:S(2)}) copy-start(f32[768]{0:T(1024)} %param.27) | copy-start | bytes 9220
  523.2 11.6 %collective-permute-start.17 = (bf16[2,3,768,768]{3,2,1,0:T(8,128)(2,1)}, bf16[2,3,768,768]{3,2,1,0:T(8,128)(2,1)}, u32[]{:S(2)}, u32[]{:S(2)}) collective-permute-start(bf16[2,3,768,768]{3,2,1,0:T(8,128)(2,1)} %pad_maximum_fusion), channel_id=1, source_target_pairs={{0,8},{8,0},{1,9},{9,1},{2,10},{10,2},{3,11},{11,3},{4,12},{12,4},... | collective-permute-start | bytes 21233672 | tf_op jit(solution)/shard_map/ppermute | solution.py:278
  544.5 89.6 %slice-start = ((s8[7077888]{0:T(1024)(128)(4,1)}), s8[4194304]{0:T(1024)(128)(4,1)S(1)}, s32[]{:S(2)}) async-start(s8[7077888]{0:T(1024)(128)(4,1)} %bitcast.191), calls=%async_computation.9 | async-start | bytes 8388608
  546.9 87.2 %slice-start.1 = ((s8[7077888]{0:T(1024)(128)(4,1)}), s8[2883584]{0:T(1024)(128)(4,1)S(1)}, s32[]{:S(2)}) async-start(s8[7077888]{0:T(1024)(128)(4,1)} %bitcast.191), calls=%async_computation.10 | async-start | bytes 5767168
  546.9 87.1 %collective-permute-start.18 = (bf16[3,768,768]{2,1,0:T(8,128)(2,1)S(1)}, bf16[3,768,768]{2,1,0:T(8,128)(2,1)S(1)}, u32[]{:S(2)}, u32[]{:S(2)}) collective-permute-start(bf16[3,768,768]{2,1,0:T(8,128)(2,1)S(1)} %slice_bitcast_fusion), channel_id=1, source_target_pairs={{0,16},{16,0},{1,17},{17,1},{2,18},{18,2},{3,19},{19,3},{4,20},{20... | collective-permute-start | bytes 10616840 | tf_op jit(solution)/shard_map/ppermute | solution.py:282
  552.3 79.2 %collective-permute-start.12 = (bf16[128,768]{1,0:T(8,128)(2,1)S(1)}, bf16[128,768]{1,0:T(8,128)(2,1)S(1)}, u32[]{:S(2)}, u32[]{:S(2)}) collective-permute-start(bf16[128,768]{1,0:T(8,128)(2,1)S(1)} %get-tuple-element.128), channel_id=1, source_target_pairs={{0,17},{1,16},{16,1},{17,0},{2,19},{3,18},{18,3},{19,2},{4,21},{5,... | collective-permute-start | bytes 589832 | tf_op jit(solution)/shard_map/ppermute | solution.py:290
  553.9 80.1 %collective-permute-start.11 = (bf16[128,768]{1,0:T(8,128)(2,1)S(1)}, bf16[128,768]{1,0:T(8,128)(2,1)S(1)}, u32[]{:S(2)}, u32[]{:S(2)}) collective-permute-start(bf16[128,768]{1,0:T(8,128)(2,1)S(1)} %get-tuple-element.128), channel_id=1, source_target_pairs={{0,16},{16,0},{1,17},{17,1},{2,18},{18,2},{3,19},{19,3},{4,20},{20... | collective-permute-start | bytes 589832 | tf_op jit(solution)/shard_map/ppermute | solution.py:289
  555.3 78.7 %collective-permute-start.10 = (bf16[128,768]{1,0:T(8,128)(2,1)S(1)}, bf16[128,768]{1,0:T(8,128)(2,1)S(1)}, u32[]{:S(2)}, u32[]{:S(2)}) collective-permute-start(bf16[128,768]{1,0:T(8,128)(2,1)S(1)} %get-tuple-element.128), channel_id=1, source_target_pairs={{0,1},{1,0},{2,3},{3,2},{4,5},{5,4},{6,7},{7,6},{8,9},{9,8},{10,11... | collective-permute-start | bytes 589832 | tf_op jit(solution)/shard_map/ppermute | solution.py:288
  636.9 199.2 %reduce-scatter.3.cloned.1.call-start = ((), (), s32[]{:S(2)}) async-start(), calls=%async_computation.4 | async-start | bytes 7864320 | tf_op jit(solution)/shard_map/reduce_scatter | solution.py:477
  644.1 10.5 %collective-permute-start.16 = (bf16[16,256,768]{2,1,0:T(8,128)(2,1)}, bf16[16,256,768]{2,1,0:T(8,128)(2,1)}, u32[]{:S(2)}, u32[]{:S(2)}) collective-permute-start(bf16[16,256,768]{2,1,0:T(8,128)(2,1)} %gen_grad.3), channel_id=1, source_target_pairs={{0,8},{8,0},{1,9},{9,1},{2,10},{10,2},{3,11},{11,3},{4,12},{12,4},... | collective-permute-start | bytes 18874376 | tf_op jit(solution)/shard_map/ppermute | solution.py:278
  664.1 296.5 %all-reduce.2.cloned.1.call-start = ((), (), s32[]{:S(2)}) async-start(), calls=%async_computation.3 | async-start | bytes 139264 | tf_op jit(solution)/shard_map/psum | solution.py:543
  677.1 102.2 %collective-permute-start.13 = (bf16[32,128,256]{2,1,0:T(8,128)(2,1)S(1)}, bf16[32,128,256]{2,1,0:T(8,128)(2,1)S(1)}, u32[]{:S(2)}, u32[]{:S(2)}) collective-permute-start(bf16[32,128,256]{2,1,0:T(8,128)(2,1)S(1)} %get-tuple-element.34), channel_id=1, source_target_pairs={{0,1},{1,0},{2,3},{3,2},{4,5},{5,4},{6,7},{7,6},{8,9},{9,8},{10,11... | collective-permute-start | bytes 6291464 | tf_op jit(solution)/shard_map/ppermute | solution.py:288
  678.6 100.7 %collective-permute-start.14 = (bf16[32,128,256]{2,1,0:T(8,128)(2,1)}, bf16[32,128,256]{2,1,0:T(8,128)(2,1)S(1)}, u32[]{:S(2)}, u32[]{:S(2)}) collective-permute-start(bf16[32,128,256]{2,1,0:T(8,128)(2,1)} %get-tuple-element.35), channel_id=1, source_target_pairs={{0,16},{16,0},{1,17},{17,1},{2,18},{18,2},{3,19},{19,3},{4,20},{20... | collective-permute-start | bytes 6291464 | tf_op jit(solution)/shard_map/ppermute | solution.py:289
  680.0 99.2 %collective-permute-start.15 = (bf16[32,128,256]{2,1,0:T(8,128)(2,1)}, bf16[32,128,256]{2,1,0:T(8,128)(2,1)S(1)}, u32[]{:S(2)}, u32[]{:S(2)}) collective-permute-start(bf16[32,128,256]{2,1,0:T(8,128)(2,1)} %get-tuple-element.36), channel_id=1, source_target_pairs={{0,17},{1,16},{16,1},{17,0},{2,19},{3,18},{18,3},{19,2},{4,21},{5,... | collective-permute-start | bytes 6291464 | tf_op jit(solution)/shard_map/ppermute | solution.py:290
  781.3 17.5 %copy-start.49 = (f32[202,128]{1,0:T(8,128)S(1)}, f32[202,128]{1,0:T(8,128)}, u32[]{:S(2)}) copy-start(f32[202,128]{1,0:T(8,128)} %copy-done.48) | copy-start | bytes 310276
  781.3 17.5 %copy-start.80 = (s32[128]{0:T(128)S(1)}, s32[128]{0:T(128)}, u32[]{:S(2)}) copy-start(s32[128]{0:T(128)} %copy-done.79) | copy-start | bytes 1540
  781.3 17.5 %copy-start.85 = (f32[202]{0:T(256)S(1)}, f32[202]{0:T(256)}, u32[]{:S(2)}) copy-start(f32[202]{0:T(256)} %copy-done.84) | copy-start | bytes 2428
  781.3 17.9 %copy-start.29 = (f32[202,64]{1,0:T(8,128)S(1)}, f32[202,64]{1,0:T(8,128)}, u32[]{:S(2)}) copy-start(f32[202,64]{1,0:T(8,128)} %copy-done.28) | copy-start | bytes 155140
  781.4 17.9 %copy-start.31 = (f32[202,64]{1,0:T(8,128)S(1)}, f32[202,64]{1,0:T(8,128)}, u32[]{:S(2)}) copy-start(f32[202,64]{1,0:T(8,128)} %copy-done.30) | copy-start | bytes 155140
  798.9 37.3 %copy-start.63 = (f32[12,64]{1,0:T(8,128)S(1)}, f32[12,64]{1,0:T(8,128)}, u32[]{:S(2)}) copy-start(f32[12,64]{1,0:T(8,128)} %get-tuple-element.209) | copy-start | bytes 9220
  798.9 37.4 %copy-start.56 = (f32[3072]{0:T(1024)S(1)}, f32[3072]{0:T(1024)}, u32[]{:S(2)}) copy-start(f32[3072]{0:T(1024)} %get-tuple-element.211) | copy-start | bytes 36868
  799.2 37.3 %copy-start.72 = (f32[768]{0:T(1024)S(1)}, f32[768]{0:T(1024)}, u32[]{:S(2)}) copy-start(f32[768]{0:T(1024)} %get-tuple-element.117) | copy-start | bytes 9220
  799.2 37.4 %copy-start.54 = (f32[768]{0:T(1024)S(1)}, f32[768]{0:T(1024)}, u32[]{:S(2)}) copy-start(f32[768]{0:T(1024)} %get-tuple-element.125) | copy-start | bytes 9220
  799.2 37.4 %copy-start.71 = (f32[768]{0:T(1024)S(1)}, f32[768]{0:T(1024)}, u32[]{:S(2)}) copy-start(f32[768]{0:T(1024)} %get-tuple-element.115) | copy-start | bytes 9220
  799.2 37.4 %copy-start.70 = (f32[768]{0:T(1024)S(1)}, f32[768]{0:T(1024)}, u32[]{:S(2)}) copy-start(f32[768]{0:T(1024)} %get-tuple-element.119) | copy-start | bytes 9220
  799.2 79.9 %copy-start.7 = (f32[128,3072]{1,0:T(8,128)S(1)}, f32[128,3072]{1,0:T(8,128)}, u32[]{:S(2)}) copy-start(f32[128,3072]{1,0:T(8,128)} %copy-done.5) | copy-start | bytes 4718596
  799.2 79.9 %copy-start.15 = (bf16[1,8,96,768]{3,2,0,1:T(8,128)(2,1)S(1)}, bf16[1,8,96,768]{3,2,0,1:T(8,128)(2,1)}, u32[]{:S(2)}) copy-start(bf16[1,8,96,768]{3,2,0,1:T(8,128)(2,1)} %get-tuple-element.158) | copy-start | bytes 3538948
  799.2 79.9 %copy-start.81 = (f32[768]{0:T(1024)S(1)}, f32[768]{0:T(1024)}, u32[]{:S(2)}) copy-start(f32[768]{0:T(1024)} %param.40) | copy-start | bytes 9220
  800.4 184.6 %all-gather.13.cloned.1.call-start = ((), (), s32[]{:S(2)}) async-start(), calls=%async_computation.8 | async-start | bytes 2211840 | tf_op jit(solution)/shard_map/all_gather | solution.py:502
  801.0 232.0 %all-gather.9.cloned.1.call-start = ((), (), s32[]{:S(2)}) async-start(), calls=%async_computation.5 | async-start | bytes 7864320 | tf_op jit(solution)/shard_map/all_gather | solution.py:478
  (66 other events, 279.2 us)
Sparse Core Ops, SparseCore 0:
  13.6 67.8 all-gather.10
  83.6 113.8 all-gather.6
  637.0 87.3 reduce-scatter.4
  727.1 108.9 reduce-scatter.2
  842.1 118.4 all-reduce.1
  962.0 22.9 all-gather.12
  986.6 46.3 all-gather.8

commit v2 on v1

v2 whole, which is shorter than its diff:
```python
import functools

import jax
import jax.numpy as jnp
from jax import lax
from jax.experimental import pallas as pl
from jax.experimental.pallas import tpu as pltpu
from jax.sharding import Mesh
from jax.sharding import PartitionSpec as P

HEADS = 12

bf16 = jnp.bfloat16
f32 = jnp.float32
highest = lax.Precision.HIGHEST
epsilon = 1e-06

AXES = ("x", "c", "z", "y")
VMEM_LIMIT = 48 * 1024 * 1024
MIX_ROWS = 16
GEN_STEP = 4
COST = pl.CostEstimate(flops=1, bytes_accessed=1, transcendentals=0)


def sincos(angles_in, out_width):
    half_width = out_width // 2
    freqs = 1.0 / 10000.0 ** (jnp.arange(half_width).astype(angles_in.dtype) * (2.0 / out_width))
    angles = angles_in[:, None] * freqs[None, :]
    return jnp.concatenate([jnp.sin(angles), jnp.cos(angles)], axis=1)


def layer_norm(inputs, gain, shift):
    center = inputs - jnp.mean(inputs, axis=-1, keepdims=True)
    spread = jnp.mean(center * center, axis=-1, keepdims=True)
    return center * lax.rsqrt(spread + epsilon) * gain + shift


def dense_dot(left, right):
    return jnp.dot(left, right, preferred_element_type=f32)


def left_dot(left, right):
    return lax.dot_general(left, right, (((0,), (0,)), ((), ())), preferred_element_type=f32)


def right_dot(left, right):
    return lax.dot_general(left, right, (((1,), (1,)), ((), ())), preferred_element_type=f32)


def row_total(values):
    return jnp.sum(values.astype(f32), axis=0)


def mix_kernel(hyper_ref, pix_ref, *outs):
    slots, rows, pixel_count = pix_ref.shape
    entries = hyper_ref.shape[0]
    mixed = dense_dot(hyper_ref[...], pix_ref[...].reshape(slots, rows * pixel_count))
    mixed = mixed.astype(bf16).reshape(entries, rows, pixel_count)
    for j, out in enumerate(outs):
        share = out.shape[0]
        out[...] = mixed[j * share : (j + 1) * share]


def mix_pixels(hyper_t, pixel_rows):
    entries = hyper_t.shape[0]
    slots, row_count, pixel_count = pixel_rows.shape
    share = entries // 4
    out = jax.ShapeDtypeStruct((share, row_count, pixel_count), bf16)
    return pl.pallas_call(
        mix_kernel,
        grid=(row_count // MIX_ROWS,),
        in_specs=[
            pl.BlockSpec((entries, slots), lambda i: (0, 0)),
            pl.BlockSpec((slots, MIX_ROWS, pixel_count), lambda i: (0, i, 0)),
        ],
        out_specs=[pl.BlockSpec((share, MIX_ROWS, pixel_count), lambda i: (0, i, 0))] * 4,
        out_shape=[out] * 4,
        compiler_params=pltpu.CompilerParams(vmem_limit_bytes=VMEM_LIMIT),
        cost_estimate=COST,
        name="mix_pixels",
    )(hyper_t, pixel_rows)


def halves(steps):
    first = lambda i: (jnp.minimum(i, steps - 1), 0, 0)
    second = lambda i: (jnp.maximum(i - steps, 0), 0, 0)
    return first, second


def project_kernel(*refs):
    parts, w, sums, out = refs[:4], refs[4], refs[5:-1], refs[-1]

    @pl.when(pl.program_id(0) == 0)
    def _():
        out[...] = sums[0][...] if sums else jnp.zeros_like(out)

    for k in range(w.shape[0]):
        left = jnp.concatenate([a[k] for a in parts], axis=0)
        out[...] += dense_dot(left, w[k])


def project(parts, gen, which, sums=()):
    share, rows, pixel_count = parts[0].shape
    width = gen.shape[2]
    steps = share // 2 // GEN_STEP
    out = pl.BlockSpec((4 * rows, width), lambda i: (0, 0))
    return pl.pallas_call(
        project_kernel,
        grid=(steps,),
        in_specs=[pl.BlockSpec((GEN_STEP, rows, pixel_count), lambda i: (i + which * steps, 0, 0))] * 4
        + [pl.BlockSpec((GEN_STEP, pixel_count, width), lambda i: (i, 0, 0))]
        + [out] * len(sums),
        out_specs=out,
        out_shape=jax.ShapeDtypeStruct((4 * rows, width), f32),
        compiler_params=pltpu.CompilerParams(vmem_limit_bytes=VMEM_LIMIT),
        cost_estimate=COST,
        name="project",
    )(*parts, gen, *sums)


def early_rows(rows):
    return rows // 4 * 3


def back_kernel(g0, g1, g2, g3, w0, w1, *outs):
    i = pl.program_id(0)
    steps = pl.num_programs(0) // 2
    rows = g0.shape[0]

    def work(w):
        grads = jnp.concatenate([g[...] for g in (g0, g1, g2, g3)], axis=0)
        for k in range(w.shape[0]):
            res = right_dot(grads, w[k]).astype(bf16)
            for j, out in enumerate(outs):
                out[k] = res[j * rows : (j + 1) * rows]

    @pl.when(i < steps)
    def _():
        work(w0)

    @pl.when(i >= steps)
    def _():
        work(w1)


def back_patches(grads, near, far, start, rows):
    share, pixel_count, width = 2 * near.shape[0], near.shape[1], near.shape[2]
    steps = share // 2 // GEN_STEP
    first, second = halves(steps)
    out = jax.ShapeDtypeStruct((share, rows, pixel_count), bf16)
    return pl.pallas_call(
        back_kernel,
        grid=(2 * steps,),
        in_specs=[pl.BlockSpec((rows, width), lambda i: (start // rows, 0))] * 4
        + [
            pl.BlockSpec((GEN_STEP, pixel_count, width), first),
            pl.BlockSpec((GEN_STEP, pixel_count, width), second),
        ],
        out_specs=[pl.BlockSpec((GEN_STEP, rows, pixel_count), lambda i: (i, 0, 0))] * 4,
        out_shape=[out] * 4,
        compiler_params=pltpu.CompilerParams(vmem_limit_bytes=VMEM_LIMIT),
        cost_estimate=COST,
        name="back_patches",
    )(*grads, near, far)


def gen_grad_kernel(*refs, others):
    parts, grad_refs = refs[:4], refs[4:8]
    grads = jnp.concatenate([g[...] for g in grad_refs], axis=0)
    outs = refs[8 + others :]
    cut = outs[0].shape[1]
    for k in range(cut * len(outs)):
        left = jnp.concatenate([a[k] for a in parts], axis=0)
        res = left_dot(left, grads)
        for other in refs[8 : 8 + others]:
            res = res + other[k].astype(f32)
        outs[k // cut][0, k % cut] = res.astype(bf16)


def gen_grad(parts, grads, which, others=(), chunks=1):
    share, rows, pixel_count = parts[0].shape
    width = grads[0].shape[1]
    steps = share // 2 // GEN_STEP
    cut = GEN_STEP // chunks
    return pl.pallas_call(
        functools.partial(gen_grad_kernel, others=len(others)),
        grid=(steps,),
        in_specs=[pl.BlockSpec((GEN_STEP, rows, pixel_count), lambda i: (i + which * steps, 0, 0))] * 4
        + [pl.BlockSpec((rows, width), lambda i: (0, 0))] * 4
        + [pl.BlockSpec((GEN_STEP, pixel_count, width), lambda i: (i, 0, 0))] * len(others),
        out_specs=[pl.BlockSpec((1, cut, pixel_count, width), lambda i: (i, 0, 0, 0))] * chunks,
        out_shape=[jax.ShapeDtypeStruct((steps, cut, pixel_count, width), bf16)] * chunks,
        compiler_params=pltpu.CompilerParams(vmem_limit_bytes=VMEM_LIMIT),
        cost_estimate=COST,
        name="gen_grad",
    )(*parts, *grads, *others)


def pixel_kernel(hyper_ref, pix_ref, g0, g1, g2, g3, *refs):
    grad_ref, total_ref = refs[-2:]
    slots, rows, pixel_count = pix_ref.shape
    entries = hyper_ref.shape[1]

    @pl.when(pl.program_id(0) == 0)
    def _():
        total_ref[...] = jnp.zeros_like(total_ref)

    grad = jnp.concatenate([g[...] for g in (g0, g1, g2, g3)], axis=0)
    grad = grad.reshape(entries, rows * pixel_count)
    pix = pix_ref[...].reshape(slots, rows * pixel_count)
    out = dense_dot(hyper_ref[...], grad).astype(bf16)
    grad_ref[...] = out.reshape(slots, rows, pixel_count)
    total_ref[...] += right_dot(pix, grad)


def pixel_back(hyper, pixel_rows, parts, start, before=()):
    slots, entries = hyper.shape
    _, row_count, pixel_count = pixel_rows.shape
    share, rows, _ = parts[0].shape
    block = pl.BlockSpec((slots, MIX_ROWS, pixel_count), lambda i: (0, start // MIX_ROWS + i, 0))
    return pl.pallas_call(
        pixel_kernel,
        grid=(rows // MIX_ROWS,),
        in_specs=[pl.BlockSpec((slots, entries), lambda i: (0, 0)), block]
        + [pl.BlockSpec((share, MIX_ROWS, pixel_count), lambda i: (0, i, 0))] * 4
        + [pl.BlockSpec(memory_space=pl.ANY)] * len(before),
        out_specs=[block, pl.BlockSpec((slots, entries), lambda i: (0, 0))],
        out_shape=[
            jax.ShapeDtypeStruct((slots, row_count, pixel_count), bf16),
            jax.ShapeDtypeStruct((slots, entries), f32),
        ],
        input_output_aliases={6: 0} if before else {},
        compiler_params=pltpu.CompilerParams(vmem_limit_bytes=VMEM_LIMIT),
        cost_estimate=COST,
        name="pixel_back",
    )(hyper, pixel_rows, *parts, *before)


def put_kernel(at_ref, *refs, count):
    for j in range(count):

        @pl.when(pl.program_id(0) == j)
        def _(j=j):
            refs[-1][...] = refs[j][...].astype(f32)


def put_parts(pieces, quarters, chunk, chunks, before=()):
    rows, width = pieces[0].shape
    count = len(pieces)
    return pl.pallas_call(
        functools.partial(put_kernel, count=count),
        grid_spec=pltpu.PrefetchScalarGridSpec(
            num_scalar_prefetch=1,
            grid=(count,),
            in_specs=[pl.BlockSpec((rows, width), lambda i, at_ref: (0, 0))] * count
            + [pl.BlockSpec(memory_space=pl.ANY)] * len(before),
            out_specs=pl.BlockSpec((rows, width), lambda i, at_ref: (at_ref[i] * chunks + chunk, 0)),
        ),
        out_shape=jax.ShapeDtypeStruct((4 * chunks * rows, width), f32),
        input_output_aliases={1 + count: 0} if before else {},
        compiler_params=pltpu.CompilerParams(vmem_limit_bytes=VMEM_LIMIT),
        cost_estimate=COST,
        name="put_parts",
    )(jnp.stack(quarters), *pieces, *before)


PAIR = [(0, 1), (1, 0)]
CORNER = [(i, i ^ 3) for i in range(4)]


def swap_core(value):
    return lax.ppermute(value, "c", PAIR)


def swap_x(value):
    return lax.ppermute(value, "x", PAIR)


def swap_y(value):
    return lax.ppermute(value, "y", PAIR)


def swap_plane(values):
    return [
        values[0],
        swap_y(values[1]),
        swap_x(values[2]),
        lax.ppermute(values[3], ("x", "y"), CORNER),
    ]


def after(values, *earlier):
    return lax.optimization_barrier((values, earlier))[0]


def pick(pieces, index):
    return lax.dynamic_index_in_dim(pieces, index, 0, keepdims=False)


UP, DOWN = ([(i, (i + step) % 4) for i in range(4)] for step in (1, 3))


def gather_z(own):
    size, at = lax.axis_size("z"), lax.axis_index("z")
    if size != 4:
        return lax.all_gather(own, "z", axis=0, tiled=False)
    half = own.shape[-2] // 2
    below, above = lax.ppermute(own, "z", UP), lax.ppermute(own, "z", DOWN)
    across = [
        lax.ppermute(below[..., :half, :], "z", UP),
        lax.ppermute(above[..., half:, :], "z", DOWN),
    ]
    out = jnp.zeros((4,) + own.shape, own.dtype)
    for piece, step in ((own, 0), (below, 3), (above, 1), (jnp.concatenate(across, axis=-2), 2)):
        out = lax.dynamic_update_index_in_dim(out, piece, (at + step) % 4, 0)
    return out


def scatter_z(pieces):
    size, at = lax.axis_size("z"), lax.axis_index("z")
    if size != 4:
        return lax.psum_scatter(pieces, "z", scatter_dimension=0, tiled=False)
    half = pieces.shape[-2] // 2
    own, above, across, below = (pick(pieces, (at + step) % 4) for step in range(4))
    from_below = lax.ppermute(across[..., :half, :], "z", UP)
    from_above = lax.ppermute(across[..., half:, :], "z", DOWN)
    above = jnp.concatenate([add_low(above[..., :half, :], from_below), above[..., half:, :]], axis=-2)
    below = jnp.concatenate([below[..., :half, :], add_low(below[..., half:, :], from_above)], axis=-2)
    total = own.astype(f32) + lax.ppermute(above, "z", UP).astype(f32)
    return (total + lax.ppermute(below, "z", DOWN).astype(f32)).astype(bf16)


def gather_quarters(own, quarter):
    across = swap_x(own)
    away = jnp.stack([own, swap_core(own), across, swap_core(across)])
    return jnp.stack([pick(away, quarter ^ j) for j in range(4)])


def total_of(value, earlier):
    value = value + swap_core(value)
    value = value + swap_x(value)
    value = after(value, earlier)
    value = value + swap_y(value)
    size, step = lax.axis_size("z"), 1
    while step < size:
        value = value + lax.ppermute(value, "z", [(i, i ^ step) for i in range(size)])
        step *= 2
    return value


def reduce_core(blocks):
    return [split_y(add_low(blocks[2 * dx], swap_core(blocks[2 * dx + 1]))) for dx in range(2)]


def add_low(left, right):
    return (left.astype(f32) + right.astype(f32)).astype(bf16)


def split_y(block):
    size = lax.axis_size("z")
    return block.reshape(size, 2, block.shape[0] // size // 2, block.shape[1])


def of_y(block, y):
    return lax.dynamic_index_in_dim(block, y, 1, keepdims=False)


def join_y(own, other):
    at_y = lax.axis_index("y")
    both = [jnp.where(at_y == 0, own, other), jnp.where(at_y == 0, other, own)]
    return jnp.stack(both, axis=1).reshape(-1, own.shape[-1])


def gather_start(column):
    half = column.shape[0] // 2
    return swap_y(column[:half]), swap_x(column[half:])


def gather_more(column, came):
    half, kinds = column.shape[0] // 2, column.shape[1]
    low = jnp.stack([join_y(column[:half, kind], came[0][:, kind]) for kind in range(kinds)])
    high = jnp.stack([column[half:], came[1]])
    return low, high


def gather_end(low, high, low_x, high_y):
    return [
        [
            jnp.concatenate([from_low[kind], join_y(high[dx][:, kind], high_y[dx][:, kind])])
            for dx, from_low in enumerate((low, low_x))
        ]
        for kind in range(low.shape[0])
    ]


def sum_start(blocks):
    at_y, half = lax.axis_index("y"), blocks[0][0].shape[0] // 2
    to_y = jnp.stack([jnp.stack([of_y(b[:half], 1 - at_y) for b in pair]) for pair in blocks])
    return to_y, jnp.stack([pair[1][half:] for pair in blocks])


def sum_more(blocks, from_y, from_x):
    at_y, half = lax.axis_index("y"), blocks[0][0].shape[0] // 2
    low = [
        jnp.stack([add_low(of_y(pair[dx][:half], at_y), from_y[kind, dx]) for kind, pair in enumerate(blocks)])
        for dx in range(2)
    ]
    high = [
        jnp.stack([add_low(of_y(pair[0][half:], y), of_y(from_x[kind], y)) for kind, pair in enumerate(blocks)])
        for y in (at_y, 1 - at_y)
    ]
    return low[0], high[0], low[1], high[1]


def sum_end(low, high, low_x, high_y):
    return jnp.concatenate([add_low(low, low_x), add_low(high, high_y)], axis=1).swapaxes(0, 1)


def body(
    pixels,
    wave_table,
    wave_weight,
    wave_bias,
    gen_weight,
    patch_bias,
    norm1_gain,
    norm1_bias,
    qkv_weight,
    query_bias,
    value_bias,
    out_weight,
    out_bias,
    norm2_gain,
    norm2_bias,
    fc1_weight,
    fc1_bias,
    fc2_weight,
    fc2_bias,
    band_count,
    band_table,
    cotangent,
):
    tile_count, seq_len, band_slots, pixel_count = pixels.shape[1:]
    model_width = gen_weight.shape[1]
    wave_width = wave_weight.shape[0]
    hidden_width = fc1_weight.shape[1]
    head_size = model_width // HEADS
    score_scale = head_size ** (-0.5)
    row_count = tile_count * seq_len
    head_shape = (tile_count, seq_len, HEADS, head_size)
    z_size = lax.axis_size("z")
    row_size = 2 * z_size
    at_x, at_c, at_y = lax.axis_index("x"), lax.axis_index("c"), lax.axis_index("y")
    quarter = 2 * at_x + at_c
    shard = qkv_weight.shape[0]
    unit = hidden_width // row_size // 4

    gen_rows = gen_weight.shape[0] // 4
    own_rows = lax.dynamic_slice_in_dim(gen_weight, quarter * gen_rows, gen_rows, 0)
    near = lax.all_gather(own_rows, "z", axis=0, tiled=True)

    unit_order = fc1_bias.reshape(row_size, 4, unit).transpose(1, 0, 2).reshape(4, row_size * unit)
    bias_fc1 = [pick(unit_order, quarter ^ d) for d in range(4)]

    onehot = (band_table[0][:, None] == jnp.arange(wave_table.shape[0])[None, :]).astype(f32)
    wavelength = jnp.dot(onehot, wave_table, precision=highest)
    wave_embed = sincos(wavelength * 1000.0, wave_width)
    live = (jnp.arange(band_slots) < band_count[0]).astype(f32)[:, None]

    def hyper_fn(weight, bias):
        return jax.nn.gelu(jnp.dot(wave_embed, weight, precision=highest) + bias) * live

    hyper, hyper_back = jax.vjp(hyper_fn, wave_weight.astype(f32), wave_bias)
    per_row = wave_width // row_size
    place = jnp.arange(wave_width)
    kk = place % (per_row // 4)
    place = place // (per_row // 4)
    entry_z = place % z_size
    place = place // z_size
    entry_c, entry_y, entry_x = (place % 2) ^ at_c, (place // 2 % 2) ^ at_y, (place // 4) ^ at_x
    entry = per_row * (2 * entry_z + entry_y) + per_row // 4 * (2 * entry_x + entry_c) + kk
    order = (jnp.arange(wave_width)[:, None] == entry[None, :]).astype(bf16)
    hyper_low = dense_dot(hyper.astype(bf16), order).astype(bf16)

    pixel_rows = pixels.reshape(row_count, band_slots, pixel_count).transpose(1, 0, 2)
    mixed_pixels = mix_pixels(hyper_low.T, pixel_rows)
    patches = swap_plane(mixed_pixels)

    weights = (qkv_weight, out_weight, fc1_weight, fc2_weight)
    qkv_weight, out_weight, fc1_weight, fc2_weight = after(weights, mixed_pixels)
    attn_piece = pick(
        jnp.stack(
            [qkv_weight[:, j * model_width : (j + 1) * model_width] for j in range(3)] + [out_weight]
        ),
        quarter,
    )
    fc1_piece = lax.dynamic_index_in_dim(fc1_weight.reshape(shard, row_size, 4, unit), quarter, 2, False)
    fc1_piece = fc1_piece.reshape(shard, row_size * unit)
    fc2_piece = pick(fc2_weight.reshape(4, unit, model_width), quarter)
    column = gather_z(jnp.stack([attn_piece, fc1_piece, fc2_piece]))
    low, high = gather_more(column, gather_start(column))
    low, high, patches = after((low, high, patches))
    near = after(near, low, high)
    far = swap_core(near)
    near = near.reshape(-1, pixel_count, model_width)
    far = far.reshape(-1, pixel_count, model_width)
    attn_came = swap_x(low[:1]), swap_y(high[:, :, :1])
    partial = project(patches, far, 1, (project(patches, near, 0),))
    partial = [partial[j * row_count : (j + 1) * row_count] for j in range(4)]
    partial = [partial[0]] + swap_plane([piece.astype(bf16) for piece in partial])[1:]
    projected = (partial[0] + partial[1]) + (partial[2] + partial[3])
    attn_came, fc_low, fc_high = after((attn_came, low[1:], high[:, :, 1:]), projected)
    fc_came = swap_x(fc_low), swap_y(fc_high)

    def both_cores(blocks):
        return [block for owned in blocks for block in (owned, swap_core(owned))]

    attn = jnp.stack(both_cores(gather_end(low[:1], high[:, :, :1], *attn_came)[0]))
    w_query, w_key, w_value, w_out = (pick(attn, j ^ quarter) for j in range(4))
    position = sincos(jnp.arange(seq_len).astype(f32), model_width)
    embedded = (projected + patch_bias).reshape(tile_count, seq_len, model_width) + position
    embedded = embedded.reshape(row_count, model_width)

    normed = layer_norm(embedded, norm1_gain, norm1_bias).astype(bf16)
    queries = (dense_dot(normed, w_query) + query_bias).astype(bf16).reshape(head_shape)
    key_rows = dense_dot(normed, w_key).astype(bf16).reshape(head_shape)
    value_rows = (dense_dot(normed, w_value) + value_bias).astype(bf16).reshape(head_shape)
    scores = (
        jnp.einsum("tqhd,tkhd->thqk", queries, key_rows, preferred_element_type=f32) * score_scale
    )
    probs_full = jax.nn.softmax(scores, axis=-1)
    probs = probs_full.astype(bf16)
    attended = (
        jnp.einsum("thqk,tkhd->tqhd", probs, value_rows, preferred_element_type=f32)
        .astype(bf16)
        .reshape(row_count, model_width)
    )
    middle = embedded + dense_dot(attended, w_out) + out_bias
    fc_came = after(fc_came, middle)
    w_fc1, w_fc2 = (both_cores(blocks) for blocks in gather_end(fc_low, fc_high, *fc_came))
    normed_two = layer_norm(middle, norm2_gain, norm2_bias).astype(bf16)
    fc_pre = [dense_dot(normed_two, w) + bias for w, bias in zip(w_fc1, bias_fc1)]
    hidden, gelu_back = zip(*(jax.vjp(jax.nn.gelu, values) for values in fc_pre))
    hidden = [values.astype(bf16) for values in hidden]
    block_out = middle + sum(dense_dot(values, w) for values, w in zip(hidden, w_fc2)) + fc2_bias

    grad_out = cotangent.reshape(row_count, model_width)
    fc2_bias_part = row_total(grad_out)
    grad_pre = [
        back(right_dot(grad_out, w))[0].astype(bf16) for back, w in zip(gelu_back, w_fc2)
    ]
    fc1_bias_part = jnp.stack([row_total(values) for values in grad_pre])
    fc1_bias_part = jnp.stack([pick(fc1_bias_part, quarter ^ j) for j in range(4)])
    fc1_bias_part = fc1_bias_part.reshape(4, row_size, unit).transpose(1, 0, 2).reshape(-1)
    grad_normed_two = sum(right_dot(values, w) for values, w in zip(grad_pre, w_fc1))
    norm_two_back = jax.vjp(layer_norm, middle, norm2_gain, norm2_bias)[1]
    grad_middle, norm2_gain_part, norm2_bias_part = norm_two_back(grad_normed_two)
    grad_middle = grad_middle + grad_out.astype(f32)
    grad_branch = grad_middle.astype(bf16)
    out_bias_part = row_total(grad_branch)
    grad_attended = right_dot(grad_branch, w_out).astype(bf16).reshape(head_shape)
    grad_probs = jnp.einsum(
        "tqhd,tkhd->thqk", grad_attended, value_rows, preferred_element_type=f32
    )
    grad_scores = probs_full * (
        grad_probs - jnp.sum(probs_full * grad_probs, axis=-1, keepdims=True)
    )
    grad_scores = grad_scores.astype(bf16)
    grad_queries = (
        jnp.einsum("thqk,tkhd->tqhd", grad_scores, key_rows, preferred_element_type=f32)
        * score_scale
    ).astype(bf16)
    grad_keys = (
        jnp.einsum("thqk,tqhd->tkhd", grad_scores, queries, preferred_element_type=f32)
        * score_scale
    ).astype(bf16)
    grad_values = jnp.einsum(
        "thqk,tqhd->tkhd", probs, grad_attended, preferred_element_type=f32
    ).astype(bf16)
    grad_queries = grad_queries.reshape(row_count, model_width)
    grad_values = grad_values.reshape(row_count, model_width)
    grad_keys = grad_keys.reshape(row_count, model_width)
    query_bias_part = row_total(grad_queries)
    value_bias_part = row_total(grad_values)
    grad_normed = right_dot(grad_queries, w_query)
    grad_normed += right_dot(grad_keys, w_key)
    grad_normed += right_dot(grad_values, w_value)
    norm_one_back = jax.vjp(layer_norm, embedded, norm1_gain, norm1_bias)[1]
    grad_from_norm, norm1_gain_part, norm1_bias_part = norm_one_back(grad_normed)
    grad_embedded = (grad_middle + grad_from_norm).astype(bf16)
    patch_bias_part = row_total(grad_embedded)

    grads = swap_plane([grad_embedded] * 4)
    (far_grad,) = gen_grad(patches, grads, 1)
    far_grad = swap_core(far_grad.reshape(-1, pixel_count, model_width))
    early = early_rows(row_count)
    back_early = back_patches(grads, near, far, 0, early)
    far_grad = after(far_grad, back_early)
    back_early = swap_plane(back_early)
    chunks = 2 if wave_width // row_size // 4 == GEN_STEP else 1
    gen_sent = gen_grad(patches, grads, 0, (far_grad,), chunks)
    gen_parts = [
        lax.psum_scatter(chunk.reshape(-1, model_width), "z", scatter_dimension=0, tiled=True)
        for chunk in gen_sent
    ]

    left = jnp.stack([normed, normed, normed, attended])
    right = jnp.stack([grad_queries, grad_keys, grad_values, grad_branch])
    near_first = [0, 2, 1, 3]
    left = jnp.stack([pick(left, quarter ^ d) for d in near_first])
    right = jnp.stack([pick(right, quarter ^ d) for d in near_first])
    hidden, grad_pre = (jnp.stack([values[d] for d in near_first]) for values in (hidden, grad_pre))
    sides = [(left, right), (jnp.stack([normed_two] * 2), grad_pre), (hidden, jnp.stack([grad_out] * 2))]
    sides = after(sides, gen_sent)

    def block_grad(side, part):
        return jnp.einsum(
            "dri,drj->dij", *(v if v.shape[0] == 2 else v[part : part + 2] for v in side), preferred_element_type=f32
        ).astype(bf16)

    block_grads = [swap_core(block_grad(side, 2)) for side in sides]
    block_grads = [add_low(block_grad(side, 0), came) for side, came in zip(sides, block_grads)]
    block_grads = [[split_y(pair[dx]) for dx in range(2)] for pair in block_grads]
    to_y, to_x = sum_start(block_grads)
    back_late = back_patches(after(grads, gen_sent), near, far, early, row_count - early)
    to_y, to_x, back_early, back_late = after((to_y, to_x, back_early, back_late))
    back_late = swap_plane(back_late)
    from_y, from_x = swap_y(to_y), swap_x(to_x)
    pixel_grad, hyper_early = pixel_back(hyper_low, pixel_rows, back_early, 0)
    back_late, from_y, from_x, hyper_early = after((back_late, from_y, from_x, hyper_early))
    low, high, low_sent, high_sent = sum_more(block_grads, from_y, from_x)
    low_x, high_y = swap_x(low_sent), swap_y(high_sent)
    across = [swap_x(gen_parts[0])]
    pixel_grad, hyper_late = pixel_back(hyper_low, pixel_rows, back_late, early, (pixel_grad,))
    low_x, high_y, hyper_late = after((low_x, high_y, hyper_late), across)
    across += [swap_x(piece) for piece in gen_parts[1:]]
    share_sum = scatter_z(sum_end(low, high, low_x, high_y))
    totals = gather_quarters(share_sum, quarter).astype(f32)
    qkv_total = jnp.concatenate([totals[0, 0], totals[1, 0], totals[2, 0]], axis=1)
    out_total = totals[3, 0]
    fc1_total = totals[:, 1].reshape(4, shard, row_size, unit).transpose(1, 2, 0, 3)
    fc1_total = fc1_total.reshape(shard, hidden_width)
    fc2_total = totals[:, 2].reshape(4 * unit, model_width)

    grad_hyper = hyper_early + hyper_late
    grad_hyper = lax.dot_general(
        grad_hyper, order.astype(f32), (((1,), (1,)), ((), ())), precision=highest
    )
    wave_weight_part, wave_bias_part = hyper_back(grad_hyper)
    small = (
        patch_bias_part,
        norm1_gain_part,
        norm1_bias_part,
        query_bias_part,
        value_bias_part,
        out_bias_part,
        norm2_gain_part,
        norm2_bias_part,
        fc2_bias_part,
        fc1_bias_part,
    )
    small = jnp.concatenate(small + (wave_bias_part,)).reshape(-1, wave_width)
    small = total_of(jnp.concatenate([wave_weight_part, small]), across)
    gen_total = ()
    for chunk, piece in enumerate(gen_parts):
        pair = piece, swap_core(piece)
        gen_total = (put_parts(pair, (quarter, quarter ^ 1), chunk, chunks, gen_total),)
        pair = across[chunk], swap_core(across[chunk])
        gen_total = (put_parts(pair, (quarter ^ 2, quarter ^ 3), chunk, chunks, gen_total),)
    gen_total = gen_total[0]
    wave_weight_total, small = small[:wave_width], small[wave_width:].reshape(-1)
    cuts = [model_width * j for j in range(1, 10)] + [9 * model_width + hidden_width]
    (
        patch_bias_total,
        norm1_gain_total,
        norm1_bias_total,
        query_bias_total,
        value_bias_total,
        out_bias_total,
        norm2_gain_total,
        norm2_bias_total,
        fc2_bias_total,
        fc1_bias_total,
        wave_bias_total,
    ) = jnp.split(small, cuts)
    block_result = block_out.astype(bf16).reshape(1, tile_count, seq_len, model_width)
    pixel_result = pixel_grad.transpose(1, 0, 2).reshape(1, tile_count, seq_len, band_slots, pixel_count)
    return (
        block_result,
        pixel_result,
        wave_weight_total,
        wave_bias_total,
        gen_total,
        patch_bias_total,
        norm1_gain_total,
        norm1_bias_total,
        qkv_total,
        query_bias_total,
        value_bias_total,
        out_total,
        out_bias_total,
        norm2_gain_total,
        norm2_bias_total,
        fc1_total,
        fc1_bias_total,
        fc2_total,
        fc2_bias_total,
    )


def solution(mesh):
    grp_size, row_size = mesh.devices.shape
    split = Mesh(mesh.devices.reshape(grp_size // 2, 2, row_size // 2, 2), AXES)
    grp, row = ("x", "c"), ("z", "y")
    return jax.shard_map(
        body,
        mesh=split,
        in_specs=(
            P(grp, row, None, None, None),
            P(),
            P(),
            P(),
            P(row, None),
            P(),
            P(),
            P(),
            P(row, None),
            P(),
            P(),
            P(row, None),
            P(),
            P(),
            P(),
            P(row, None),
            P(),
            P(row, None),
            P(),
            P(grp),
            P(grp, None),
            P(grp, row, None, None),
        ),
        out_specs=(
            P(grp, row, None, None),
            P(grp, row, None, None, None),
            P(),
            P(),
            P(row, None),
            P(),
            P(),
            P(),
            P(row, None),
            P(),
            P(),
            P(row, None),
            P(),
            P(),
            P(),
            P(row, None),
            P(),
            P(row, None),
            P(),
        ),
        check_vma=False,
    )
```

time: 1050 us -> 592 us (0.56)
  waiting for transfers between devices: 731 us -> 257 us
  blocking collectives: 41.2 us -> 0 us
  starting transfers between devices: 20 us -> 60.6 us
  Pallas kernels: 70.3 us -> 94.5 us
    all_gather x3 -> x0, waiting for transfers between devices: 123 us -> none  [the longest x1 65.2 us: body(): gathered = lax.all_gather(own_pieces, ('z', 'y'), axis=0, tiled=False)]
    all_gather x1, waiting for transfers between devices: 112 us -> 0.02 us  [body(): near = lax.all_gather(own_rows, 'z', axis=0, tiled=True)]
    ppermute x4 -> x5, waiting for transfers between devices: 128 us -> 47.3 us  [swap_plane(): lax.ppermute(values[3], ('x', 'y'), CORNER)]
    ppermute x3 -> x14, waiting for transfers between devices: 109 us -> 44.5 us  [swap_x(): return lax.ppermute(value, 'x', PAIR)]
    psum x1 -> x0, waiting for transfers between devices: 64.2 us -> none  [body(): lax.psum(jnp.concatenate([wave_weight_part, wave_bias_part[None]], axis=0...]
    psum x1 -> x0, blocking collectives: 41.2 us -> none  [body(): early_total = lax.psum(jnp.concatenate(early), axes)]
    reduce_scatter x2, waiting for transfers between devices: 34.8 us -> 0.01 us  [body(): lax.psum_scatter(chunk.reshape(-1, model_width), 'z', scatter_dimension=0...]
    pallas_call x5 -> x12, Pallas kernels: 57.2 us -> 81.4 us  [the longest x2 22.3 us: back_patches(): pl.pallas_call(back_kernel, grid=(2 * steps,), in_specs=[pl.BlockSpec((ro...]
  transfers between devices with their start and end apart: 26 -> 61, of which waited for: 18 -> 25; matrix products, arithmetic and copies ran while one was open for 9% -> 17% of each run, Pallas kernels for 6% -> 14%
where the time goes in v2:
time: 592 us; the launch traced here: 585 us
  waiting for transfers between devices  257 us (43%)
  Pallas kernels  94.5 us (16%)
  local copies, waits for them, and re-layouts  65.1 us (11%)
  starting transfers between devices  60.6 us (10%)
  matrix products  46.2 us (8%)
  other arithmetic  43.8 us (7%)
  between operations  17.4 us (3%)
    ppermute x11, waiting for transfers between devices, swap_y(): return lax.ppermute(value, 'y', PAIR)  90.8 us
    ppermute x5, waiting for transfers between devices, swap_plane(): lax.ppermute(values[3], ('x', 'y'), CORNER)  47.3 us
    ppermute x14, waiting for transfers between devices, swap_x(): return lax.ppermute(value, 'x', PAIR)  44.5 us
    ppermute x2, waiting for transfers between devices, gather_z(): below, above = (lax.ppermute(own, 'z', UP), lax.ppermute(own, 'z', DOWN))  36.3 us
    pallas_call x2, Pallas kernels, back_patches(): pl.pallas_call(back_kernel, grid=(2 * steps,), in_specs=[pl.BlockSpec((ro...  22.3 us
    pallas_call x2, Pallas kernels, pixel_back(): pl.pallas_call(pixel_kernel, grid=(rows // MIX_ROWS,), in_specs=[pl.Block...  21.1 us
    ppermute x2, waiting for transfers between devices, total_of(): lax.ppermute(value, 'z', [(i, i ^ step) for i in range(size)])  20.5 us
    unnamed x330, local copies, waits for them, and re-layouts  19.8 us
  transfers between devices with their start and end apart: 61, of which 25 were waited for; matrix products, arithmetic and copies ran while one was open for 17% of the time, Pallas kernels for 14%

profile of v2, /device:TPU:0, one launch (start us, length us, event | category | flops | bytes accessed | tf_op | source)
XLA Modules:
  0.0 584.8 jit_solution(14871030654491420983)
XLA Ops:
  7.3 2.7 constant_dynamic-slice_fusion.20
  13.2 13.1 %mix_pixels.1 = (bf16[32,128,256]{2,1,0:T(8,128)(2,1)S(1)}, bf16[32,128,256]{2,1,0:T(8,128)(2,1)}, bf16[32,128,256]{2,1,0:T(8,128)(2,1)}, bf16[32,128,256]{2,1,0:T(8,128)(2,1)}) custom-call(bf16[128,202]{1,0:T(8,128)(2,1)S(1)} %copy.143.hyper_ref, bf16[202,128,256]{2,1,0:T(8,128)(2,1)} %bitcast.457), custom_call_target="tpu_custom_call" | custom-call | flops 1 | bytes 1 | tf_op jit(solution)/shard_map/mix_pixels/pallas_call | solution.py:69
  33.7 5.1 collective-permute-start.1
  42.5 34.9 %collective-permute-done.1 = bf16[3,96,768]{2,1,0:T(8,128)(2,1)S(1)} collective-permute-done((bf16[3,96,768]{2,1,0:T(8,128)(2,1)}, bf16[3,96,768]{2,1,0:T(8,128)(2,1)S(1)}, u32[]{:S(2)}, u32[]{:S(2)}) %collective-permute-start.1) | collective-permute-done | bytes 442400 | tf_op jit(solution)/shard_map/ppermute | solution.py:308
  81.1 17.7 %collective-permute-done.3 = bf16[3,48,768]{2,1,0:T(8,128)(2,1)S(1)} collective-permute-done((bf16[3,48,768]{2,1,0:T(8,128)(2,1)S(1)}, bf16[3,48,768]{2,1,0:T(8,128)(2,1)S(1)}, u32[]{:S(2)}, u32[]{:S(2)}) %collective-permute-start.3) | collective-permute-done | bytes 221216 | tf_op jit(solution)/shard_map/ppermute | solution.py:311
  100.9 2.4 collective-permute-start.4
  103.3 2.8 collective-permute-start.5
  106.1 45.9 %collective-permute-done.4 = bf16[2,3,96,768]{3,2,1,0:T(8,128)(2,1)} collective-permute-done((bf16[2,3,96,768]{3,2,1,0:T(8,128)(2,1)}, bf16[2,3,96,768]{3,2,1,0:T(8,128)(2,1)}, u32[]{:S(2)}, u32[]{:S(2)}) %collective-permute-start.4) | collective-permute-done | bytes 884768 | tf_op jit(solution)/shard_map/ppermute | solution.py:280
  154.7 2.6 pad_maximum_fusion.2
  165.9 6.7 %project.2.refs_5_ = f32[512,768]{1,0:T(8,128)S(1)} custom-call(bf16[32,128,256]{2,1,0:T(8,128)(2,1)S(1)} %get-tuple-element.94.refs_0_, bf16[32,128,256]{2,1,0:T(8,128)(2,1)} %collective-permute-done.6.refs_1_, bf16[32,128,256]{2,1,0:T(8,128)(2,1)} %collective-permute-done.7.refs_2_, bf16[32,128,256]{2,1,0:T(8,128)(2,1)} %collective-permute-done.8.refs_3_, ...), custom_call_target="tpu_custom_call" | custom-call | flops 1 | bytes 1 | tf_op jit(solution)/shard_map/project/pallas_call | solution.py:107
  172.6 2.7 copy-done.12
  175.3 6.7 %project.3 = f32[512,768]{1,0:T(8,128)S(1)} custom-call(bf16[32,128,256]{2,1,0:T(8,128)(2,1)S(1)} %get-tuple-element.94.refs_0_, bf16[32,128,256]{2,1,0:T(8,128)(2,1)} %collective-permute-done.6.refs_1_, bf16[32,128,256]{2,1,0:T(8,128)(2,1)} %collective-permute-done.7.refs_2_, bf16[32,128,256]{2,1,0:T(8,128)(2,1)} %collective-permute-done.8.refs_3_, ...), custom_call_target="tpu_custom_call" | custom-call | flops 1 | bytes 1 | tf_op jit(solution)/shard_map/project/pallas_call | solution.py:107
  189.9 3.2 collective-permute-done.12
  197.1 2.6 fusion.163
  223.2 7.7 %collective-permute-done.17 = bf16[2,384,768]{2,1,0:T(8,128)(2,1)} collective-permute-done((bf16[2,384,768]{2,1,0:T(8,128)(2,1)}, bf16[2,384,768]{2,1,0:T(8,128)(2,1)}, u32[]{:S(2)}, u32[]{:S(2)}) %collective-permute-start.17) | collective-permute-done | bytes 1179680 | tf_op jit(solution)/shard_map/ppermute | solution.py:276
  252.8 3.1 convert_reduce_fusion.6
  268.3 3.2 collective-permute-done.23.refs_5_.g1
  271.5 2.4 collective-permute-done.24.refs_6_.g2
  273.9 3.0 collective-permute-done.25.refs_7_.g3
  276.9 7.1 %gen_grad.2 = bf16[4,4,256,768]{3,2,1,0:T(8,128)(2,1)} custom-call(bf16[32,128,256]{2,1,0:T(8,128)(2,1)S(1)} %get-tuple-element.94.refs_0_, bf16[32,128,256]{2,1,0:T(8,128)(2,1)} %collective-permute-done.6.refs_1_, bf16[32,128,256]{2,1,0:T(8,128)(2,1)} %collective-permute-done.7.refs_2_, bf16[32,128,256]{2,1,0:T(8,128)(2,1)} %collective-permute-done.8.refs_3_, ...), custom_call_target="tpu_custom_call" | custom-call | flops 1 | bytes 1 | tf_op jit(solution)/shard_map/gen_grad/pallas_call | solution.py:185
  284.0 12.0 %back_patches.2 = (bf16[32,96,256]{2,1,0:T(8,128)(2,1)S(1)}, bf16[32,96,256]{2,1,0:T(8,128)(2,1)}, bf16[32,96,256]{2,1,0:T(8,128)(2,1)}, bf16[32,96,256]{2,1,0:T(8,128)(2,1)}) custom-call(bf16[128,768]{1,0:T(8,128)(2,1)S(1)} %get-tuple-element.120.refs_4_.g0, bf16[128,768]{1,0:T(8,128)(2,1)S(1)} %collective-permute-done.23.refs_5_.g1, ...), custom_call_target="tpu_custom_call" | custom-call | flops 1 | bytes 1 | tf_op jit(solution)/shard_map/back_patches/pallas_call | solution.py:151
  296.0 2.7 copy-done.24
  298.7 8.2 %gen_grad.3 = (bf16[4,2,256,768]{3,2,1,0:T(8,128)(2,1)}, bf16[4,2,256,768]{3,2,1,0:T(8,128)(2,1)}) custom-call(bf16[32,128,256]{2,1,0:T(8,128)(2,1)S(1)} %get-tuple-element.94.refs_0_, bf16[32,128,256]{2,1,0:T(8,128)(2,1)} %collective-permute-done.6.refs_1_, bf16[32,128,256]{2,1,0:T(8,128)(2,1)} %collective-permute-done.7.refs_2_, ...), custom_call_target="tpu_custom_call" | custom-call | flops 1 | bytes 1 | tf_op jit(solution)/shard_map/gen_grad/pallas_call | solution.py:185
  327.6 10.3 %back_patches.3 = (bf16[32,32,256]{2,1,0:T(8,128)(2,1)S(1)}, bf16[32,32,256]{2,1,0:T(8,128)(2,1)S(1)}, bf16[32,32,256]{2,1,0:T(8,128)(2,1)S(1)}, bf16[32,32,256]{2,1,0:T(8,128)(2,1)S(1)}) custom-call(bf16[128,768]{1,0:T(8,128)(2,1)S(1)} %get-tuple-element.120.refs_4_.g0, bf16[128,768]{1,0:T(8,128)(2,1)S(1)} %collective-permute-done.23.refs_5_.g1, ...), custom_call_target="tpu_custom_call" | custom-call | flops 1 | bytes 1 | tf_op jit(solution)/shard_map/back_patches/pallas_call | solution.py:151
  338.3 2.6 add_convert_fusion
  342.5 2.5 add_convert_fusion.1
  346.6 2.5 add_convert_fusion.2
  353.7 7.4 %collective-permute-done.30.g1 = bf16[32,96,256]{2,1,0:T(8,128)(2,1)} collective-permute-done((bf16[32,96,256]{2,1,0:T(8,128)(2,1)}, bf16[32,96,256]{2,1,0:T(8,128)(2,1)}, u32[]{:S(2)}, u32[]{:S(2)}) %collective-permute-start.30) | collective-permute-done | bytes 1572896 | tf_op jit(solution)/shard_map/ppermute | solution.py:280
  361.1 2.4 collective-permute-done.31.g2
  363.5 32.4 %collective-permute-done.32.g3 = bf16[32,96,256]{2,1,0:T(8,128)(2,1)} collective-permute-done((bf16[32,96,256]{2,1,0:T(8,128)(2,1)S(1)}, bf16[32,96,256]{2,1,0:T(8,128)(2,1)}, u32[]{:S(2)}, u32[]{:S(2)}) %collective-permute-start.32) | collective-permute-done | bytes 1572896 | tf_op jit(solution)/shard_map/ppermute | solution.py:288
  400.4 2.6 collective-permute-start.35
  403.4 14.6 %pixel_back.2 = (bf16[202,128,256]{2,1,0:T(8,128)(2,1)}, f32[202,128]{1,0:T(8,128)S(1)}) custom-call(bf16[202,128]{1,0:T(8,128)(2,1)S(1)} %convolution_convert_fusion.5.hyper_ref, bf16[202,128,256]{2,1,0:T(8,128)(2,1)} %bitcast.458, bf16[32,96,256]{2,1,0:T(8,128)(2,1)S(1)} %copy-done.3, bf16[32,96,256]{2,1,0:T(8,128)(2,1)} %collective-permute-done.30.g1, ...), custom_call_target="tpu_custom_call" | custom-call | flops 1 | bytes 1 | tf_op jit(solution)/shard_map/pixel_back/pallas_call | solution.py:221
  418.0 30.0 %collective-permute-done.33.g1 = bf16[32,32,256]{2,1,0:T(8,128)(2,1)S(1)} collective-permute-done((bf16[32,32,256]{2,1,0:T(8,128)(2,1)}, bf16[32,32,256]{2,1,0:T(8,128)(2,1)S(1)}, u32[]{:S(2)}, u32[]{:S(2)}) %collective-permute-start.33) | collective-permute-done | bytes 524320 | tf_op jit(solution)/shard_map/ppermute | solution.py:280
  448.0 2.6 collective-permute-done.34.g2
  450.5 8.7 %collective-permute-done.35.g3 = bf16[32,32,256]{2,1,0:T(8,128)(2,1)} collective-permute-done((bf16[32,32,256]{2,1,0:T(8,128)(2,1)S(1)}, bf16[32,32,256]{2,1,0:T(8,128)(2,1)}, u32[]{:S(2)}, u32[]{:S(2)}) %collective-permute-start.35) | collective-permute-done | bytes 524320 | tf_op jit(solution)/shard_map/ppermute | solution.py:288
  460.4 2.5 fusion.51
  472.5 6.5 %pixel_back.3 = (bf16[202,128,256]{2,1,0:T(8,128)(2,1)}, f32[202,128]{1,0:T(8,128)S(1)}) custom-call(bf16[202,128]{1,0:T(8,128)(2,1)S(1)} %convolution_convert_fusion.5.hyper_ref, bf16[202,128,256]{2,1,0:T(8,128)(2,1)} %bitcast.459, bf16[32,32,256]{2,1,0:T(8,128)(2,1)S(1)} %get-tuple-element.139.g0, ...), custom_call_target="tpu_custom_call", output_to_operand_aliasing={{0}: (6, {})} | custom-call | flops 1 | bytes 1 | tf_op jit(solution)/shard_map/pixel_back/pallas_call | solution.py:221
  481.5 5.3 collective-permute-done.38
  486.8 2.8 collective-permute-done.39
  489.6 13.9 %collective-permute-done.40.refs_0_ = bf16[512,768]{1,0:T(8,128)(2,1)S(1)} collective-permute-done((bf16[512,768]{1,0:T(8,128)(2,1)}, bf16[512,768]{1,0:T(8,128)(2,1)S(1)}, u32[]{:S(2)}, u32[]{:S(2)}) %collective-permute-start.40) | collective-permute-done | bytes 786464 | tf_op jit(solution)/shard_map/ppermute | solution.py:276
  507.9 3.6 collective-permute-start.53
  513.8 5.5 collective-permute-done.42
  521.1 3.6 collective-permute-start.54
  526.6 18.2 %collective-permute-done.45 = f32[207,128]{1,0:T(8,128)S(1)} collective-permute-done((f32[207,128]{1,0:T(8,128)S(1)}, f32[207,128]{1,0:T(8,128)S(1)}, u32[]{:S(2)}, u32[]{:S(2)}) %collective-permute-start.45) | collective-permute-done | bytes 106016 | tf_op jit(solution)/shard_map/ppermute | solution.py:346
  554.8 3.4 collective-permute-done.56
  559.4 2.3 put_parts.5.refs_2_
  564.1 2.3 put_parts.7
  573.4 3.7 reshape.1030
  (635 shorter events, 176.6 us)
Async XLA Ops:
  7.2 151.5 %all-gather.2.cloned.1.call-start = ((), (), s32[]{:S(2)}) async-start(), calls=%async_computation.2 | async-start | bytes 7864320 | tf_op jit(solution)/shard_map/all_gather | solution.py:460
  10.1 461.9 %reduce-scatter.3.cloned.1.call-start = ((), (), s32[]{:S(2)}) async-start(), calls=%async_computation.3 | async-start | bytes 3932160 | tf_op jit(solution)/shard_map/reduce_scatter | solution.py:603
  33.7 43.7 %collective-permute-start.1 = (bf16[3,96,768]{2,1,0:T(8,128)(2,1)}, bf16[3,96,768]{2,1,0:T(8,128)(2,1)S(1)}, u32[]{:S(2)}, u32[]{:S(2)}) collective-permute-start(bf16[3,96,768]{2,1,0:T(8,128)(2,1)} %pad_maximum_fusion.33), channel_id=1, source_target_pairs={{0,6},{2,0},{4,2},{6,4},{1,7},{3,1},{5,3},{7,5},{8,14},{10,8},{12,... | collective-permute-start | bytes 1327112 | tf_op jit(solution)/shard_map/ppermute | solution.py:308
  38.8 40.1 %collective-permute-start = (bf16[3,96,768]{2,1,0:T(8,128)(2,1)}, bf16[3,96,768]{2,1,0:T(8,128)(2,1)S(1)}, u32[]{:S(2)}, u32[]{:S(2)}) collective-permute-start(bf16[3,96,768]{2,1,0:T(8,128)(2,1)} %pad_maximum_fusion.33), channel_id=1, source_target_pairs={{0,2},{2,4},{4,6},{6,0},{1,3},{3,5},{5,7},{7,1},{8,10},{10,12},{12... | collective-permute-start | bytes 1327112 | tf_op jit(solution)/shard_map/ppermute | solution.py:308
  38.8 119.9 %collective-permute-start.6 = (bf16[32,128,256]{2,1,0:T(8,128)(2,1)}, bf16[32,128,256]{2,1,0:T(8,128)(2,1)}, u32[]{:S(2)}, u32[]{:S(2)}) collective-permute-start(bf16[32,128,256]{2,1,0:T(8,128)(2,1)} %get-tuple-element.87), channel_id=1, source_target_pairs={{0,1},{1,0},{2,3},{3,2},{4,5},{5,4},{6,7},{7,6},{8,9},{9,8},{10,11... | collective-permute-start | bytes 6291464 | tf_op jit(solution)/shard_map/ppermute | solution.py:280
  40.3 118.4 %collective-permute-start.7 = (bf16[32,128,256]{2,1,0:T(8,128)(2,1)}, bf16[32,128,256]{2,1,0:T(8,128)(2,1)}, u32[]{:S(2)}, u32[]{:S(2)}) collective-permute-start(bf16[32,128,256]{2,1,0:T(8,128)(2,1)} %get-tuple-element.88), channel_id=1, source_target_pairs={{0,16},{16,0},{1,17},{17,1},{2,18},{18,2},{3,19},{19,3},{4,20},{20... | collective-permute-start | bytes 6291464 | tf_op jit(solution)/shard_map/ppermute | solution.py:276
  41.8 116.9 %collective-permute-start.8 = (bf16[32,128,256]{2,1,0:T(8,128)(2,1)}, bf16[32,128,256]{2,1,0:T(8,128)(2,1)}, u32[]{:S(2)}, u32[]{:S(2)}) collective-permute-start(bf16[32,128,256]{2,1,0:T(8,128)(2,1)} %get-tuple-element.89), channel_id=1, source_target_pairs={{0,17},{1,16},{16,1},{17,0},{2,19},{3,18},{18,3},{19,2},{4,21},{5,... | collective-permute-start | bytes 6291464 | tf_op jit(solution)/shard_map/ppermute | solution.py:288
  77.4 21.4 %collective-permute-start.3 = (bf16[3,48,768]{2,1,0:T(8,128)(2,1)S(1)}, bf16[3,48,768]{2,1,0:T(8,128)(2,1)S(1)}, u32[]{:S(2)}, u32[]{:S(2)}) collective-permute-start(bf16[3,48,768]{2,1,0:T(8,128)(2,1)S(1)} %slice.437), channel_id=1, source_target_pairs={{0,6},{2,0},{4,2},{6,4},{1,7},{3,1},{5,3},{7,5},{8,14},{10,8},{12,... | collective-permute-start | bytes 663560 | tf_op jit(solution)/shard_map/ppermute | solution.py:311
  78.9 19.9 %collective-permute-start.2 = (bf16[3,48,768]{2,1,0:T(8,128)(2,1)S(1)}, bf16[3,48,768]{2,1,0:T(8,128)(2,1)S(1)}, u32[]{:S(2)}, u32[]{:S(2)}) collective-permute-start(bf16[3,48,768]{2,1,0:T(8,128)(2,1)S(1)} %slice.436), channel_id=1, source_target_pairs={{0,2},{2,4},{4,6},{6,0},{1,3},{3,5},{5,7},{7,1},{8,10},{10,12},{12... | collective-permute-start | bytes 663560 | tf_op jit(solution)/shard_map/ppermute | solution.py:310
  100.9 51.0 %collective-permute-start.4 = (bf16[2,3,96,768]{3,2,1,0:T(8,128)(2,1)}, bf16[2,3,96,768]{3,2,1,0:T(8,128)(2,1)}, u32[]{:S(2)}, u32[]{:S(2)}) collective-permute-start(bf16[2,3,96,768]{3,2,1,0:T(8,128)(2,1)} %get-tuple-element.219), channel_id=1, source_target_pairs={{0,1},{1,0},{2,3},{3,2},{4,5},{5,4},{6,7},{7,6},{8,9},{9,8},{10,11... | collective-permute-start | bytes 2654216 | tf_op jit(solution)/shard_map/ppermute | solution.py:280
  103.3 50.4 %collective-permute-start.5 = (bf16[2,3,96,768]{3,2,1,0:T(8,128)(2,1)}, bf16[2,3,96,768]{3,2,1,0:T(8,128)(2,1)}, u32[]{:S(2)}, u32[]{:S(2)}) collective-permute-start(bf16[2,3,96,768]{3,2,1,0:T(8,128)(2,1)} %get-tuple-element.218), channel_id=1, source_target_pairs={{0,16},{16,0},{1,17},{17,1},{2,18},{18,2},{3,19},{19,3},{4,20},{20... | collective-permute-start | bytes 2654216 | tf_op jit(solution)/shard_map/ppermute | solution.py:276
  158.7 13.8 %collective-permute-start.9 = (bf16[4096,768]{1,0:T(8,128)(2,1)}, bf16[4096,768]{1,0:T(8,128)(2,1)S(1)}, u32[]{:S(2)}, u32[]{:S(2)}) collective-permute-start(bf16[4096,768]{1,0:T(8,128)(2,1)} %all-gather.2.cloned.1.call-done), channel_id=1, source_target_pairs={{0,8},{8,0},{1,9},{9,1},{2,10},{10,2},{3,11},{11,3},{4,12},{12,4},... | collective-permute-start | bytes 18874376 | tf_op jit(solution)/shard_map/ppermute | solution.py:272
  161.7 33.0 %collective-permute-start.13 = (bf16[1,384,768]{2,1,0:T(8,128)(2,1)}, bf16[1,384,768]{2,1,0:T(8,128)(2,1)}, u32[]{:S(2)}, u32[]{:S(2)}) collective-permute-start(bf16[1,384,768]{2,1,0:T(8,128)(2,1)} %get-tuple-element.216), channel_id=1, source_target_pairs={{0,16},{16,0},{1,17},{17,1},{2,18},{18,2},{3,19},{19,3},{4,20},{20... | collective-permute-start | bytes 1769480 | tf_op jit(solution)/shard_map/ppermute | solution.py:276
  164.3 30.4 %collective-permute-start.14 = (bf16[2,2,1,96,768]{4,3,1,2,0:T(8,128)(2,1)}, bf16[2,2,1,96,768]{4,3,1,2,0:T(8,128)(2,1)}, u32[]{:S(2)}, u32[]{:S(2)}) collective-permute-start(bf16[2,2,1,96,768]{4,3,1,2,0:T(8,128)(2,1)} %slice.451), channel_id=1, source_target_pairs={{0,1},{1,0},{2,3},{3,2},{4,5},{5,4},{6,7},{7,6},{8,9},{9,8},{10,11... | collective-permute-start | bytes 1769480 | tf_op jit(solution)/shard_map/ppermute | solution.py:280
  182.4 10.7 %collective-permute-start.12 = (bf16[128,768]{1,0:T(8,128)(2,1)S(1)}, bf16[128,768]{1,0:T(8,128)(2,1)S(1)}, u32[]{:S(2)}, u32[]{:S(2)}) collective-permute-start(bf16[128,768]{1,0:T(8,128)(2,1)S(1)} %get-tuple-element.253), channel_id=1, source_target_pairs={{0,17},{1,16},{16,1},{17,0},{2,19},{3,18},{18,3},{19,2},{4,21},{5,... | collective-permute-start | bytes 589832 | tf_op jit(solution)/shard_map/ppermute | solution.py:288
  184.1 10.4 %collective-permute-start.10 = (bf16[128,768]{1,0:T(8,128)(2,1)S(1)}, bf16[128,768]{1,0:T(8,128)(2,1)S(1)}, u32[]{:S(2)}, u32[]{:S(2)}) collective-permute-start(bf16[128,768]{1,0:T(8,128)(2,1)S(1)} %get-tuple-element.252), channel_id=1, source_target_pairs={{0,1},{1,0},{2,3},{3,2},{4,5},{5,4},{6,7},{7,6},{8,9},{9,8},{10,11... | collective-permute-start | bytes 589832 | tf_op jit(solution)/shard_map/ppermute | solution.py:280
  202.7 28.2 %collective-permute-start.17 = (bf16[2,384,768]{2,1,0:T(8,128)(2,1)}, bf16[2,384,768]{2,1,0:T(8,128)(2,1)}, u32[]{:S(2)}, u32[]{:S(2)}) collective-permute-start(bf16[2,384,768]{2,1,0:T(8,128)(2,1)} %slice.364), channel_id=1, source_target_pairs={{0,16},{16,0},{1,17},{17,1},{2,18},{18,2},{3,19},{19,3},{4,20},{20... | collective-permute-start | bytes 3538952 | tf_op jit(solution)/shard_map/ppermute | solution.py:276
  203.0 27.9 %collective-permute-start.18 = (bf16[2,2,2,96,768]{4,3,2,1,0:T(8,128)(2,1)}, bf16[2,2,2,96,768]{4,3,2,1,0:T(8,128)(2,1)}, u32[]{:S(2)}, u32[]{:S(2)}) collective-permute-start(bf16[2,2,2,96,768]{4,3,2,1,0:T(8,128)(2,1)} %slice.365), channel_id=1, source_target_pairs={{0,1},{1,0},{2,3},{3,2},{4,5},{5,4},{6,7},{7,6},{8,9},{9,8},{10,11... | collective-permute-start | bytes 3538952 | tf_op jit(solution)/shard_map/ppermute | solution.py:280
  236.1 9.1 %collective-permute-start.22 = (bf16[768,768]{1,0:T(8,128)(2,1)S(1)}, bf16[768,768]{1,0:T(8,128)(2,1)S(1)}, u32[]{:S(2)}, u32[]{:S(2)}) collective-permute-start(bf16[768,768]{1,0:T(8,128)(2,1)S(1)} %pad_maximum_fusion.11), channel_id=1, source_target_pairs={{0,8},{8,0},{1,9},{9,1},{2,10},{10,2},{3,11},{11,3},{4,12},{12,4},... | collective-permute-start | bytes 3538952 | tf_op jit(solution)/shard_map/ppermute | solution.py:272
  267.8 9.1 %collective-permute-start.25 = (bf16[128,768]{1,0:T(8,128)(2,1)S(1)}, bf16[128,768]{1,0:T(8,128)(2,1)S(1)}, u32[]{:S(2)}, u32[]{:S(2)}) collective-permute-start(bf16[128,768]{1,0:T(8,128)(2,1)S(1)} %get-tuple-element.120.refs_4_.g0), channel_id=1, source_target_pairs={{0,17},{1,16},{16,1},{17,0},{2,19},{3,18},{18,3},{19,2},{4,21},{5,... | collective-permute-start | bytes 589832 | tf_op jit(solution)/shard_map/ppermute | solution.py:288
  284.0 12.0 %collective-permute-start.26 = (bf16[16,256,768]{2,1,0:T(8,128)(2,1)}, bf16[16,256,768]{2,1,0:T(8,128)(2,1)S(1)}, u32[]{:S(2)}, u32[]{:S(2)}) collective-permute-start(bf16[16,256,768]{2,1,0:T(8,128)(2,1)} %bitcast.470), channel_id=1, source_target_pairs={{0,8},{8,0},{1,9},{9,1},{2,10},{10,2},{3,11},{11,3},{4,12},{12,4},... | collective-permute-start | bytes 18874376 | tf_op jit(solution)/shard_map/ppermute | solution.py:272
  307.0 172.8 %reduce-scatter.5.cloned.1.call-start = ((), (), s32[]{:S(2)}) async-start(), calls=%async_computation.4 | async-start | bytes 3932160 | tf_op jit(solution)/shard_map/reduce_scatter | solution.py:603
  318.9 19.1 %collective-permute-start.29 = (bf16[2,768,768]{2,1,0:T(8,128)(2,1)}, bf16[2,768,768]{2,1,0:T(8,128)(2,1)}, u32[]{:S(2)}, u32[]{:S(2)}) collective-permute-start(bf16[2,768,768]{2,1,0:T(8,128)(2,1)} %convolution_convert_fusion), channel_id=1, source_target_pairs={{0,8},{8,0},{1,9},{9,1},{2,10},{10,2},{3,11},{11,3},{4,12},{12,4},... | collective-permute-start | bytes 7077896 | tf_op jit(solution)/shard_map/ppermute | solution.py:272
  321.6 20.5 %collective-permute-start.28 = (bf16[2,768,768]{2,1,0:T(8,128)(2,1)}, bf16[2,768,768]{2,1,0:T(8,128)(2,1)}, u32[]{:S(2)}, u32[]{:S(2)}) collective-permute-start(bf16[2,768,768]{2,1,0:T(8,128)(2,1)} %convolution_convert_fusion.2), channel_id=1, source_target_pairs={{0,8},{8,0},{1,9},{9,1},{2,10},{10,2},{3,11},{11,3},{4,12},{12,4},... | collective-permute-start | bytes 7077896 | tf_op jit(solution)/shard_map/ppermute | solution.py:272
  323.9 22.1 %collective-permute-start.27 = (bf16[2,768,768]{2,1,0:T(8,128)(2,1)}, bf16[2,768,768]{2,1,0:T(8,128)(2,1)}, u32[]{:S(2)}, u32[]{:S(2)}) collective-permute-start(bf16[2,768,768]{2,1,0:T(8,128)(2,1)} %convolution_convert_fusion.1), channel_id=1, source_target_pairs={{0,8},{8,0},{1,9},{9,1},{2,10},{10,2},{3,11},{11,3},{4,12},{12,4},... | collective-permute-start | bytes 7077896 | tf_op jit(solution)/shard_map/ppermute | solution.py:272
  324.4 36.7 %collective-permute-start.30 = (bf16[32,96,256]{2,1,0:T(8,128)(2,1)}, bf16[32,96,256]{2,1,0:T(8,128)(2,1)}, u32[]{:S(2)}, u32[]{:S(2)}) collective-permute-start(bf16[32,96,256]{2,1,0:T(8,128)(2,1)} %get-tuple-element.108), channel_id=1, source_target_pairs={{0,1},{1,0},{2,3},{3,2},{4,5},{5,4},{6,7},{7,6},{8,9},{9,8},{10,11... | collective-permute-start | bytes 4718600 | tf_op jit(solution)/shard_map/ppermute | solution.py:280
  325.9 37.6 %collective-permute-start.31 = (bf16[32,96,256]{2,1,0:T(8,128)(2,1)}, bf16[32,96,256]{2,1,0:T(8,128)(2,1)}, u32[]{:S(2)}, u32[]{:S(2)}) collective-permute-start(bf16[32,96,256]{2,1,0:T(8,128)(2,1)} %get-tuple-element.109), channel_id=1, source_target_pairs={{0,16},{16,0},{1,17},{17,1},{2,18},{18,2},{3,19},{19,3},{4,20},{20... | collective-permute-start | bytes 4718600 | tf_op jit(solution)/shard_map/ppermute | solution.py:276
  338.0 57.9 %collective-permute-start.32 = (bf16[32,96,256]{2,1,0:T(8,128)(2,1)S(1)}, bf16[32,96,256]{2,1,0:T(8,128)(2,1)}, u32[]{:S(2)}, u32[]{:S(2)}) collective-permute-start(bf16[32,96,256]{2,1,0:T(8,128)(2,1)S(1)} %copy-done.153), channel_id=1, source_target_pairs={{0,17},{1,16},{16,1},{17,0},{2,19},{3,18},{18,3},{19,2},{4,21},{5,... | collective-permute-start | bytes 4718600 | tf_op jit(solution)/shard_map/ppermute | solution.py:288
  395.9 63.3 %collective-permute-start.36 = (bf16[3,2,2,96,768]{4,3,2,1,0:T(8,128)(2,1)}, bf16[3,2,2,96,768]{4,3,2,1,0:T(8,128)(2,1)}, u32[]{:S(2)}, u32[]{:S(2)}) collective-permute-start(bf16[3,2,2,96,768]{4,3,2,1,0:T(8,128)(2,1)} %pad_maximum_fusion.3), channel_id=1, source_target_pairs={{0,1},{1,0},{2,3},{3,2},{4,5},{5,4},{6,7},{7,6},{8,9},{9,8},{10,11... | collective-permute-start | bytes 5308424 | tf_op jit(solution)/shard_map/ppermute | solution.py:280
  397.4 61.8 %collective-permute-start.37 = (bf16[3,2,2,96,768]{4,3,1,2,0:T(8,128)(2,1)}, bf16[3,2,2,96,768]{4,3,1,2,0:T(8,128)(2,1)}, u32[]{:S(2)}, u32[]{:S(2)}) collective-permute-start(bf16[3,2,2,96,768]{4,3,1,2,0:T(8,128)(2,1)} %copy.204), channel_id=1, source_target_pairs={{0,16},{16,0},{1,17},{17,1},{2,18},{18,2},{3,19},{19,3},{4,20},{20... | collective-permute-start | bytes 5308424 | tf_op jit(solution)/shard_map/ppermute | solution.py:276
  399.5 48.5 %collective-permute-start.33 = (bf16[32,32,256]{2,1,0:T(8,128)(2,1)}, bf16[32,32,256]{2,1,0:T(8,128)(2,1)S(1)}, u32[]{:S(2)}, u32[]{:S(2)}) collective-permute-start(bf16[32,32,256]{2,1,0:T(8,128)(2,1)} %copy-done.11), channel_id=1, source_target_pairs={{0,1},{1,0},{2,3},{3,2},{4,5},{5,4},{6,7},{7,6},{8,9},{9,8},{10,11... | collective-permute-start | bytes 1572872 | tf_op jit(solution)/shard_map/ppermute | solution.py:280
  400.0 50.5 %collective-permute-start.34 = (bf16[32,32,256]{2,1,0:T(8,128)(2,1)}, bf16[32,32,256]{2,1,0:T(8,128)(2,1)}, u32[]{:S(2)}, u32[]{:S(2)}) collective-permute-start(bf16[32,32,256]{2,1,0:T(8,128)(2,1)} %copy-done.10), channel_id=1, source_target_pairs={{0,16},{16,0},{1,17},{17,1},{2,18},{18,2},{3,19},{19,3},{4,20},{20... | collective-permute-start | bytes 1572872 | tf_op jit(solution)/shard_map/ppermute | solution.py:276
  400.4 58.9 %collective-permute-start.35 = (bf16[32,32,256]{2,1,0:T(8,128)(2,1)S(1)}, bf16[32,32,256]{2,1,0:T(8,128)(2,1)}, u32[]{:S(2)}, u32[]{:S(2)}) collective-permute-start(bf16[32,32,256]{2,1,0:T(8,128)(2,1)S(1)} %copy-done.9), channel_id=1, source_target_pairs={{0,17},{1,16},{16,1},{17,0},{2,19},{3,18},{18,3},{19,2},{4,21},{5,... | collective-permute-start | bytes 1572872 | tf_op jit(solution)/shard_map/ppermute | solution.py:288
  463.9 22.9 %collective-permute-start.38 = (bf16[3,2,96,768]{3,2,0,1:T(8,128)(2,1)}, bf16[3,2,96,768]{3,2,0,1:T(8,128)(2,1)}, u32[]{:S(2)}, u32[]{:S(2)}) collective-permute-start(bf16[3,2,96,768]{3,2,0,1:T(8,128)(2,1)} %pad_maximum_fusion.12), channel_id=1, source_target_pairs={{0,16},{16,0},{1,17},{17,1},{2,18},{18,2},{3,19},{19,3},{4,20},{20... | collective-permute-start | bytes 2654216 | tf_op jit(solution)/shard_map/ppermute | solution.py:276
  470.4 19.2 %collective-permute-start.39 = (bf16[3,2,96,768]{3,2,0,1:T(8,128)(2,1)}, bf16[3,2,96,768]{3,2,0,1:T(8,128)(2,1)}, u32[]{:S(2)}, u32[]{:S(2)}) collective-permute-start(bf16[3,2,96,768]{3,2,0,1:T(8,128)(2,1)} %pad_maximum_fusion.13), channel_id=1, source_target_pairs={{0,1},{1,0},{2,3},{3,2},{4,5},{5,4},{6,7},{7,6},{8,9},{9,8},{10,11... | collective-permute-start | bytes 2654216 | tf_op jit(solution)/shard_map/ppermute | solution.py:280
  471.9 31.6 %collective-permute-start.40 = (bf16[512,768]{1,0:T(8,128)(2,1)}, bf16[512,768]{1,0:T(8,128)(2,1)S(1)}, u32[]{:S(2)}, u32[]{:S(2)}) collective-permute-start(bf16[512,768]{1,0:T(8,128)(2,1)} %reduce-scatter.3.cloned.1.call-done.refs_0_), channel_id=1, source_target_pairs={{0,16},{16,0},{1,17},{17,1},{2,18},{18,2},{3,19},{19,3},{4,20},{20... | collective-permute-start | bytes 2359304 | tf_op jit(solution)/shard_map/ppermute | solution.py:276
  479.8 39.5 %collective-permute-start.43 = (bf16[512,768]{1,0:T(8,128)(2,1)}, bf16[512,768]{1,0:T(8,128)(2,1)S(1)}, u32[]{:S(2)}, u32[]{:S(2)}) collective-permute-start(bf16[512,768]{1,0:T(8,128)(2,1)} %reduce-scatter.5.cloned.1.call-done.refs_0_), channel_id=1, source_target_pairs={{0,16},{16,0},{1,17},{17,1},{2,18},{18,2},{3,19},{19,3},{4,20},{20... | collective-permute-start | bytes 2359304 | tf_op jit(solution)/shard_map/ppermute | solution.py:276
  507.9 13.1 %collective-permute-start.53 = (bf16[3,48,768]{2,1,0:T(8,128)(2,1)S(1)}, bf16[3,48,768]{2,1,0:T(8,128)(2,1)S(1)}, u32[]{:S(2)}, u32[]{:S(2)}) collective-permute-start(bf16[3,48,768]{2,1,0:T(8,128)(2,1)S(1)} %get-tuple-element.257), channel_id=1, source_target_pairs={{0,6},{2,0},{4,2},{6,4},{1,7},{3,1},{5,3},{7,5},{8,14},{10,8},{12,... | collective-permute-start | bytes 663560 | tf_op jit(solution)/shard_map/ppermute | solution.py:326
  513.6 32.6 %collective-permute-start.50 = (bf16[512,768]{1,0:T(8,128)(2,1)S(1)}, bf16[512,768]{1,0:T(8,128)(2,1)S(1)}, u32[]{:S(2)}, u32[]{:S(2)}) collective-permute-start(bf16[512,768]{1,0:T(8,128)(2,1)S(1)} %copy-done.5), channel_id=1, source_target_pairs={{0,8},{8,0},{1,9},{9,1},{2,10},{10,2},{3,11},{11,3},{4,12},{12,4},... | collective-permute-start | bytes 2359304 | tf_op jit(solution)/shard_map/ppermute | solution.py:272
  513.8 10.9 %collective-permute-start.51 = (bf16[3,48,768]{2,1,0:T(8,128)(2,1)S(1)}, bf16[3,48,768]{2,1,0:T(8,128)(2,1)S(1)}, u32[]{:S(2)}, u32[]{:S(2)}) collective-permute-start(bf16[3,48,768]{2,1,0:T(8,128)(2,1)S(1)} %get-tuple-element.256), channel_id=1, source_target_pairs={{0,2},{2,4},{4,6},{6,0},{1,3},{3,5},{5,7},{7,1},{8,10},{10,12},{12... | collective-permute-start | bytes 663560 | tf_op jit(solution)/shard_map/ppermute | solution.py:325
  521.1 23.7 %collective-permute-start.54 = (bf16[3,96,768]{2,1,0:T(8,128)(2,1)S(1)}, bf16[3,96,768]{2,1,0:T(8,128)(2,1)S(1)}, u32[]{:S(2)}, u32[]{:S(2)}) collective-permute-start(bf16[3,96,768]{2,1,0:T(8,128)(2,1)S(1)} %pad_maximum_fusion.35), channel_id=1, source_target_pairs={{0,6},{2,0},{4,2},{6,4},{1,7},{3,1},{5,3},{7,5},{8,14},{10,8},{12,... | collective-permute-start | bytes 1327112 | tf_op jit(solution)/shard_map/ppermute | solution.py:330
  524.8 20.6 %collective-permute-start.52 = (bf16[3,96,768]{2,1,0:T(8,128)(2,1)S(1)}, bf16[3,96,768]{2,1,0:T(8,128)(2,1)S(1)}, u32[]{:S(2)}, u32[]{:S(2)}) collective-permute-start(bf16[3,96,768]{2,1,0:T(8,128)(2,1)S(1)} %pad_maximum_fusion.34), channel_id=1, source_target_pairs={{0,2},{2,4},{4,6},{6,0},{1,3},{3,5},{5,7},{7,1},{8,10},{10,12},{12... | collective-permute-start | bytes 1327112 | tf_op jit(solution)/shard_map/ppermute | solution.py:329
  525.3 19.5 %collective-permute-start.45 = (f32[207,128]{1,0:T(8,128)S(1)}, f32[207,128]{1,0:T(8,128)S(1)}, u32[]{:S(2)}, u32[]{:S(2)}) collective-permute-start(f32[207,128]{1,0:T(8,128)S(1)} %add.684), channel_id=1, source_target_pairs={{0,2},{2,0},{4,6},{6,4},{1,3},{3,1},{5,7},{7,5},{8,10},{10,8},{12,... | collective-permute-start | bytes 317960 | tf_op jit(solution)/shard_map/ppermute | solution.py:346
  526.5 35.2 %collective-permute-start.48 = (bf16[512,768]{1,0:T(8,128)(2,1)S(1)}, bf16[512,768]{1,0:T(8,128)(2,1)S(1)}, u32[]{:S(2)}, u32[]{:S(2)}) collective-permute-start(bf16[512,768]{1,0:T(8,128)(2,1)S(1)} %copy-done.4), channel_id=1, source_target_pairs={{0,8},{8,0},{1,9},{9,1},{2,10},{10,2},{3,11},{11,3},{4,12},{12,4},... | collective-permute-start | bytes 2359304 | tf_op jit(solution)/shard_map/ppermute | solution.py:272
  544.8 19.3 %collective-permute-start.47 = (bf16[512,768]{1,0:T(8,128)(2,1)S(1)}, bf16[512,768]{1,0:T(8,128)(2,1)S(1)}, u32[]{:S(2)}, u32[]{:S(2)}) collective-permute-start(bf16[512,768]{1,0:T(8,128)(2,1)S(1)} %collective-permute-done.43.refs_0_), channel_id=1, source_target_pairs={{0,8},{8,0},{1,9},{9,1},{2,10},{10,2},{3,11},{11,3},{4,12},{12,4},... | collective-permute-start | bytes 2359304 | tf_op jit(solution)/shard_map/ppermute | solution.py:272
  544.8 14.6 %collective-permute-start.49 = (bf16[512,768]{1,0:T(8,128)(2,1)S(1)}, bf16[512,768]{1,0:T(8,128)(2,1)S(1)}, u32[]{:S(2)}, u32[]{:S(2)}) collective-permute-start(bf16[512,768]{1,0:T(8,128)(2,1)S(1)} %collective-permute-done.40.refs_0_), channel_id=1, source_target_pairs={{0,8},{8,0},{1,9},{9,1},{2,10},{10,2},{3,11},{11,3},{4,12},{12,4},... | collective-permute-start | bytes 2359304 | tf_op jit(solution)/shard_map/ppermute | solution.py:272
  546.3 11.9 %collective-permute-start.56 = (bf16[3,96,768]{2,1,0:T(8,128)(2,1)S(1)}, bf16[3,96,768]{2,1,0:T(8,128)(2,1)S(1)}, u32[]{:S(2)}, u32[]{:S(2)}) collective-permute-start(bf16[3,96,768]{2,1,0:T(8,128)(2,1)S(1)} %fusion.44), channel_id=1, source_target_pairs={{0,16},{16,0},{1,17},{17,1},{2,18},{18,2},{3,19},{19,3},{4,20},{20... | collective-permute-start | bytes 1327112 | tf_op jit(solution)/shard_map/ppermute | solution.py:276
  554.8 11.6 %collective-permute-start.55 = (bf16[3,96,768]{2,1,0:T(8,128)(2,1)S(1)}, bf16[3,96,768]{2,1,0:T(8,128)(2,1)S(1)}, u32[]{:S(2)}, u32[]{:S(2)}) collective-permute-start(bf16[3,96,768]{2,1,0:T(8,128)(2,1)S(1)} %fusion.44), channel_id=1, source_target_pairs={{0,8},{8,0},{1,9},{9,1},{2,10},{10,2},{3,11},{11,3},{4,12},{12,4},... | collective-permute-start | bytes 1327112 | tf_op jit(solution)/shard_map/ppermute | solution.py:272
  (173 other events, 1784.9 us)
Sparse Core Ops, SparseCore 0:
  10.2 146.3 all-gather.1
  307.1 61.7 reduce-scatter.2
  371.2 60.2 reduce-scatter.4

commit v3 on v2

--- a/solution.py
+++ b/solution.py
@@ -2,6 +2,7 @@
 
 import jax
 import jax.numpy as jnp
+import numpy as np
 from jax import lax
 from jax.experimental import pallas as pl
 from jax.experimental.pallas import tpu as pltpu
@@ -16,6 +17,7 @@
 epsilon = 1e-06
 
 AXES = ("x", "c", "z", "y")
+PLANNED = (4, 8)
 VMEM_LIMIT = 48 * 1024 * 1024
 MIX_ROWS = 16
 GEN_STEP = 4
@@ -48,7 +50,7 @@
 
 
 def row_total(values):
-    return jnp.sum(values.astype(f32), axis=0)
+    return jnp.sum(values.astype(f32), axis=0, keepdims=True)
 
 
 def mix_kernel(hyper_ref, pix_ref, *outs):
@@ -81,119 +83,90 @@
     )(hyper_t, pixel_rows)
 
 
-def halves(steps):
-    first = lambda i: (jnp.minimum(i, steps - 1), 0, 0)
-    second = lambda i: (jnp.maximum(i - steps, 0), 0, 0)
-    return first, second
-
-
-def project_kernel(*refs):
-    parts, w, sums, out = refs[:4], refs[4], refs[5:-1], refs[-1]
-
+def project_kernel(a0, a1, a2, a3, w, out):
     @pl.when(pl.program_id(0) == 0)
     def _():
-        out[...] = sums[0][...] if sums else jnp.zeros_like(out)
+        out[...] = jnp.zeros_like(out)
 
     for k in range(w.shape[0]):
-        left = jnp.concatenate([a[k] for a in parts], axis=0)
+        left = jnp.concatenate([a[k] for a in (a0, a1, a2, a3)], axis=0)
         out[...] += dense_dot(left, w[k])
 
 
-def project(parts, gen, which, sums=()):
+def project(parts, gen):
     share, rows, pixel_count = parts[0].shape
     width = gen.shape[2]
-    steps = share // 2 // GEN_STEP
-    out = pl.BlockSpec((4 * rows, width), lambda i: (0, 0))
     return pl.pallas_call(
         project_kernel,
-        grid=(steps,),
-        in_specs=[pl.BlockSpec((GEN_STEP, rows, pixel_count), lambda i: (i + which * steps, 0, 0))] * 4
-        + [pl.BlockSpec((GEN_STEP, pixel_count, width), lambda i: (i, 0, 0))]
-        + [out] * len(sums),
-        out_specs=out,
+        grid=(share // GEN_STEP,),
+        in_specs=[pl.BlockSpec((GEN_STEP, rows, pixel_count), lambda i: (i, 0, 0))] * 4
+        + [pl.BlockSpec((GEN_STEP, pixel_count, width), lambda i: (i, 0, 0))],
+        out_specs=pl.BlockSpec((4 * rows, width), lambda i: (0, 0)),
         out_shape=jax.ShapeDtypeStruct((4 * rows, width), f32),
         compiler_params=pltpu.CompilerParams(vmem_limit_bytes=VMEM_LIMIT),
         cost_estimate=COST,
         name="project",
-    )(*parts, gen, *sums)
+    )(*parts, gen)
 
 
 def early_rows(rows):
     return rows // 4 * 3
 
 
-def back_kernel(g0, g1, g2, g3, w0, w1, *outs):
-    i = pl.program_id(0)
-    steps = pl.num_programs(0) // 2
+def back_kernel(g0, g1, g2, g3, w, *outs):
     rows = g0.shape[0]
-
-    def work(w):
-        grads = jnp.concatenate([g[...] for g in (g0, g1, g2, g3)], axis=0)
-        for k in range(w.shape[0]):
-            res = right_dot(grads, w[k]).astype(bf16)
-            for j, out in enumerate(outs):
-                out[k] = res[j * rows : (j + 1) * rows]
-
-    @pl.when(i < steps)
-    def _():
-        work(w0)
-
-    @pl.when(i >= steps)
-    def _():
-        work(w1)
-
-
-def back_patches(grads, near, far, start, rows):
-    share, pixel_count, width = 2 * near.shape[0], near.shape[1], near.shape[2]
-    steps = share // 2 // GEN_STEP
-    first, second = halves(steps)
-    out = jax.ShapeDtypeStruct((share, rows, pixel_count), bf16)
+    grads = jnp.concatenate([g[...] for g in (g0, g1, g2, g3)], axis=0)
+    for k in range(w.shape[0]):
+        res = right_dot(grads, w[k]).astype(bf16)
+        for j, out in enumerate(outs):
+            out[k] = res[j * rows : (j + 1) * rows]
+
+
+def back_patches(grads, gen, start, rows):
+    share, pixel_count, width = gen.shape
     return pl.pallas_call(
         back_kernel,
-        grid=(2 * steps,),
+        grid=(share // GEN_STEP,),
         in_specs=[pl.BlockSpec((rows, width), lambda i: (start // rows, 0))] * 4
-        + [
-            pl.BlockSpec((GEN_STEP, pixel_count, width), first),
-            pl.BlockSpec((GEN_STEP, pixel_count, width), second),
-        ],
+        + [pl.BlockSpec((GEN_STEP, pixel_count, width), lambda i: (i, 0, 0))],
         out_specs=[pl.BlockSpec((GEN_STEP, rows, pixel_count), lambda i: (i, 0, 0))] * 4,
-        out_shape=[out] * 4,
+        out_shape=[jax.ShapeDtypeStruct((share, rows, pixel_count), bf16)] * 4,
         compiler_params=pltpu.CompilerParams(vmem_limit_bytes=VMEM_LIMIT),
         cost_estimate=COST,
         name="back_patches",
-    )(*grads, near, far)
-
-
-def gen_grad_kernel(*refs, others):
-    parts, grad_refs = refs[:4], refs[4:8]
+    )(*grads, gen)
+
+
+def gen_grad_kernel(core_ref, *refs):
+    parts, grad_refs, outs = refs[:8], refs[8:13], refs[13:]
     grads = jnp.concatenate([g[...] for g in grad_refs], axis=0)
-    outs = refs[8 + others :]
     cut = outs[0].shape[1]
     for k in range(cut * len(outs)):
         left = jnp.concatenate([a[k] for a in parts], axis=0)
-        res = left_dot(left, grads)
-        for other in refs[8 : 8 + others]:
-            res = res + other[k].astype(f32)
-        outs[k // cut][0, k % cut] = res.astype(bf16)
-
-
-def gen_grad(parts, grads, which, others=(), chunks=1):
-    share, rows, pixel_count = parts[0].shape
-    width = grads[0].shape[1]
+        outs[k // cut][0, k % cut] = left_dot(left, grads).astype(bf16)
+
+
+def gen_grad(parts, others, grads, other_grads, chunks, at_c):
+    share, rows, pixel_count = others[0].shape
+    width = other_grads.shape[1]
     steps = share // 2 // GEN_STEP
     cut = GEN_STEP // chunks
+    block = (GEN_STEP, rows, pixel_count)
     return pl.pallas_call(
-        functools.partial(gen_grad_kernel, others=len(others)),
-        grid=(steps,),
-        in_specs=[pl.BlockSpec((GEN_STEP, rows, pixel_count), lambda i: (i + which * steps, 0, 0))] * 4
-        + [pl.BlockSpec((rows, width), lambda i: (0, 0))] * 4
-        + [pl.BlockSpec((GEN_STEP, pixel_count, width), lambda i: (i, 0, 0))] * len(others),
-        out_specs=[pl.BlockSpec((1, cut, pixel_count, width), lambda i: (i, 0, 0, 0))] * chunks,
+        gen_grad_kernel,
+        grid_spec=pltpu.PrefetchScalarGridSpec(
+            num_scalar_prefetch=1,
+            grid=(steps,),
+            in_specs=[pl.BlockSpec(block, lambda i, core: (core[0] * steps + i, 0, 0))] * 8
+            + [pl.BlockSpec((rows, width), lambda i, core: (0, 0))] * 4
+            + [pl.BlockSpec((4 * rows, width), lambda i, core: (0, 0))],
+            out_specs=[pl.BlockSpec((1, cut, pixel_count, width), lambda i, core: (i, 0, 0, 0))] * chunks,
+        ),
         out_shape=[jax.ShapeDtypeStruct((steps, cut, pixel_count, width), bf16)] * chunks,
         compiler_params=pltpu.CompilerParams(vmem_limit_bytes=VMEM_LIMIT),
         cost_estimate=COST,
         name="gen_grad",
-    )(*parts, *grads, *others)
+    )(at_c.reshape(1), *parts, *others, *grads, other_grads)
 
 
 def pixel_kernel(hyper_ref, pix_ref, g0, g1, g2, g3, *refs):
@@ -264,6 +237,192 @@
     )(jnp.stack(quarters), *pieces, *before)
 
 
+def take_kernel(quarter_ref, qkv, out_w, fc1, fc2, pieces):
+    unit, width = fc2.shape
+    for q in range(4):
+
+        @pl.when(quarter_ref[0] == q)
+        def _(q=q):
+            pieces[0] = out_w[...] if q == 3 else qkv[:, q * width : (q + 1) * width]
+            low = fc1[...].astype(f32)
+            starts = range(q * unit, fc1.shape[1], 4 * unit)
+            pieces[1] = jnp.concatenate([low[:, i : i + unit] for i in starts], axis=1).astype(bf16)
+
+    pieces[2] = fc2[...]
+
+
+def take_pieces(qkv, out_w, fc1, fc2, quarter):
+    rows, width = out_w.shape
+    unit = fc2.shape[0] // 4
+    whole = lambda i, at: (0, 0)
+    return pl.pallas_call(
+        take_kernel,
+        grid_spec=pltpu.PrefetchScalarGridSpec(
+            num_scalar_prefetch=1,
+            grid=(1,),
+            in_specs=[pl.BlockSpec(array.shape, whole) for array in (qkv, out_w, fc1)]
+            + [pl.BlockSpec((unit, width), lambda i, at: (at[0], 0))],
+            out_specs=pl.BlockSpec((3, rows, width), lambda i, at: (0, 0, 0)),
+        ),
+        out_shape=jax.ShapeDtypeStruct((3, rows, width), bf16),
+        compiler_params=pltpu.CompilerParams(vmem_limit_bytes=VMEM_LIMIT),
+        cost_estimate=COST,
+        name="take_pieces",
+    )(quarter.reshape(1), qkv, out_w, fc1, fc2)
+
+
+def give_kernel(order_ref, pieces, qkv, out_w, fc1, fc2):
+    unit, width = fc2.shape
+    for q in range(4):
+
+        @pl.when(pl.program_id(0) == q)
+        def _(q=q):
+            piece = pieces[0, 0].astype(f32)
+            if q == 3:
+                out_w[...] = piece
+            else:
+                qkv[:, q * width : (q + 1) * width] = piece
+            piece = pieces[0, 1].astype(f32)
+            for r, i in enumerate(range(q * unit, fc1.shape[1], 4 * unit)):
+                fc1[:, i : i + unit] = piece[:, r * unit : (r + 1) * unit]
+
+    fc2[...] = pieces[0, 2].astype(f32)
+
+
+def give_pieces(pieces, quarter, hidden_width):
+    _, _, rows, width = pieces.shape
+    unit = rows * hidden_width // (4 * width)
+    whole = lambda i, order: (0, 0)
+    shapes = [(rows, 3 * width), (rows, width), (rows, hidden_width)]
+    return pl.pallas_call(
+        give_kernel,
+        grid_spec=pltpu.PrefetchScalarGridSpec(
+            num_scalar_prefetch=1,
+            grid=(4,),
+            in_specs=[pl.BlockSpec((1, 3, rows, width), lambda i, order: (order[i], 0, 0, 0))],
+            out_specs=[pl.BlockSpec(shape, whole) for shape in shapes]
+            + [pl.BlockSpec((unit, width), lambda i, order: (i, 0))],
+        ),
+        out_shape=[jax.ShapeDtypeStruct(shape, f32) for shape in shapes + [(4 * unit, width)]],
+        compiler_params=pltpu.CompilerParams(vmem_limit_bytes=VMEM_LIMIT),
+        cost_estimate=COST,
+        name="give_pieces",
+    )(quarter ^ jnp.arange(4), pieces)
+
+
+def sum_kernel(left_at, late_at, y_at, left, right, late, left_came, right_came, late_came, *refs):
+    to_y, kept_y, kept_x, to_x, scratch = refs
+    dx, kind = pl.program_id(0), pl.program_id(1)
+    half, shard, _ = to_y.shape[2:]
+    lefts = jnp.concatenate([left[0], left_came[0]], axis=0)
+    rights = jnp.concatenate([right[0], right_came[0]], axis=0)
+    lates = jnp.concatenate([late[0], late_came[0]], axis=0)
+    scratch[...] = left_dot(lefts, jnp.where(kind == 0, lates, rights))
+
+    def rows_of(z, y):
+        start = pl.multiple_of((2 * z + y) * shard, 8)
+        return scratch[pl.ds(start, shard), :].astype(bf16)
+
+    for z in range(half):
+        to_y[0, 0, z] = rows_of(z, 1 - y_at[0])
+        kept_y[0, 0, z] = rows_of(z, y_at[0])
+
+    def write(out):
+        for z in range(half):
+            for y in range(2):
+                out[0, z, y] = rows_of(half + z, y)
+
+    @pl.when(dx == 0)
+    def _():
+        write(kept_x)
+
+    @pl.when(dx == 1)
+    def _():
+        write(to_x)
+
+
+def sum_blocks(early, late, early_came, late_came, quarter, at_y, z_size):
+    _, rows, width = early.shape
+    half, kinds = z_size // 2, 3
+    shard = width // (2 * z_size)
+    low = (2, kinds, half, shard, width)
+    high = (kinds, half, 2, shard, width)
+    low_spec = pl.BlockSpec((1, 1) + low[2:], lambda d, k, *_: (d, k, 0, 0, 0))
+    block = (1, rows, width)
+    quarters = jnp.stack([quarter, quarter ^ 2])
+    left = pl.BlockSpec(
+        block, lambda d, k, left, *_: (jnp.where(k == 0, left[d], jnp.where(k == 1, 2, 4 + d)), 0, 0)
+    )
+    right = pl.BlockSpec(block, lambda d, k, *_: (jnp.where(k == 2, 3, 6 + d), 0, 0))
+    last = pl.BlockSpec(block, lambda d, k, left, late, y: (late[d], 0, 0))
+    return pl.pallas_call(
+        sum_kernel,
+        grid_spec=pltpu.PrefetchScalarGridSpec(
+            num_scalar_prefetch=3,
+            grid=(2, kinds),
+            in_specs=[left, right, last] * 2,
+            out_specs=[
+                low_spec,
+                low_spec,
+                pl.BlockSpec((1,) + high[1:], lambda d, k, *_: (jnp.where(d == 0, k, kinds - 1), 0, 0, 0, 0)),
+                pl.BlockSpec((1,) + high[1:], lambda d, k, *_: (jnp.where(d == 1, k, 0), 0, 0, 0, 0)),
+            ],
+            scratch_shapes=[pltpu.VMEM((width, width), f32)],
+        ),
+        out_shape=[jax.ShapeDtypeStruct(shape, bf16) for shape in (low, low, high, high)],
+        compiler_params=pltpu.CompilerParams(vmem_limit_bytes=VMEM_LIMIT),
+        cost_estimate=COST,
+        name="sum_blocks",
+    )(
+        jnp.where(quarters == 3, 1, 0),
+        quarters,
+        at_y.reshape(1),
+        early,
+        early,
+        late,
+        early_came,
+        early_came,
+        late_came,
+    )
+
+
+def pack_kernel(quarter_ref, weight, fc1_bias, *refs, unit):
+    vectors, out = refs[:-1], refs[-1]
+    lanes = out.shape[1]
+    out[0 : weight.shape[0], :] = weight[...]
+    row = weight.shape[0]
+    fc1_rows = [fc1_bias[pl.ds(quarter_ref[0] ^ q, 1), :] for q in range(4)]
+    pieces = [
+        fc1_rows[q][:, i : i + unit] for i in range(0, fc1_bias.shape[1], unit) for q in range(4)
+    ]
+    for vector in [v[...] for v in vectors] + [jnp.concatenate(pieces, axis=1)]:
+        for i in range(0, vector.shape[1], lanes):
+            out[row : row + 1, :] = vector[:, i : i + lanes]
+            row += 1
+    out[row:, :] = jnp.zeros((out.shape[0] - row, lanes), f32)
+
+
+def pack_small(weight, vectors, fc1_bias, unit, quarter):
+    lanes = weight.shape[1]
+    count = weight.shape[0] + (sum(v.shape[1] for v in vectors) + fc1_bias.size) // lanes
+    shape = (-(-count // 8) * 8, lanes)
+    whole = lambda i, at: (0, 0)
+    arrays = (weight, fc1_bias, *vectors)
+    return pl.pallas_call(
+        functools.partial(pack_kernel, unit=unit),
+        grid_spec=pltpu.PrefetchScalarGridSpec(
+            num_scalar_prefetch=1,
+            grid=(1,),
+            in_specs=[pl.BlockSpec(array.shape, whole) for array in arrays],
+            out_specs=pl.BlockSpec(shape, whole),
+        ),
+        out_shape=jax.ShapeDtypeStruct(shape, f32),
+        compiler_params=pltpu.CompilerParams(vmem_limit_bytes=VMEM_LIMIT),
+        cost_estimate=COST,
+        name="pack_small",
+    )(quarter.reshape(1), *arrays)
+
+
 PAIR = [(0, 1), (1, 0)]
 CORNER = [(i, i ^ 3) for i in range(4)]
 
@@ -300,12 +459,18 @@
 UP, DOWN = ([(i, (i + step) % 4) for i in range(4)] for step in (1, 3))
 
 
-def gather_z(own):
-    size, at = lax.axis_size("z"), lax.axis_index("z")
-    if size != 4:
-        return lax.all_gather(own, "z", axis=0, tiled=False)
+def gather_z_start(own):
+    if lax.axis_size("z") != 4:
+        return (lax.all_gather(own, "z", axis=0, tiled=False),)
+    return lax.ppermute(own, "z", UP), lax.ppermute(own, "z", DOWN)
+
+
+def gather_z_end(own, came):
+    at = lax.axis_index("z")
+    if lax.axis_size("z") != 4:
+        return came[0]
     half = own.shape[-2] // 2
-    below, above = lax.ppermute(own, "z", UP), lax.ppermute(own, "z", DOWN)
+    below, above = came
     across = [
         lax.ppermute(below[..., :half, :], "z", UP),
         lax.ppermute(above[..., half:, :], "z", DOWN),
@@ -330,17 +495,16 @@
     return (total + lax.ppermute(below, "z", DOWN).astype(f32)).astype(bf16)
 
 
-def gather_quarters(own, quarter):
+def gather_quarters(own):
     across = swap_x(own)
-    away = jnp.stack([own, swap_core(own), across, swap_core(across)])
-    return jnp.stack([pick(away, quarter ^ j) for j in range(4)])
+    return jnp.stack([own, swap_core(own), across, swap_core(across)])
 
 
 def total_of(value, earlier):
     value = value + swap_core(value)
     value = value + swap_x(value)
+    value = value + swap_y(value)
     value = after(value, earlier)
-    value = value + swap_y(value)
     size, step = lax.axis_size("z"), 1
     while step < size:
         value = value + lax.ppermute(value, "z", [(i, i ^ step) for i in range(size)])
@@ -348,21 +512,8 @@
     return value
 
 
-def reduce_core(blocks):
-    return [split_y(add_low(blocks[2 * dx], swap_core(blocks[2 * dx + 1]))) for dx in range(2)]
-
-
 def add_low(left, right):
     return (left.astype(f32) + right.astype(f32)).astype(bf16)
-
-
-def split_y(block):
-    size = lax.axis_size("z")
-    return block.reshape(size, 2, block.shape[0] // size // 2, block.shape[1])
-
-
-def of_y(block, y):
-    return lax.dynamic_index_in_dim(block, y, 1, keepdims=False)
 
 
 def join_y(own, other):
@@ -393,21 +544,10 @@
     ]
 
 
-def sum_start(blocks):
-    at_y, half = lax.axis_index("y"), blocks[0][0].shape[0] // 2
-    to_y = jnp.stack([jnp.stack([of_y(b[:half], 1 - at_y) for b in pair]) for pair in blocks])
-    return to_y, jnp.stack([pair[1][half:] for pair in blocks])
-
-
-def sum_more(blocks, from_y, from_x):
-    at_y, half = lax.axis_index("y"), blocks[0][0].shape[0] // 2
-    low = [
-        jnp.stack([add_low(of_y(pair[dx][:half], at_y), from_y[kind, dx]) for kind, pair in enumerate(blocks)])
-        for dx in range(2)
-    ]
+def sum_more(kept_y, kept_x, from_y, from_x, at_y):
+    low = [add_low(kept_y[dx], from_y[dx]) for dx in range(2)]
     high = [
-        jnp.stack([add_low(of_y(pair[0][half:], y), of_y(from_x[kind], y)) for kind, pair in enumerate(blocks)])
-        for y in (at_y, 1 - at_y)
+        add_low(*(lax.dynamic_index_in_dim(v, y, 2, False) for v in (kept_x, from_x))) for y in (at_y, 1 - at_y)
     ]
     return low[0], high[0], low[1], high[1]
 
@@ -457,7 +597,7 @@
 
     gen_rows = gen_weight.shape[0] // 4
     own_rows = lax.dynamic_slice_in_dim(gen_weight, quarter * gen_rows, gen_rows, 0)
-    near = lax.all_gather(own_rows, "z", axis=0, tiled=True)
+    gen = lax.all_gather(own_rows, ("c", "z"), axis=0, tiled=True).reshape(-1, pixel_count, model_width)
 
     unit_order = fc1_bias.reshape(row_size, 4, unit).transpose(1, 0, 2).reshape(4, row_size * unit)
     bias_fc1 = [pick(unit_order, quarter ^ d) for d in range(4)]
@@ -477,7 +617,7 @@
     place = place // (per_row // 4)
     entry_z = place % z_size
     place = place // z_size
-    entry_c, entry_y, entry_x = (place % 2) ^ at_c, (place // 2 % 2) ^ at_y, (place // 4) ^ at_x
+    entry_c, entry_y, entry_x = place % 2, (place // 2 % 2) ^ at_y, (place // 4) ^ at_x
     entry = per_row * (2 * entry_z + entry_y) + per_row // 4 * (2 * entry_x + entry_c) + kk
     order = (jnp.arange(wave_width)[:, None] == entry[None, :]).astype(bf16)
     hyper_low = dense_dot(hyper.astype(bf16), order).astype(bf16)
@@ -486,36 +626,27 @@
     mixed_pixels = mix_pixels(hyper_low.T, pixel_rows)
     patches = swap_plane(mixed_pixels)
 
-    weights = (qkv_weight, out_weight, fc1_weight, fc2_weight)
-    qkv_weight, out_weight, fc1_weight, fc2_weight = after(weights, mixed_pixels)
-    attn_piece = pick(
-        jnp.stack(
-            [qkv_weight[:, j * model_width : (j + 1) * model_width] for j in range(3)] + [out_weight]
-        ),
-        quarter,
-    )
-    fc1_piece = lax.dynamic_index_in_dim(fc1_weight.reshape(shard, row_size, 4, unit), quarter, 2, False)
-    fc1_piece = fc1_piece.reshape(shard, row_size * unit)
-    fc2_piece = pick(fc2_weight.reshape(4, unit, model_width), quarter)
-    column = gather_z(jnp.stack([attn_piece, fc1_piece, fc2_piece]))
-    low, high = gather_more(column, gather_start(column))
-    low, high, patches = after((low, high, patches))
-    near = after(near, low, high)
-    far = swap_core(near)
-    near = near.reshape(-1, pixel_count, model_width)
-    far = far.reshape(-1, pixel_count, model_width)
-    attn_came = swap_x(low[:1]), swap_y(high[:, :, :1])
-    partial = project(patches, far, 1, (project(patches, near, 0),))
+    weights = after((qkv_weight, out_weight, fc1_weight, fc2_weight), mixed_pixels)
+    own_pieces = take_pieces(*weights, quarter)
+    column = gather_z_end(own_pieces, gather_z_start(own_pieces))
+    column, patches = after((column, patches))
+    column_came = gather_start(column)
+    low, high = gather_more(column, column_came)
+    attn, fc = (low[:1], high[:, :, :1]), (low[1:], high[:, :, 1:])
+    attn_came = swap_x(attn[0]), swap_y(attn[1])
+    attn_came, fc = after((attn_came, fc))
+    fc_came = swap_x(fc[0]), swap_y(fc[1])
+
+    def both_cores(blocks):
+        return [block for owned in blocks for block in (owned, swap_core(owned))]
+
+    attn = jnp.stack(both_cores(gather_end(*attn, *attn_came)[0]))
+    gen = after(gen, attn_came)
+    partial = project(patches, gen)
     partial = [partial[j * row_count : (j + 1) * row_count] for j in range(4)]
     partial = [partial[0]] + swap_plane([piece.astype(bf16) for piece in partial])[1:]
     projected = (partial[0] + partial[1]) + (partial[2] + partial[3])
-    attn_came, fc_low, fc_high = after((attn_came, low[1:], high[:, :, 1:]), projected)
-    fc_came = swap_x(fc_low), swap_y(fc_high)
-
-    def both_cores(blocks):
-        return [block for owned in blocks for block in (owned, swap_core(owned))]
-
-    attn = jnp.stack(both_cores(gather_end(low[:1], high[:, :, :1], *attn_came)[0]))
+    fc_came = after(fc_came, projected)
     w_query, w_key, w_value, w_out = (pick(attn, j ^ quarter) for j in range(4))
     position = sincos(jnp.arange(seq_len).astype(f32), model_width)
     embedded = (projected + patch_bias).reshape(tile_count, seq_len, model_width) + position
@@ -537,7 +668,8 @@
     )
     middle = embedded + dense_dot(attended, w_out) + out_bias
     fc_came = after(fc_came, middle)
-    w_fc1, w_fc2 = (both_cores(blocks) for blocks in gather_end(fc_low, fc_high, *fc_came))
+    w_fc1, w_fc2 = (both_cores(blocks) for blocks in gather_end(*fc, *fc_came))
+    other_patches = [swap_core(part) for part in after(patches, middle)]
     normed_two = layer_norm(middle, norm2_gain, norm2_bias).astype(bf16)
     fc_pre = [dense_dot(normed_two, w) + bias for w, bias in zip(w_fc1, bias_fc1)]
     hidden, gelu_back = zip(*(jax.vjp(jax.nn.gelu, values) for values in fc_pre))
@@ -549,9 +681,10 @@
     grad_pre = [
         back(right_dot(grad_out, w))[0].astype(bf16) for back, w in zip(gelu_back, w_fc2)
     ]
-    fc1_bias_part = jnp.stack([row_total(values) for values in grad_pre])
-    fc1_bias_part = jnp.stack([pick(fc1_bias_part, quarter ^ j) for j in range(4)])
-    fc1_bias_part = fc1_bias_part.reshape(4, row_size, unit).transpose(1, 0, 2).reshape(-1)
+    fc1_bias_part = jnp.concatenate([row_total(values) for values in grad_pre])
+    common = [normed, attended, normed_two, grad_out]
+    early_values = jnp.stack(common + [hidden[0], hidden[2], grad_pre[0], grad_pre[2]])
+    early_came = swap_core(jnp.stack(common + [hidden[1], hidden[3], grad_pre[1], grad_pre[3]]))
     grad_normed_two = sum(right_dot(values, w) for values, w in zip(grad_pre, w_fc1))
     norm_two_back = jax.vjp(layer_norm, middle, norm2_gain, norm2_bias)[1]
     grad_middle, norm2_gain_part, norm2_bias_part = norm_two_back(grad_normed_two)
@@ -585,103 +718,77 @@
     grad_normed = right_dot(grad_queries, w_query)
     grad_normed += right_dot(grad_keys, w_key)
     grad_normed += right_dot(grad_values, w_value)
+    grad_normed, early_came, other_patches = after((grad_normed, early_came, other_patches))
     norm_one_back = jax.vjp(layer_norm, embedded, norm1_gain, norm1_bias)[1]
     grad_from_norm, norm1_gain_part, norm1_bias_part = norm_one_back(grad_normed)
     grad_embedded = (grad_middle + grad_from_norm).astype(bf16)
     patch_bias_part = row_total(grad_embedded)
 
     grads = swap_plane([grad_embedded] * 4)
-    (far_grad,) = gen_grad(patches, grads, 1)
-    far_grad = swap_core(far_grad.reshape(-1, pixel_count, model_width))
     early = early_rows(row_count)
-    back_early = back_patches(grads, near, far, 0, early)
-    far_grad = after(far_grad, back_early)
+    back_early = back_patches(grads, gen, 0, early)
+    grads, back_early = after((grads, back_early))
     back_early = swap_plane(back_early)
+    other_grads = swap_core(jnp.concatenate(grads))
     chunks = 2 if wave_width // row_size // 4 == GEN_STEP else 1
-    gen_sent = gen_grad(patches, grads, 0, (far_grad,), chunks)
+    gen_sent = gen_grad(patches, other_patches, grads, other_grads, chunks, at_c)
     gen_parts = [
         lax.psum_scatter(chunk.reshape(-1, model_width), "z", scatter_dimension=0, tiled=True)
         for chunk in gen_sent
     ]
 
-    left = jnp.stack([normed, normed, normed, attended])
-    right = jnp.stack([grad_queries, grad_keys, grad_values, grad_branch])
-    near_first = [0, 2, 1, 3]
-    left = jnp.stack([pick(left, quarter ^ d) for d in near_first])
-    right = jnp.stack([pick(right, quarter ^ d) for d in near_first])
-    hidden, grad_pre = (jnp.stack([values[d] for d in near_first]) for values in (hidden, grad_pre))
-    sides = [(left, right), (jnp.stack([normed_two] * 2), grad_pre), (hidden, jnp.stack([grad_out] * 2))]
-    sides = after(sides, gen_sent)
-
-    def block_grad(side, part):
-        return jnp.einsum(
-            "dri,drj->dij", *(v if v.shape[0] == 2 else v[part : part + 2] for v in side), preferred_element_type=f32
-        ).astype(bf16)
-
-    block_grads = [swap_core(block_grad(side, 2)) for side in sides]
-    block_grads = [add_low(block_grad(side, 0), came) for side, came in zip(sides, block_grads)]
-    block_grads = [[split_y(pair[dx]) for dx in range(2)] for pair in block_grads]
-    to_y, to_x = sum_start(block_grads)
-    back_late = back_patches(after(grads, gen_sent), near, far, early, row_count - early)
+    late_values = jnp.stack([grad_queries, grad_keys, grad_values, grad_branch])
+    late_came = swap_core(late_values)
+    to_y, kept_y, kept_x, to_x = sum_blocks(
+        early_values, late_values, early_came, late_came, quarter, at_y, z_size
+    )
+    back_late = back_patches(after(grads, gen_sent), gen, early, row_count - early)
     to_y, to_x, back_early, back_late = after((to_y, to_x, back_early, back_late))
     back_late = swap_plane(back_late)
     from_y, from_x = swap_y(to_y), swap_x(to_x)
     pixel_grad, hyper_early = pixel_back(hyper_low, pixel_rows, back_early, 0)
     back_late, from_y, from_x, hyper_early = after((back_late, from_y, from_x, hyper_early))
-    low, high, low_sent, high_sent = sum_more(block_grads, from_y, from_x)
+    low, high, low_sent, high_sent = sum_more(kept_y, kept_x, from_y, from_x, at_y)
     low_x, high_y = swap_x(low_sent), swap_y(high_sent)
-    across = [swap_x(gen_parts[0])]
     pixel_grad, hyper_late = pixel_back(hyper_low, pixel_rows, back_late, early, (pixel_grad,))
-    low_x, high_y, hyper_late = after((low_x, high_y, hyper_late), across)
-    across += [swap_x(piece) for piece in gen_parts[1:]]
-    share_sum = scatter_z(sum_end(low, high, low_x, high_y))
-    totals = gather_quarters(share_sum, quarter).astype(f32)
-    qkv_total = jnp.concatenate([totals[0, 0], totals[1, 0], totals[2, 0]], axis=1)
-    out_total = totals[3, 0]
-    fc1_total = totals[:, 1].reshape(4, shard, row_size, unit).transpose(1, 2, 0, 3)
-    fc1_total = fc1_total.reshape(shard, hidden_width)
-    fc2_total = totals[:, 2].reshape(4 * unit, model_width)
-
-    grad_hyper = hyper_early + hyper_late
-    grad_hyper = lax.dot_general(
-        grad_hyper, order.astype(f32), (((1,), (1,)), ((), ())), precision=highest
-    )
-    wave_weight_part, wave_bias_part = hyper_back(grad_hyper)
-    small = (
-        patch_bias_part,
-        norm1_gain_part,
-        norm1_bias_part,
-        query_bias_part,
-        value_bias_part,
-        out_bias_part,
-        norm2_gain_part,
-        norm2_bias_part,
-        fc2_bias_part,
-        fc1_bias_part,
-    )
-    small = jnp.concatenate(small + (wave_bias_part,)).reshape(-1, wave_width)
-    small = total_of(jnp.concatenate([wave_weight_part, small]), across)
+    low_x, high_y, hyper_late, gen_parts = after((low_x, high_y, hyper_late, gen_parts))
+    across = [swap_x(piece) for piece in gen_parts]
     gen_total = ()
     for chunk, piece in enumerate(gen_parts):
         pair = piece, swap_core(piece)
         gen_total = (put_parts(pair, (quarter, quarter ^ 1), chunk, chunks, gen_total),)
-        pair = across[chunk], swap_core(across[chunk])
+    share_sum = scatter_z(sum_end(low, high, low_x, high_y))
+    qkv_total, out_total, fc1_total, fc2_total = give_pieces(gather_quarters(share_sum), quarter, hidden_width)
+
+    grad_hyper = hyper_early + hyper_late
+    grad_hyper = lax.dot_general(
+        grad_hyper, order.astype(f32), (((1,), (1,)), ((), ())), precision=highest
+    )
+    wave_weight_part, wave_bias_part = hyper_back(grad_hyper)
+    norm_parts = [norm1_gain_part, norm1_bias_part, norm2_gain_part, norm2_bias_part, wave_bias_part]
+    norm_parts = [part.reshape(1, -1) for part in norm_parts]
+    small = [*norm_parts, patch_bias_part, query_bias_part, value_bias_part, out_bias_part, fc2_bias_part]
+    cuts = np.cumsum([part.shape[1] for part in small] + [hidden_width])
+    small = pack_small(wave_weight_part, small, fc1_bias_part, unit, quarter)
+    small = total_of(small, (share_sum, gen_total))
+    for chunk, piece in enumerate(across):
+        pair = piece, swap_core(piece)
         gen_total = (put_parts(pair, (quarter ^ 2, quarter ^ 3), chunk, chunks, gen_total),)
     gen_total = gen_total[0]
     wave_weight_total, small = small[:wave_width], small[wave_width:].reshape(-1)
-    cuts = [model_width * j for j in range(1, 10)] + [9 * model_width + hidden_width]
     (
-        patch_bias_total,
         norm1_gain_total,
         norm1_bias_total,
+        norm2_gain_total,
+        norm2_bias_total,
+        wave_bias_total,
+        patch_bias_total,
         query_bias_total,
         value_bias_total,
         out_bias_total,
-        norm2_gain_total,
-        norm2_bias_total,
         fc2_bias_total,
         fc1_bias_total,
-        wave_bias_total,
+        _,
     ) = jnp.split(small, cuts)
     block_result = block_out.astype(bf16).reshape(1, tile_count, seq_len, model_width)
     pixel_result = pixel_grad.transpose(1, 0, 2).reshape(1, tile_count, seq_len, band_slots, pixel_count)
@@ -708,13 +815,248 @@
     )
 
 
+def row_sum(values):
+    return jnp.sum(values.astype(f32), axis=0)
+
+
+def general_body(
+    pixels,
+    wave_table,
+    wave_weight,
+    wave_bias,
+    gen_weight,
+    patch_bias,
+    norm1_gain,
+    norm1_bias,
+    qkv_weight,
+    query_bias,
+    value_bias,
+    out_weight,
+    out_bias,
+    norm2_gain,
+    norm2_bias,
+    fc1_weight,
+    fc1_bias,
+    fc2_weight,
+    fc2_bias,
+    band_count,
+    band_table,
+    cotangent,
+):
+    tile_count, seq_len, band_slots, pixel_count = pixels.shape[1:]
+    model_width = gen_weight.shape[1]
+    wave_width = wave_weight.shape[0]
+    head_size = model_width // HEADS
+    score_scale = head_size ** (-0.5)
+    row_count = tile_count * seq_len
+    head_shape = (tile_count, seq_len, HEADS, head_size)
+    pixel_rows = pixels.reshape(row_count, band_slots, pixel_count)
+    onehot = (band_table[0][:, None] == jnp.arange(wave_table.shape[0])[None, :]).astype(
+        f32
+    )
+    wavelength = jnp.dot(onehot, wave_table, precision=highest)
+    wave_embed = sincos(wavelength * 1000.0, wave_width)
+    live = (jnp.arange(band_slots) < band_count[0]).astype(f32)[:, None]
+
+    def hyper_fn(weight, bias):
+        return jax.nn.gelu(jnp.dot(wave_embed, weight, precision=highest) + bias) * live
+
+    hyper, hyper_back = jax.vjp(hyper_fn, wave_weight.astype(f32), wave_bias)
+    hyper_low = hyper.astype(bf16)
+    patches = jnp.einsum("bk,rbp->rkp", hyper_low, pixel_rows, preferred_element_type=f32)
+    patches = patches.astype(bf16).reshape(row_count, wave_width * pixel_count)
+    position = sincos(jnp.arange(seq_len).astype(f32), model_width)
+    columns = patches
+    projected = dense_dot(columns, lax.all_gather(gen_weight, "row", axis=0, tiled=True))
+    embedded = (projected + patch_bias).reshape(tile_count, seq_len, model_width) + position
+    embedded = embedded.reshape(row_count, model_width)
+    w_qkv, w_out, w_fc1, w_fc2 = (
+        lax.all_gather(qkv_weight, "row", axis=0, tiled=True),
+        lax.all_gather(out_weight, "row", axis=0, tiled=True),
+        lax.all_gather(fc1_weight, "row", axis=0, tiled=True),
+        lax.all_gather(fc2_weight, "row", axis=0, tiled=True),
+    )
+
+    def front(inputs):
+        normed = layer_norm(inputs, norm1_gain, norm1_bias).astype(bf16)
+        mixed = dense_dot(normed, w_qkv)
+        queries = (mixed[:, :model_width] + query_bias).astype(bf16).reshape(head_shape)
+        key_rows = mixed[:, model_width : 2 * model_width].astype(bf16).reshape(head_shape)
+        value_rows = (
+            (mixed[:, 2 * model_width :] + value_bias).astype(bf16).reshape(head_shape)
+        )
+        return (normed, queries, key_rows, value_rows)
+
+    def scores_of(queries, key_rows):
+        return (
+            jnp.einsum("tqhd,tkhd->thqk", queries, key_rows, preferred_element_type=f32)
+            * score_scale
+        )
+
+    def attend(probs, value_rows):
+        mixed_heads = jnp.einsum(
+            "thqk,tkhd->tqhd", probs, value_rows, preferred_element_type=f32
+        )
+        return mixed_heads.astype(bf16).reshape(row_count, model_width)
+
+    def back_half(inputs, attended):
+        middle = inputs + dense_dot(attended, w_out) + out_bias
+        normed_two = layer_norm(middle, norm2_gain, norm2_bias).astype(bf16)
+        fc_pre = dense_dot(normed_two, w_fc1) + fc1_bias
+        hidden = jax.nn.gelu(fc_pre).astype(bf16)
+        return (middle, normed_two, fc_pre, hidden)
+
+    normed, queries, key_rows, value_rows = front(embedded)
+    scores = scores_of(queries, key_rows)
+    log_total = jax.nn.logsumexp(scores, axis=-1, keepdims=True)
+    attended = attend(jnp.exp(scores - log_total).astype(bf16), value_rows)
+    middle, normed_two, fc_pre, hidden = back_half(embedded, attended)
+    block_out = middle + dense_dot(hidden, w_fc2) + fc2_bias
+    grad_out = cotangent.reshape(row_count, model_width)
+    normed, queries, key_rows, value_rows = front(embedded)
+    probs_full = jnp.exp(scores_of(queries, key_rows) - log_total)
+    probs = probs_full.astype(bf16)
+    attended = attend(probs, value_rows)
+    middle, normed_two, fc_pre, hidden = back_half(embedded, attended)
+    fc2_bias_part = row_sum(grad_out)
+    fc2_grad = left_dot(hidden, grad_out)
+    grad_hidden = right_dot(grad_out, w_fc2)
+    grad_pre = jax.vjp(jax.nn.gelu, fc_pre)[1](grad_hidden)[0].astype(bf16)
+    fc1_bias_part = row_sum(grad_pre)
+    fc1_grad = left_dot(normed_two, grad_pre)
+    grad_normed_two = right_dot(grad_pre, w_fc1)
+    norm_two_back = jax.vjp(layer_norm, middle, norm2_gain, norm2_bias)[1]
+    grad_middle, norm2_gain_part, norm2_bias_part = norm_two_back(grad_normed_two)
+    grad_middle = grad_middle + grad_out.astype(f32)
+    grad_branch = grad_middle.astype(bf16)
+    out_bias_part = row_sum(grad_branch)
+    out_grad = left_dot(attended, grad_branch)
+    grad_attended = right_dot(grad_branch, w_out).astype(bf16).reshape(head_shape)
+    grad_probs = jnp.einsum(
+        "tqhd,tkhd->thqk", grad_attended, value_rows, preferred_element_type=f32
+    )
+    grad_scores = probs_full * (
+        grad_probs - jnp.sum(probs_full * grad_probs, axis=-1, keepdims=True)
+    )
+    grad_scores = grad_scores.astype(bf16)
+    grad_queries = (
+        jnp.einsum("thqk,tkhd->tqhd", grad_scores, key_rows, preferred_element_type=f32)
+        * score_scale
+    ).astype(bf16)
+    grad_keys = (
+        jnp.einsum("thqk,tqhd->tkhd", grad_scores, queries, preferred_element_type=f32)
+        * score_scale
+    ).astype(bf16)
+    grad_values = jnp.einsum(
+        "thqk,tqhd->tkhd", probs, grad_attended, preferred_element_type=f32
+    ).astype(bf16)
+    grad_queries = grad_queries.reshape(row_count, model_width)
+    grad_values = grad_values.reshape(row_count, model_width)
+    grad_mixed = jnp.concatenate(
+        [grad_queries, grad_keys.reshape(row_count, model_width), grad_values], axis=1
+    )
+    query_bias_part = row_sum(grad_queries)
+    value_bias_part = row_sum(grad_values)
+    qkv_grad = left_dot(normed, grad_mixed)
+    grad_normed = right_dot(grad_mixed, w_qkv)
+    norm_one_back = jax.vjp(layer_norm, embedded, norm1_gain, norm1_bias)[1]
+    grad_from_norm, norm1_gain_part, norm1_bias_part = norm_one_back(grad_normed)
+    grad_embedded = (grad_middle + grad_from_norm).astype(bf16)
+    patch_bias_part = row_sum(grad_embedded)
+    grad_patches = right_dot(
+        grad_embedded, lax.all_gather(gen_weight, "row", axis=0, tiled=True)
+    ).astype(bf16)
+    grad_cube = grad_patches.reshape(row_count, wave_width, pixel_count)
+    pixel_grad = jnp.einsum(
+        "rkp,bk->rbp", grad_cube, hyper_low, preferred_element_type=f32
+    ).astype(bf16)
+    grad_hyper = jnp.einsum(
+        "rkp,rbp->bk", grad_cube, pixel_rows, preferred_element_type=f32
+    )
+    wave_weight_part, wave_bias_part = hyper_back(grad_hyper)
+    columns = patches
+    gen_part = lax.psum_scatter(
+        left_dot(columns, grad_embedded), "row", scatter_dimension=0, tiled=True
+    )
+    qkv_share, out_share, fc1_share, fc2_share = (
+        lax.psum_scatter(qkv_grad, "row", scatter_dimension=0, tiled=True),
+        lax.psum_scatter(out_grad, "row", scatter_dimension=0, tiled=True),
+        lax.psum_scatter(fc1_grad, "row", scatter_dimension=0, tiled=True),
+        lax.psum_scatter(fc2_grad, "row", scatter_dimension=0, tiled=True),
+    )
+    gen_total, qkv_total, out_total, fc1_total, fc2_total = (
+        lax.psum(gen_part.astype(bf16), "grp").astype(f32),
+        lax.psum(qkv_share.astype(bf16), "grp").astype(f32),
+        lax.psum(out_share.astype(bf16), "grp").astype(f32),
+        lax.psum(fc1_share.astype(bf16), "grp").astype(f32),
+        lax.psum(fc2_share.astype(bf16), "grp").astype(f32),
+    )
+    small_totals = lax.psum(
+        (
+            wave_weight_part,
+            wave_bias_part,
+            patch_bias_part,
+            norm1_gain_part,
+            norm1_bias_part,
+            query_bias_part,
+            value_bias_part,
+            out_bias_part,
+            norm2_gain_part,
+            norm2_bias_part,
+            fc1_bias_part,
+            fc2_bias_part,
+        ),
+        ("grp", "row"),
+    )
+    (
+        wave_weight_total,
+        wave_bias_total,
+        patch_bias_total,
+        norm1_gain_total,
+        norm1_bias_total,
+        query_bias_total,
+        value_bias_total,
+        out_bias_total,
+        norm2_gain_total,
+        norm2_bias_total,
+        fc1_bias_total,
+        fc2_bias_total,
+    ) = small_totals
+    block_result = block_out.astype(bf16).reshape(1, tile_count, seq_len, model_width)
+    pixel_result = pixel_grad.reshape(1, tile_count, seq_len, band_slots, pixel_count)
+    return (
+        block_result,
+        pixel_result,
+        wave_weight_total,
+        wave_bias_total,
+        gen_total,
+        patch_bias_total,
+        norm1_gain_total,
+        norm1_bias_total,
+        qkv_total,
+        query_bias_total,
+        value_bias_total,
+        out_total,
+        out_bias_total,
+        norm2_gain_total,
+        norm2_bias_total,
+        fc1_total,
+        fc1_bias_total,
+        fc2_total,
+        fc2_bias_total,
+    )
+
+
 def solution(mesh):
     grp_size, row_size = mesh.devices.shape
-    split = Mesh(mesh.devices.reshape(grp_size // 2, 2, row_size // 2, 2), AXES)
-    grp, row = ("x", "c"), ("z", "y")
+    if (grp_size, row_size) == PLANNED:
+        step, grp, row = body, ("x", "c"), ("z", "y")
+        mesh = Mesh(mesh.devices.reshape(grp_size // 2, 2, row_size // 2, 2), AXES)
+    else:
+        step, grp, row = general_body, "grp", "row"
     return jax.shard_map(
-        body,
-        mesh=split,
+        step,
+        mesh=mesh,
         in_specs=(
             P(grp, row, None, None, None),
             P(),

time: 592 us -> 552 us (0.932)
  local copies, waits for them, and re-layouts: 65.1 us -> 31.3 us
  other arithmetic: 43.8 us -> 30.5 us
  waiting for transfers between devices: 257 us -> 268 us
    ppermute x2, waiting for transfers between devices: 20.5 us -> 1.94 us  [total_of(): lax.ppermute(value, 'z', [(i, i ^ step) for i in range(size)])]
    dot_general x6 -> x0, matrix products: 14.3 us -> none  [block_grad(): jnp.einsum('dri,drj->dij', *(v if v.shape[0] == 2 else v[part:part + 2] f...]
    ppermute x5, waiting for transfers between devices: 47.3 us -> 61.6 us  [swap_plane(): lax.ppermute(values[3], ('x', 'y'), CORNER)]
    unnamed x330 -> x227, local copies, waits for them, and re-layouts: 19.8 us -> 6.66 us
    dot_general x12, matrix products: 13.2 us -> 23.4 us  [right_dot(): lax.dot_general(left, right, (((1,), (1,)), ((), ())), preferred_element_...]
    another operation x28 -> x6, other arithmetic: 15.8 us -> 7.94 us  [the longest x3 6.32 us: body(): attn = jnp.stack(both_cores(gather_end(*attn, *attn_came)[0]))]
    ppermute x11, waiting for transfers between devices: 90.8 us -> 83 us  [swap_y(): return lax.ppermute(value, 'y', PAIR)]
    ppermute x18 -> x20, waiting for transfers between devices: 0.05 us -> 7.46 us  [swap_core(): return lax.ppermute(value, 'c', PAIR)]
  transfers between devices with their start and end apart: 61 -> 63, of which waited for: 25 -> 28; matrix products, arithmetic and copies ran while one was open for 17% -> 14% of each run, Pallas kernels for 14% -> 13%
where the time goes in v3:
time: 552 us; the launch traced here: 549 us
  waiting for transfers between devices  268 us (49%)
  Pallas kernels  97.5 us (18%)
  starting transfers between devices  61 us (11%)
  matrix products  43.9 us (8%)
  local copies, waits for them, and re-layouts  31.3 us (6%)
  other arithmetic  30.5 us (6%)
  between operations  16.6 us (3%)
    ppermute x11, waiting for transfers between devices, swap_y(): return lax.ppermute(value, 'y', PAIR)  83 us
    ppermute x5, waiting for transfers between devices, swap_plane(): lax.ppermute(values[3], ('x', 'y'), CORNER)  61.6 us
    ppermute x2, waiting for transfers between devices, gather_z_start(): return (lax.ppermute(own, 'z', UP), lax.ppermute(own, 'z', DOWN))  39.6 us
    ppermute x14, waiting for transfers between devices, swap_x(): return lax.ppermute(value, 'x', PAIR)  37.9 us
    dot_general x12, matrix products, right_dot(): lax.dot_general(left, right, (((1,), (1,)), ((), ())), preferred_element_...  23.4 us
    pallas_call x2, Pallas kernels, back_patches(): pl.pallas_call(back_kernel, grid=(share // GEN_STEP,), in_specs=[pl.Block...  21.3 us
    ppermute x1, waiting for transfers between devices, gather_z_end(): lax.ppermute(above[..., half:, :], 'z', DOWN)  20.9 us
    pallas_call x2, Pallas kernels, pixel_back(): pl.pallas_call(pixel_kernel, grid=(rows // MIX_ROWS,), in_specs=[pl.Block...  20.7 us
  transfers between devices with their start and end apart: 63, of which 28 were waited for; matrix products, arithmetic and copies ran while one was open for 14% of the time, Pallas kernels for 13%

profile of v3, /device:TPU:0, one launch (start us, length us, event | category | flops | bytes accessed | tf_op | source)
XLA Modules:
  0.0 549.1 jit_solution(588698105102942912)
XLA Ops:
  7.3 2.7 constant_dynamic-slice_fusion.4
  12.6 13.4 %mix_pixels.1 = (bf16[32,128,256]{2,1,0:T(8,128)(2,1)}, bf16[32,128,256]{2,1,0:T(8,128)(2,1)S(1)}, bf16[32,128,256]{2,1,0:T(8,128)(2,1)}, bf16[32,128,256]{2,1,0:T(8,128)(2,1)}) custom-call(bf16[128,202]{1,0:T(8,128)(2,1)S(1)} %copy.147.hyper_ref, bf16[202,128,256]{2,1,0:T(8,128)(2,1)} %bitcast.324), custom_call_target="tpu_custom_call" | custom-call | flops 1 | bytes 1 | tf_op jit(solution)/shard_map/mix_pixels/pallas_call | solution.py:71
  26.1 2.9 collective-permute-start.4
  30.6 4.1 collective-permute-start.1
  34.9 35.7 %collective-permute-done.1 = bf16[3,96,768]{2,1,0:T(8,128)(2,1)S(1)} collective-permute-done((bf16[3,96,768]{2,1,0:T(8,128)(2,1)S(1)}, bf16[3,96,768]{2,1,0:T(8,128)(2,1)S(1)}, u32[]{:S(2)}, u32[]{:S(2)}) %collective-permute-start.1) | collective-permute-done | bytes 442400 | tf_op jit(solution)/shard_map/ppermute | solution.py:465
  70.7 3.9 collective-permute-done
  76.7 20.9 %collective-permute-done.3 = bf16[3,48,768]{2,1,0:T(8,128)(2,1)S(1)} collective-permute-done((bf16[3,48,768]{2,1,0:T(8,128)(2,1)S(1)}, bf16[3,48,768]{2,1,0:T(8,128)(2,1)S(1)}, u32[]{:S(2)}, u32[]{:S(2)}) %collective-permute-start.3) | collective-permute-done | bytes 221216 | tf_op jit(solution)/shard_map/ppermute | solution.py:476
  97.7 23.4 %collective-permute-done.6.a3.refs_3_ = bf16[32,128,256]{2,1,0:T(8,128)(2,1)} collective-permute-done((bf16[32,128,256]{2,1,0:T(8,128)(2,1)}, bf16[32,128,256]{2,1,0:T(8,128)(2,1)}, u32[]{:S(2)}, u32[]{:S(2)}) %collective-permute-start.6) | collective-permute-done | bytes 2097184 | tf_op jit(solution)/shard_map/ppermute | solution.py:447
  125.5 17.4 %collective-permute-done.7 = bf16[2,3,96,768]{3,2,1,0:T(8,128)(2,1)} collective-permute-done((bf16[2,3,96,768]{3,2,1,0:T(8,128)(2,1)}, bf16[2,3,96,768]{3,2,1,0:T(8,128)(2,1)}, u32[]{:S(2)}, u32[]{:S(2)}) %collective-permute-start.7) | collective-permute-done | bytes 884768 | tf_op jit(solution)/shard_map/ppermute | solution.py:439
  149.6 8.0 %collective-permute-done.8 = bf16[1,384,768]{2,1,0:T(8,128)(2,1)S(1)} collective-permute-done((bf16[1,384,768]{2,1,0:T(8,128)(2,1)S(1)}, bf16[1,384,768]{2,1,0:T(8,128)(2,1)S(1)}, u32[]{:S(2)}, u32[]{:S(2)}) %collective-permute-start.8) | collective-permute-done | bytes 589856 | tf_op jit(solution)/shard_map/ppermute | solution.py:435
  166.0 2.4 slice_bitcast_fusion.4
  170.5 12.4 %project.1 = f32[512,768]{1,0:T(8,128)S(1)} custom-call(bf16[32,128,256]{2,1,0:T(8,128)(2,1)} %get-tuple-element.130.a0.refs_0_, bf16[32,128,256]{2,1,0:T(8,128)(2,1)} %collective-permute-done.4.a1.refs_1_, bf16[32,128,256]{2,1,0:T(8,128)(2,1)} %collective-permute-done.5.a2.refs_2_, bf16[32,128,256]{2,1,0:T(8,128)(2,1)} %collective-permute-done.6.a3.refs_3_, ...), custom_call_target="tpu_custom_call" | custom-call | flops 1 | bytes 1 | tf_op jit(solution)/shard_map/project/pallas_call | solution.py:99
  186.6 4.0 pad_maximum_fusion
  190.7 10.5 %collective-permute-done.11 = bf16[128,768]{1,0:T(8,128)(2,1)S(1)} collective-permute-done((bf16[128,768]{1,0:T(8,128)(2,1)S(1)}, bf16[128,768]{1,0:T(8,128)(2,1)S(1)}, u32[]{:S(2)}, u32[]{:S(2)}) %collective-permute-start.11) | collective-permute-done | bytes 196640 | tf_op jit(solution)/shard_map/ppermute | solution.py:439
  222.2 2.3 collective-permute-done.18
  234.2 3.2 multiply_reduce_fusion
  237.4 3.0 convert_reduce_fusion.2
  245.2 12.6 %convolution_add_fusion.1 = f32[128,768]{1,0:T(8,128)S(1)} fusion(f32[128,768]{1,0:T(8,128)S(1)} %fusion.11, bf16[128,768]{0,1:T(8,128)(2,1)S(1)} %bitcast.354, bf16[4,768,768]{2,1,0:T(8,128)(2,1)} %pad_maximum_fusion, s32[]{:T(128)S(6)} %select_n.319), kind=kOutput, calls=%fused_computation.23 | convolution fusion | flops 151093248 | bytes 2162692 | tf_op jit(solution)/shard_map/dot_general | solution.py:49
  264.6 5.2 collective-permute-done.30.g3.refs_11_
  269.8 3.2 collective-permute-done.29.g2.refs_10_
  273.4 11.0 %back_patches.2 = (bf16[32,96,256]{2,1,0:T(8,128)(2,1)S(1)}, bf16[32,96,256]{2,1,0:T(8,128)(2,1)S(1)}, bf16[32,96,256]{2,1,0:T(8,128)(2,1)S(1)}, bf16[32,96,256]{2,1,0:T(8,128)(2,1)}) custom-call(bf16[128,768]{1,0:T(8,128)(2,1)S(1)} %get-tuple-element.156.g0.refs_8_, bf16[128,768]{1,0:T(8,128)(2,1)S(1)} %collective-permute-done.28.g1.refs_9_, ...), custom_call_target="tpu_custom_call" | custom-call | flops 1 | bytes 1 | tf_op jit(solution)/shard_map/back_patches/pallas_call | solution.py:127
  286.8 2.3 collective-permute-done.34.refs_12_
  289.1 10.1 %gen_grad.1 = (bf16[4,2,256,768]{3,2,1,0:T(8,128)(2,1)}, bf16[4,2,256,768]{3,2,1,0:T(8,128)(2,1)}) custom-call(s32[1]{0:T(128)} %bitcast.97.core_ref, bf16[32,128,256]{2,1,0:T(8,128)(2,1)} %get-tuple-element.130.a0.refs_0_, bf16[32,128,256]{2,1,0:T(8,128)(2,1)} %collective-permute-done.4.a1.refs_1_, bf16[32,128,256]{2,1,0:T(8,128)(2,1)} %collective-permute-done.5.a2.refs_2_, ...), custom_call_target="tpu_custom_call" | custom-call | flops 1 | bytes 1 | tf_op jit(solution)/shard_map/gen_grad/pallas_call | solution.py:155
  310.3 2.2 collective-permute-done.27.late_came
  312.5 6.4 %sum_blocks.1 = (bf16[2,3,2,96,768]{4,3,2,1,0:T(8,128)(2,1)}, bf16[2,3,2,96,768]{4,3,2,1,0:T(8,128)(2,1)}, bf16[3,2,2,96,768]{4,3,2,1,0:T(8,128)(2,1)}, bf16[3,2,2,96,768]{4,3,2,1,0:T(8,128)(2,1)}) custom-call(s32[2]{0:T(128)S(1)} %get-tuple-element.219.left_at, s32[2]{0:T(128)S(1)} %get-tuple-element.220.late_at, s32[1]{0:T(128)} %bitcast.60.y_at, ...), custom_call_target="tpu_custom_call" | custom-call | flops 1 | bytes 1 | tf_op jit(solution)/shard_map/sum_blocks/pallas_call | solution.py:358
  318.9 10.2 %back_patches.3 = (bf16[32,32,256]{2,1,0:T(8,128)(2,1)S(1)}, bf16[32,32,256]{2,1,0:T(8,128)(2,1)}, bf16[32,32,256]{2,1,0:T(8,128)(2,1)}, bf16[32,32,256]{2,1,0:T(8,128)(2,1)}) custom-call(bf16[128,768]{1,0:T(8,128)(2,1)S(1)} %get-tuple-element.156.g0.refs_8_, bf16[128,768]{1,0:T(8,128)(2,1)S(1)} %copy-done.5, bf16[128,768]{1,0:T(8,128)(2,1)S(1)} %copy-done.3, ...), custom_call_target="tpu_custom_call" | custom-call | flops 1 | bytes 1 | tf_op jit(solution)/shard_map/back_patches/pallas_call | solution.py:127
  329.2 7.6 %collective-permute-done.31.g1 = bf16[32,96,256]{2,1,0:T(8,128)(2,1)} collective-permute-done((bf16[32,96,256]{2,1,0:T(8,128)(2,1)}, bf16[32,96,256]{2,1,0:T(8,128)(2,1)}, u32[]{:S(2)}, u32[]{:S(2)}) %collective-permute-start.31) | collective-permute-done | bytes 1572896 | tf_op jit(solution)/shard_map/ppermute | solution.py:439
  338.7 33.0 %collective-permute-done.33.g3 = bf16[32,96,256]{2,1,0:T(8,128)(2,1)} collective-permute-done((bf16[32,96,256]{2,1,0:T(8,128)(2,1)}, bf16[32,96,256]{2,1,0:T(8,128)(2,1)}, u32[]{:S(2)}, u32[]{:S(2)}) %collective-permute-start.33) | collective-permute-done | bytes 1572896 | tf_op jit(solution)/shard_map/ppermute | solution.py:447
  381.1 14.6 %pixel_back.2 = (bf16[202,128,256]{2,1,0:T(8,128)(2,1)}, f32[202,128]{1,0:T(8,128)S(1)}) custom-call(bf16[202,128]{1,0:T(8,128)(2,1)S(1)} %copy-done.13, bf16[202,128,256]{2,1,0:T(8,128)(2,1)} %bitcast.325, bf16[32,96,256]{2,1,0:T(8,128)(2,1)S(1)} %copy-done.7, bf16[32,96,256]{2,1,0:T(8,128)(2,1)} %collective-permute-done.31.g1, ...), custom_call_target="tpu_custom_call" | custom-call | flops 1 | bytes 1 | tf_op jit(solution)/shard_map/pixel_back/pallas_call | solution.py:194
  395.7 42.5 %collective-permute-done.35.g1 = bf16[32,32,256]{2,1,0:T(8,128)(2,1)S(1)} collective-permute-done((bf16[32,32,256]{2,1,0:T(8,128)(2,1)}, bf16[32,32,256]{2,1,0:T(8,128)(2,1)S(1)}, u32[]{:S(2)}, u32[]{:S(2)}) %collective-permute-start.35) | collective-permute-done | bytes 524320 | tf_op jit(solution)/shard_map/ppermute | solution.py:439
  438.2 2.3 fusion.43
  441.7 2.5 fusion.44
  446.5 6.1 %pixel_back.3 = (bf16[202,128,256]{2,1,0:T(8,128)(2,1)}, f32[202,128]{1,0:T(8,128)S(1)}) custom-call(bf16[202,128]{1,0:T(8,128)(2,1)S(1)} %copy-done.13, bf16[202,128,256]{2,1,0:T(8,128)(2,1)} %bitcast.326, bf16[32,32,256]{2,1,0:T(8,128)(2,1)S(1)} %get-tuple-element.175.g0, ...), custom_call_target="tpu_custom_call", output_to_operand_aliasing={{0}: (6, {})} | custom-call | flops 1 | bytes 1 | tf_op jit(solution)/shard_map/pixel_back/pallas_call | solution.py:194
  452.7 7.5 %collective-permute-done.40 = bf16[3,2,96,768]{3,2,0,1:T(8,128)(2,1)S(1)} collective-permute-done((bf16[3,2,96,768]{3,2,0,1:T(8,128)(2,1)}, bf16[3,2,96,768]{3,2,0,1:T(8,128)(2,1)S(1)}, u32[]{:S(2)}, u32[]{:S(2)}) %collective-permute-start.40) | collective-permute-done | bytes 884768 | tf_op jit(solution)/shard_map/ppermute | solution.py:435
  460.2 3.7 collective-permute-done.41
  469.5 3.8 collective-permute-start.47
  474.7 3.8 collective-permute-done.43
  479.5 4.1 collective-permute-start.48
  487.5 7.1 %collective-permute-done.48 = bf16[3,96,768]{2,1,0:T(8,128)(2,1)S(1)} collective-permute-done((bf16[3,96,768]{2,1,0:T(8,128)(2,1)S(1)}, bf16[3,96,768]{2,1,0:T(8,128)(2,1)S(1)}, u32[]{:S(2)}, u32[]{:S(2)}) %collective-permute-start.48) | collective-permute-done | bytes 442400 | tf_op jit(solution)/shard_map/ppermute | solution.py:495
  496.1 7.0 %collective-permute-done.46 = bf16[3,96,768]{2,1,0:T(8,128)(2,1)S(1)} collective-permute-done((bf16[3,96,768]{2,1,0:T(8,128)(2,1)S(1)}, bf16[3,96,768]{2,1,0:T(8,128)(2,1)S(1)}, u32[]{:S(2)}, u32[]{:S(2)}) %collective-permute-start.46) | collective-permute-done | bytes 442400 | tf_op jit(solution)/shard_map/ppermute | solution.py:494
  503.4 2.6 put_parts.4.refs_2_
  506.0 2.3 put_parts.5.refs_2_
  513.2 2.9 collective-permute-start.52
  517.6 6.7 %collective-permute-done.55.refs_0_ = bf16[512,768]{1,0:T(8,128)(2,1)S(1)} collective-permute-done((bf16[512,768]{1,0:T(8,128)(2,1)S(1)}, bf16[512,768]{1,0:T(8,128)(2,1)S(1)}, u32[]{:S(2)}, u32[]{:S(2)}) %collective-permute-start.55) | collective-permute-done | bytes 786464 | tf_op jit(solution)/shard_map/ppermute | solution.py:435
  524.9 6.8 %collective-permute-done.58 = bf16[3,96,768]{2,1,0:T(8,128)(2,1)S(1)} collective-permute-done((bf16[3,96,768]{2,1,0:T(8,128)(2,1)S(1)}, bf16[3,96,768]{2,1,0:T(8,128)(2,1)S(1)}, u32[]{:S(2)}, u32[]{:S(2)}) %collective-permute-start.58) | collective-permute-done | bytes 442400 | tf_op jit(solution)/shard_map/ppermute | solution.py:435
  534.4 3.3 give_pieces.1
  537.6 2.3 put_parts.6.refs_2_
  540.0 2.3 put_parts.7
  (491 shorter events, 124.4 us)
Async XLA Ops:
  7.2 163.3 %all-gather.2.cloned.1.call-start = ((), (), s32[]{:S(2)}) async-start(), calls=%async_computation.2 | async-start | bytes 14155776 | tf_op jit(solution)/shard_map/all_gather | solution.py:600
  10.0 453.9 %reduce-scatter.5.cloned.1.call-start = ((), (), s32[]{:S(2)}) async-start(), calls=%async_computation.4 | async-start | bytes 3932160 | tf_op jit(solution)/shard_map/reduce_scatter | solution.py:736
  26.1 71.6 %collective-permute-start.4 = (bf16[32,128,256]{2,1,0:T(8,128)(2,1)S(1)}, bf16[32,128,256]{2,1,0:T(8,128)(2,1)}, u32[]{:S(2)}, u32[]{:S(2)}) collective-permute-start(bf16[32,128,256]{2,1,0:T(8,128)(2,1)S(1)} %get-tuple-element.109), channel_id=1, source_target_pairs={{0,1},{1,0},{2,3},{3,2},{4,5},{5,4},{6,7},{7,6},{8,9},{9,8},{10,11... | collective-permute-start | bytes 6291464 | tf_op jit(solution)/shard_map/ppermute | solution.py:439
  28.9 68.7 %collective-permute-start.5 = (bf16[32,128,256]{2,1,0:T(8,128)(2,1)}, bf16[32,128,256]{2,1,0:T(8,128)(2,1)}, u32[]{:S(2)}, u32[]{:S(2)}) collective-permute-start(bf16[32,128,256]{2,1,0:T(8,128)(2,1)} %get-tuple-element.110), channel_id=1, source_target_pairs={{0,16},{16,0},{1,17},{17,1},{2,18},{18,2},{3,19},{19,3},{4,20},{20... | collective-permute-start | bytes 6291464 | tf_op jit(solution)/shard_map/ppermute | solution.py:435
  30.4 90.6 %collective-permute-start.6 = (bf16[32,128,256]{2,1,0:T(8,128)(2,1)}, bf16[32,128,256]{2,1,0:T(8,128)(2,1)}, u32[]{:S(2)}, u32[]{:S(2)}) collective-permute-start(bf16[32,128,256]{2,1,0:T(8,128)(2,1)} %get-tuple-element.111), channel_id=1, source_target_pairs={{0,17},{1,16},{16,1},{17,0},{2,19},{3,18},{18,3},{19,2},{4,21},{5,... | collective-permute-start | bytes 6291464 | tf_op jit(solution)/shard_map/ppermute | solution.py:447
  30.6 40.0 %collective-permute-start.1 = (bf16[3,96,768]{2,1,0:T(8,128)(2,1)S(1)}, bf16[3,96,768]{2,1,0:T(8,128)(2,1)S(1)}, u32[]{:S(2)}, u32[]{:S(2)}) collective-permute-start(bf16[3,96,768]{2,1,0:T(8,128)(2,1)S(1)} %take_pieces.1), channel_id=1, source_target_pairs={{0,6},{2,0},{4,2},{6,4},{1,7},{3,1},{5,3},{7,5},{8,14},{10,8},{12,... | collective-permute-start | bytes 1327112 | tf_op jit(solution)/shard_map/ppermute | solution.py:465
  34.7 39.9 %collective-permute-start = (bf16[3,96,768]{2,1,0:T(8,128)(2,1)S(1)}, bf16[3,96,768]{2,1,0:T(8,128)(2,1)S(1)}, u32[]{:S(2)}, u32[]{:S(2)}) collective-permute-start(bf16[3,96,768]{2,1,0:T(8,128)(2,1)S(1)} %take_pieces.1), channel_id=1, source_target_pairs={{0,2},{2,4},{4,6},{6,0},{1,3},{3,5},{5,7},{7,1},{8,10},{10,12},{12... | collective-permute-start | bytes 1327112 | tf_op jit(solution)/shard_map/ppermute | solution.py:465
  70.7 26.9 %collective-permute-start.3 = (bf16[3,48,768]{2,1,0:T(8,128)(2,1)S(1)}, bf16[3,48,768]{2,1,0:T(8,128)(2,1)S(1)}, u32[]{:S(2)}, u32[]{:S(2)}) collective-permute-start(bf16[3,48,768]{2,1,0:T(8,128)(2,1)S(1)} %slice.224), channel_id=1, source_target_pairs={{0,6},{2,0},{4,2},{6,4},{1,7},{3,1},{5,3},{7,5},{8,14},{10,8},{12,... | collective-permute-start | bytes 663560 | tf_op jit(solution)/shard_map/ppermute | solution.py:476
  74.6 23.0 %collective-permute-start.2 = (bf16[3,48,768]{2,1,0:T(8,128)(2,1)S(1)}, bf16[3,48,768]{2,1,0:T(8,128)(2,1)S(1)}, u32[]{:S(2)}, u32[]{:S(2)}) collective-permute-start(bf16[3,48,768]{2,1,0:T(8,128)(2,1)S(1)} %slice.223), channel_id=1, source_target_pairs={{0,2},{2,4},{4,6},{6,0},{1,3},{3,5},{5,7},{7,1},{8,10},{10,12},{12... | collective-permute-start | bytes 663560 | tf_op jit(solution)/shard_map/ppermute | solution.py:475
  122.1 20.8 %collective-permute-start.7 = (bf16[2,3,96,768]{3,2,1,0:T(8,128)(2,1)}, bf16[2,3,96,768]{3,2,1,0:T(8,128)(2,1)}, u32[]{:S(2)}, u32[]{:S(2)}) collective-permute-start(bf16[2,3,96,768]{3,2,1,0:T(8,128)(2,1)} %slice.179), channel_id=1, source_target_pairs={{0,1},{1,0},{2,3},{3,2},{4,5},{5,4},{6,7},{7,6},{8,9},{9,8},{10,11... | collective-permute-start | bytes 2654216 | tf_op jit(solution)/shard_map/ppermute | solution.py:439
  123.9 21.7 %collective-permute-start.9 = (bf16[2,3,96,768]{3,2,0,1:T(8,128)(2,1)S(1)}, bf16[2,3,96,768]{3,2,0,1:T(8,128)(2,1)S(1)}, u32[]{:S(2)}, u32[]{:S(2)}) collective-permute-start(bf16[2,3,96,768]{3,2,0,1:T(8,128)(2,1)S(1)} %slice.226), channel_id=1, source_target_pairs={{0,16},{16,0},{1,17},{17,1},{2,18},{18,2},{3,19},{19,3},{4,20},{20... | collective-permute-start | bytes 2654216 | tf_op jit(solution)/shard_map/ppermute | solution.py:435
  144.2 13.3 %collective-permute-start.8 = (bf16[1,384,768]{2,1,0:T(8,128)(2,1)S(1)}, bf16[1,384,768]{2,1,0:T(8,128)(2,1)S(1)}, u32[]{:S(2)}, u32[]{:S(2)}) collective-permute-start(bf16[1,384,768]{2,1,0:T(8,128)(2,1)S(1)} %bitcast.335), channel_id=1, source_target_pairs={{0,16},{16,0},{1,17},{17,1},{2,18},{18,2},{3,19},{19,3},{4,20},{20... | collective-permute-start | bytes 1769480 | tf_op jit(solution)/shard_map/ppermute | solution.py:435
  145.7 12.8 %collective-permute-start.10 = (bf16[2,2,1,96,768]{4,3,2,1,0:T(8,128)(2,1)S(1)}, bf16[2,2,1,96,768]{4,3,2,1,0:T(8,128)(2,1)S(1)}, u32[]{:S(2)}, u32[]{:S(2)}) collective-permute-start(bf16[2,2,1,96,768]{4,3,2,1,0:T(8,128)(2,1)S(1)} %pad_maximum_fusion.12), channel_id=1, source_target_pairs={{0,1},{1,0},{2,3},{3,2},{4,5},{5,4},{6,7},{7,6},{8,9},{9,8},{10,11... | collective-permute-start | bytes 1769480 | tf_op jit(solution)/shard_map/ppermute | solution.py:439
  160.0 24.1 %collective-permute-start.14 = (bf16[768,768]{1,0:T(8,128)(2,1)}, bf16[768,768]{1,0:T(8,128)(2,1)}, u32[]{:S(2)}, u32[]{:S(2)}) collective-permute-start(bf16[768,768]{1,0:T(8,128)(2,1)} %get-tuple-element.252), channel_id=1, source_target_pairs={{0,8},{8,0},{1,9},{9,1},{2,10},{10,2},{3,11},{11,3},{4,12},{12,4},... | collective-permute-start | bytes 3538952 | tf_op jit(solution)/shard_map/ppermute | solution.py:431
  161.2 24.8 %collective-permute-start.15 = (bf16[768,768]{1,0:T(8,128)(2,1)}, bf16[768,768]{1,0:T(8,128)(2,1)}, u32[]{:S(2)}, u32[]{:S(2)}) collective-permute-start(bf16[768,768]{1,0:T(8,128)(2,1)} %get-tuple-element.254), channel_id=1, source_target_pairs={{0,8},{8,0},{1,9},{9,1},{2,10},{10,2},{3,11},{11,3},{4,12},{12,4},... | collective-permute-start | bytes 3538952 | tf_op jit(solution)/shard_map/ppermute | solution.py:431
  164.0 37.4 %collective-permute-start.16 = (bf16[2,384,768]{2,1,0:T(8,128)(2,1)}, bf16[2,384,768]{2,1,0:T(8,128)(2,1)}, u32[]{:S(2)}, u32[]{:S(2)}) collective-permute-start(bf16[2,384,768]{2,1,0:T(8,128)(2,1)} %pad_maximum_fusion.3), channel_id=1, source_target_pairs={{0,16},{16,0},{1,17},{17,1},{2,18},{18,2},{3,19},{19,3},{4,20},{20... | collective-permute-start | bytes 3538952 | tf_op jit(solution)/shard_map/ppermute | solution.py:435
  164.9 36.5 %collective-permute-start.17 = (bf16[2,2,2,96,768]{4,3,2,1,0:T(8,128)(2,1)}, bf16[2,2,2,96,768]{4,3,2,1,0:T(8,128)(2,1)}, u32[]{:S(2)}, u32[]{:S(2)}) collective-permute-start(bf16[2,2,2,96,768]{4,3,2,1,0:T(8,128)(2,1)} %pad_maximum_fusion.2), channel_id=1, source_target_pairs={{0,1},{1,0},{2,3},{3,2},{4,5},{5,4},{6,7},{7,6},{8,9},{9,8},{10,11... | collective-permute-start | bytes 3538952 | tf_op jit(solution)/shard_map/ppermute | solution.py:439
  183.1 18.1 %collective-permute-start.11 = (bf16[128,768]{1,0:T(8,128)(2,1)S(1)}, bf16[128,768]{1,0:T(8,128)(2,1)S(1)}, u32[]{:S(2)}, u32[]{:S(2)}) collective-permute-start(bf16[128,768]{1,0:T(8,128)(2,1)S(1)} %get-tuple-element.255), channel_id=1, source_target_pairs={{0,1},{1,0},{2,3},{3,2},{4,5},{5,4},{6,7},{7,6},{8,9},{9,8},{10,11... | collective-permute-start | bytes 589832 | tf_op jit(solution)/shard_map/ppermute | solution.py:439
  184.1 17.0 %collective-permute-start.13 = (bf16[128,768]{1,0:T(8,128)(2,1)S(1)}, bf16[128,768]{1,0:T(8,128)(2,1)S(1)}, u32[]{:S(2)}, u32[]{:S(2)}) collective-permute-start(bf16[128,768]{1,0:T(8,128)(2,1)S(1)} %get-tuple-element.256), channel_id=1, source_target_pairs={{0,17},{1,16},{16,1},{17,0},{2,19},{3,18},{18,3},{19,2},{4,21},{5,... | collective-permute-start | bytes 589832 | tf_op jit(solution)/shard_map/ppermute | solution.py:447
  186.0 15.2 %collective-permute-start.12 = (bf16[128,768]{1,0:T(8,128)(2,1)S(1)}, bf16[128,768]{1,0:T(8,128)(2,1)S(1)}, u32[]{:S(2)}, u32[]{:S(2)}) collective-permute-start(bf16[128,768]{1,0:T(8,128)(2,1)S(1)} %get-tuple-element.257), channel_id=1, source_target_pairs={{0,16},{16,0},{1,17},{17,1},{2,18},{18,2},{3,19},{19,3},{4,20},{20... | collective-permute-start | bytes 589832 | tf_op jit(solution)/shard_map/ppermute | solution.py:435
  215.1 12.9 %collective-permute-start.21 = (bf16[768,768]{1,0:T(8,128)(2,1)S(1)}, bf16[768,768]{1,0:T(8,128)(2,1)S(1)}, u32[]{:S(2)}, u32[]{:S(2)}) collective-permute-start(bf16[768,768]{1,0:T(8,128)(2,1)S(1)} %pad_maximum_fusion.9), channel_id=1, source_target_pairs={{0,8},{8,0},{1,9},{9,1},{2,10},{10,2},{3,11},{11,3},{4,12},{12,4},... | collective-permute-start | bytes 3538952 | tf_op jit(solution)/shard_map/ppermute | solution.py:431
  218.5 41.2 %collective-permute-start.23 = (bf16[32,128,256]{2,1,0:T(8,128)(2,1)}, bf16[32,128,256]{2,1,0:T(8,128)(2,1)}, u32[]{:S(2)}, u32[]{:S(2)}) collective-permute-start(bf16[32,128,256]{2,1,0:T(8,128)(2,1)} %get-tuple-element.130.a0.refs_0_), channel_id=1, source_target_pairs={{0,8},{8,0},{1,9},{9,1},{2,10},{10,2},{3,11},{11,3},{4,12},{12,4},... | collective-permute-start | bytes 6291464 | tf_op jit(solution)/shard_map/ppermute | solution.py:431
  224.5 35.3 %collective-permute-start.24 = (bf16[32,128,256]{2,1,0:T(8,128)(2,1)}, bf16[32,128,256]{2,1,0:T(8,128)(2,1)}, u32[]{:S(2)}, u32[]{:S(2)}) collective-permute-start(bf16[32,128,256]{2,1,0:T(8,128)(2,1)} %collective-permute-done.4.a1.refs_1_), channel_id=1, source_target_pairs={{0,8},{8,0},{1,9},{9,1},{2,10},{10,2},{3,11},{11,3},{4,12},{12,4},... | collective-permute-start | bytes 6291464 | tf_op jit(solution)/shard_map/ppermute | solution.py:431
  225.1 34.8 %collective-permute-start.25 = (bf16[32,128,256]{2,1,0:T(8,128)(2,1)}, bf16[32,128,256]{2,1,0:T(8,128)(2,1)}, u32[]{:S(2)}, u32[]{:S(2)}) collective-permute-start(bf16[32,128,256]{2,1,0:T(8,128)(2,1)} %collective-permute-done.5.a2.refs_2_), channel_id=1, source_target_pairs={{0,8},{8,0},{1,9},{9,1},{2,10},{10,2},{3,11},{11,3},{4,12},{12,4},... | collective-permute-start | bytes 6291464 | tf_op jit(solution)/shard_map/ppermute | solution.py:431
  225.9 33.9 %collective-permute-start.26 = (bf16[32,128,256]{2,1,0:T(8,128)(2,1)}, bf16[32,128,256]{2,1,0:T(8,128)(2,1)}, u32[]{:S(2)}, u32[]{:S(2)}) collective-permute-start(bf16[32,128,256]{2,1,0:T(8,128)(2,1)} %collective-permute-done.6.a3.refs_3_), channel_id=1, source_target_pairs={{0,8},{8,0},{1,9},{9,1},{2,10},{10,2},{3,11},{11,3},{4,12},{12,4},... | collective-permute-start | bytes 6291464 | tf_op jit(solution)/shard_map/ppermute | solution.py:431
  234.0 25.8 %collective-permute-start.22 = (bf16[8,128,768]{2,1,0:T(8,128)(2,1)}, bf16[8,128,768]{2,1,0:T(8,128)(2,1)S(1)}, u32[]{:S(2)}, u32[]{:S(2)}) collective-permute-start(bf16[8,128,768]{2,1,0:T(8,128)(2,1)} %copy-done.44), channel_id=1, source_target_pairs={{0,8},{8,0},{1,9},{9,1},{2,10},{10,2},{3,11},{11,3},{4,12},{12,4},... | collective-permute-start | bytes 4718600 | tf_op jit(solution)/shard_map/ppermute | solution.py:431
  299.2 164.6 %reduce-scatter.3.cloned.1.call-start = ((), (), s32[]{:S(2)}) async-start(), calls=%async_computation.3 | async-start | bytes 3932160 | tf_op jit(solution)/shard_map/reduce_scatter | solution.py:736
  300.0 36.8 %collective-permute-start.31 = (bf16[32,96,256]{2,1,0:T(8,128)(2,1)}, bf16[32,96,256]{2,1,0:T(8,128)(2,1)}, u32[]{:S(2)}, u32[]{:S(2)}) collective-permute-start(bf16[32,96,256]{2,1,0:T(8,128)(2,1)} %copy-done.17), channel_id=1, source_target_pairs={{0,1},{1,0},{2,3},{3,2},{4,5},{5,4},{6,7},{7,6},{8,9},{9,8},{10,11... | collective-permute-start | bytes 4718600 | tf_op jit(solution)/shard_map/ppermute | solution.py:439
  301.1 37.6 %collective-permute-start.32 = (bf16[32,96,256]{2,1,0:T(8,128)(2,1)}, bf16[32,96,256]{2,1,0:T(8,128)(2,1)}, u32[]{:S(2)}, u32[]{:S(2)}) collective-permute-start(bf16[32,96,256]{2,1,0:T(8,128)(2,1)} %copy-done.16), channel_id=1, source_target_pairs={{0,16},{16,0},{1,17},{17,1},{2,18},{18,2},{3,19},{19,3},{4,20},{20... | collective-permute-start | bytes 4718600 | tf_op jit(solution)/shard_map/ppermute | solution.py:435
  302.5 69.2 %collective-permute-start.33 = (bf16[32,96,256]{2,1,0:T(8,128)(2,1)}, bf16[32,96,256]{2,1,0:T(8,128)(2,1)}, u32[]{:S(2)}, u32[]{:S(2)}) collective-permute-start(bf16[32,96,256]{2,1,0:T(8,128)(2,1)} %get-tuple-element.145), channel_id=1, source_target_pairs={{0,17},{1,16},{16,1},{17,0},{2,19},{3,18},{18,3},{19,2},{4,21},{5,... | collective-permute-start | bytes 4718600 | tf_op jit(solution)/shard_map/ppermute | solution.py:447
  375.2 63.0 %collective-permute-start.39 = (bf16[3,2,2,96,768]{4,3,0,1,2:T(8,128)(2,1)}, bf16[3,2,2,96,768]{4,3,0,1,2:T(8,128)(2,1)}, u32[]{:S(2)}, u32[]{:S(2)}) collective-permute-start(bf16[3,2,2,96,768]{4,3,0,1,2:T(8,128)(2,1)} %copy.173), channel_id=1, source_target_pairs={{0,16},{16,0},{1,17},{17,1},{2,18},{18,2},{3,19},{19,3},{4,20},{20... | collective-permute-start | bytes 5308424 | tf_op jit(solution)/shard_map/ppermute | solution.py:435
  376.3 61.9 %collective-permute-start.38 = (bf16[2,3,2,96,768]{4,3,1,2,0:T(8,128)(2,1)}, bf16[2,3,2,96,768]{4,3,1,2,0:T(8,128)(2,1)}, u32[]{:S(2)}, u32[]{:S(2)}) collective-permute-start(bf16[2,3,2,96,768]{4,3,1,2,0:T(8,128)(2,1)} %copy.172), channel_id=1, source_target_pairs={{0,1},{1,0},{2,3},{3,2},{4,5},{5,4},{6,7},{7,6},{8,9},{9,8},{10,11... | collective-permute-start | bytes 5308424 | tf_op jit(solution)/shard_map/ppermute | solution.py:439
  377.6 60.6 %collective-permute-start.35 = (bf16[32,32,256]{2,1,0:T(8,128)(2,1)}, bf16[32,32,256]{2,1,0:T(8,128)(2,1)S(1)}, u32[]{:S(2)}, u32[]{:S(2)}) collective-permute-start(bf16[32,32,256]{2,1,0:T(8,128)(2,1)} %get-tuple-element.165), channel_id=1, source_target_pairs={{0,1},{1,0},{2,3},{3,2},{4,5},{5,4},{6,7},{7,6},{8,9},{9,8},{10,11... | collective-permute-start | bytes 1572872 | tf_op jit(solution)/shard_map/ppermute | solution.py:439
  378.3 59.9 %collective-permute-start.36 = (bf16[32,32,256]{2,1,0:T(8,128)(2,1)}, bf16[32,32,256]{2,1,0:T(8,128)(2,1)S(1)}, u32[]{:S(2)}, u32[]{:S(2)}) collective-permute-start(bf16[32,32,256]{2,1,0:T(8,128)(2,1)} %get-tuple-element.166), channel_id=1, source_target_pairs={{0,16},{16,0},{1,17},{17,1},{2,18},{18,2},{3,19},{19,3},{4,20},{20... | collective-permute-start | bytes 1572872 | tf_op jit(solution)/shard_map/ppermute | solution.py:435
  379.3 59.0 %collective-permute-start.37 = (bf16[32,32,256]{2,1,0:T(8,128)(2,1)}, bf16[32,32,256]{2,1,0:T(8,128)(2,1)}, u32[]{:S(2)}, u32[]{:S(2)}) collective-permute-start(bf16[32,32,256]{2,1,0:T(8,128)(2,1)} %get-tuple-element.167), channel_id=1, source_target_pairs={{0,17},{1,16},{16,1},{17,0},{2,19},{3,18},{18,3},{19,2},{4,21},{5,... | collective-permute-start | bytes 1572872 | tf_op jit(solution)/shard_map/ppermute | solution.py:447
  440.5 19.6 %collective-permute-start.40 = (bf16[3,2,96,768]{3,2,0,1:T(8,128)(2,1)}, bf16[3,2,96,768]{3,2,0,1:T(8,128)(2,1)S(1)}, u32[]{:S(2)}, u32[]{:S(2)}) collective-permute-start(bf16[3,2,96,768]{3,2,0,1:T(8,128)(2,1)} %fusion.43), channel_id=1, source_target_pairs={{0,16},{16,0},{1,17},{17,1},{2,18},{18,2},{3,19},{19,3},{4,20},{20... | collective-permute-start | bytes 2654216 | tf_op jit(solution)/shard_map/ppermute | solution.py:435
  444.2 19.7 %collective-permute-start.41 = (bf16[3,2,96,768]{3,2,0,1:T(8,128)(2,1)}, bf16[3,2,96,768]{3,2,0,1:T(8,128)(2,1)}, u32[]{:S(2)}, u32[]{:S(2)}) collective-permute-start(bf16[3,2,96,768]{3,2,0,1:T(8,128)(2,1)} %fusion.44), channel_id=1, source_target_pairs={{0,1},{1,0},{2,3},{3,2},{4,5},{5,4},{6,7},{7,6},{8,9},{9,8},{10,11... | collective-permute-start | bytes 2654216 | tf_op jit(solution)/shard_map/ppermute | solution.py:439
  474.1 31.9 %collective-permute-start.49 = (bf16[512,768]{1,0:T(8,128)(2,1)S(1)}, bf16[512,768]{1,0:T(8,128)(2,1)S(1)}, u32[]{:S(2)}, u32[]{:S(2)}) collective-permute-start(bf16[512,768]{1,0:T(8,128)(2,1)S(1)} %copy-done.8), channel_id=1, source_target_pairs={{0,8},{8,0},{1,9},{9,1},{2,10},{10,2},{3,11},{11,3},{4,12},{12,4},... | collective-permute-start | bytes 2359304 | tf_op jit(solution)/shard_map/ppermute | solution.py:431
  474.1 29.3 %collective-permute-start.50 = (bf16[512,768]{1,0:T(8,128)(2,1)S(1)}, bf16[512,768]{1,0:T(8,128)(2,1)S(1)}, u32[]{:S(2)}, u32[]{:S(2)}) collective-permute-start(bf16[512,768]{1,0:T(8,128)(2,1)S(1)} %copy-done.9), channel_id=1, source_target_pairs={{0,8},{8,0},{1,9},{9,1},{2,10},{10,2},{3,11},{11,3},{4,12},{12,4},... | collective-permute-start | bytes 2359304 | tf_op jit(solution)/shard_map/ppermute | solution.py:431
  479.5 15.1 %collective-permute-start.48 = (bf16[3,96,768]{2,1,0:T(8,128)(2,1)S(1)}, bf16[3,96,768]{2,1,0:T(8,128)(2,1)S(1)}, u32[]{:S(2)}, u32[]{:S(2)}) collective-permute-start(bf16[3,96,768]{2,1,0:T(8,128)(2,1)S(1)} %pad_maximum_fusion.23), channel_id=1, source_target_pairs={{0,6},{2,0},{4,2},{6,4},{1,7},{3,1},{5,3},{7,5},{8,14},{10,8},{12,... | collective-permute-start | bytes 1327112 | tf_op jit(solution)/shard_map/ppermute | solution.py:495
  484.8 18.4 %collective-permute-start.46 = (bf16[3,96,768]{2,1,0:T(8,128)(2,1)S(1)}, bf16[3,96,768]{2,1,0:T(8,128)(2,1)S(1)}, u32[]{:S(2)}, u32[]{:S(2)}) collective-permute-start(bf16[3,96,768]{2,1,0:T(8,128)(2,1)S(1)} %pad_maximum_fusion.22), channel_id=1, source_target_pairs={{0,2},{2,4},{4,6},{6,0},{1,3},{3,5},{5,7},{7,1},{8,10},{10,12},{12... | collective-permute-start | bytes 1327112 | tf_op jit(solution)/shard_map/ppermute | solution.py:494
  486.9 30.2 %collective-permute-start.53 = (bf16[512,768]{1,0:T(8,128)(2,1)S(1)}, bf16[512,768]{1,0:T(8,128)(2,1)S(1)}, u32[]{:S(2)}, u32[]{:S(2)}) collective-permute-start(bf16[512,768]{1,0:T(8,128)(2,1)S(1)} %copy-done.8), channel_id=1, source_target_pairs={{0,16},{16,0},{1,17},{17,1},{2,18},{18,2},{3,19},{19,3},{4,20},{20... | collective-permute-start | bytes 2359304 | tf_op jit(solution)/shard_map/ppermute | solution.py:435
  494.6 29.7 %collective-permute-start.55 = (bf16[512,768]{1,0:T(8,128)(2,1)S(1)}, bf16[512,768]{1,0:T(8,128)(2,1)S(1)}, u32[]{:S(2)}, u32[]{:S(2)}) collective-permute-start(bf16[512,768]{1,0:T(8,128)(2,1)S(1)} %copy-done.9), channel_id=1, source_target_pairs={{0,16},{16,0},{1,17},{17,1},{2,18},{18,2},{3,19},{19,3},{4,20},{20... | collective-permute-start | bytes 2359304 | tf_op jit(solution)/shard_map/ppermute | solution.py:435
  510.6 21.2 %collective-permute-start.58 = (bf16[3,96,768]{2,1,0:T(8,128)(2,1)S(1)}, bf16[3,96,768]{2,1,0:T(8,128)(2,1)S(1)}, u32[]{:S(2)}, u32[]{:S(2)}) collective-permute-start(bf16[3,96,768]{2,1,0:T(8,128)(2,1)S(1)} %fusion.48), channel_id=1, source_target_pairs={{0,16},{16,0},{1,17},{17,1},{2,18},{18,2},{3,19},{19,3},{4,20},{20... | collective-permute-start | bytes 1327112 | tf_op jit(solution)/shard_map/ppermute | solution.py:435
  513.2 11.1 %collective-permute-start.52 = (f32[208,128]{1,0:T(8,128)S(1)}, f32[208,128]{1,0:T(8,128)S(1)}, u32[]{:S(2)}, u32[]{:S(2)}) collective-permute-start(f32[208,128]{1,0:T(8,128)S(1)} %add.531), channel_id=1, source_target_pairs={{0,4},{2,6},{4,0},{6,2},{1,5},{3,7},{5,1},{7,3},{8,12},{10,14},{12... | collective-permute-start | bytes 319496 | tf_op jit(solution)/shard_map/ppermute | solution.py:510
  517.1 15.8 %collective-permute-start.57 = (bf16[3,96,768]{2,1,0:T(8,128)(2,1)S(1)}, bf16[3,96,768]{2,1,0:T(8,128)(2,1)S(1)}, u32[]{:S(2)}, u32[]{:S(2)}) collective-permute-start(bf16[3,96,768]{2,1,0:T(8,128)(2,1)S(1)} %fusion.48), channel_id=1, source_target_pairs={{0,8},{8,0},{1,9},{9,1},{2,10},{10,2},{3,11},{11,3},{4,12},{12,4},... | collective-permute-start | bytes 1327112 | tf_op jit(solution)/shard_map/ppermute | solution.py:431
  517.1 22.9 %collective-permute-start.54 = (bf16[512,768]{1,0:T(8,128)(2,1)S(1)}, bf16[512,768]{1,0:T(8,128)(2,1)S(1)}, u32[]{:S(2)}, u32[]{:S(2)}) collective-permute-start(bf16[512,768]{1,0:T(8,128)(2,1)S(1)} %collective-permute-done.53.refs_0_), channel_id=1, source_target_pairs={{0,8},{8,0},{1,9},{9,1},{2,10},{10,2},{3,11},{11,3},{4,12},{12,4},... | collective-permute-start | bytes 2359304 | tf_op jit(solution)/shard_map/ppermute | solution.py:431
  524.3 13.4 %collective-permute-start.56 = (bf16[512,768]{1,0:T(8,128)(2,1)S(1)}, bf16[512,768]{1,0:T(8,128)(2,1)S(1)}, u32[]{:S(2)}, u32[]{:S(2)}) collective-permute-start(bf16[512,768]{1,0:T(8,128)(2,1)S(1)} %collective-permute-done.55.refs_0_), channel_id=1, source_target_pairs={{0,8},{8,0},{1,9},{9,1},{2,10},{10,2},{3,11},{11,3},{4,12},{12,4},... | collective-permute-start | bytes 2359304 | tf_op jit(solution)/shard_map/ppermute | solution.py:431
  (127 other events, 814.7 us)
Sparse Core Ops, SparseCore 0:
  10.1 147.6 all-gather.1
  299.4 61.0 reduce-scatter.4
  363.4 60.2 reduce-scatter.2

commit v4 on v3

--- a/solution.py
+++ b/solution.py
@@ -19,7 +19,7 @@
 AXES = ("x", "c", "z", "y")
 PLANNED = (4, 8)
 VMEM_LIMIT = 48 * 1024 * 1024
-MIX_ROWS = 16
+MIX_ROWS = 32
 GEN_STEP = 4
 COST = pl.CostEstimate(flops=1, bytes_accessed=1, transcendentals=0)
 

time: 552 us -> 551 us (level)
  transfers between devices with their start and end apart: 63 -> 63, of which waited for: 28 -> 28; matrix products, arithmetic and copies ran while one was open for 14% -> 15% of each run, Pallas kernels for 13% -> 13%
where the time goes in v4:
time: 551 us; the launch traced here: 548 us
  waiting for transfers between devices  269 us (49%)
  Pallas kernels  96.3 us (17%)
  starting transfers between devices  60.1 us (11%)
  matrix products  44.8 us (8%)
  local copies, waits for them, and re-layouts  31.3 us (6%)
  other arithmetic  30.5 us (6%)
  between operations  16.6 us (3%)
    ppermute x11, waiting for transfers between devices, swap_y(): return lax.ppermute(value, 'y', PAIR)  83 us
    ppermute x5, waiting for transfers between devices, swap_plane(): lax.ppermute(values[3], ('x', 'y'), CORNER)  64.9 us
    ppermute x2, waiting for transfers between devices, gather_z_start(): return (lax.ppermute(own, 'z', UP), lax.ppermute(own, 'z', DOWN))  39.6 us
    ppermute x14, waiting for transfers between devices, swap_x(): return lax.ppermute(value, 'x', PAIR)  36.7 us
    dot_general x12, matrix products, right_dot(): lax.dot_general(left, right, (((1,), (1,)), ((), ())), preferred_element_...  24.2 us
    pallas_call x2, Pallas kernels, pixel_back(): pl.pallas_call(pixel_kernel, grid=(rows // MIX_ROWS,), in_specs=[pl.Block...  21.5 us
    pallas_call x2, Pallas kernels, back_patches(): pl.pallas_call(back_kernel, grid=(share // GEN_STEP,), in_specs=[pl.Block...  21.3 us
    ppermute x1, waiting for transfers between devices, gather_z_end(): lax.ppermute(above[..., half:, :], 'z', DOWN)  18.6 us
  transfers between devices with their start and end apart: 63, of which 28 were waited for; matrix products, arithmetic and copies ran while one was open for 15% of the time, Pallas kernels for 13%

profile of v4, /device:TPU:0, one launch (start us, length us, event | category | flops | bytes accessed | tf_op | source)
XLA Modules:
  0.0 548.3 jit_solution(2683933368605991894)
XLA Ops:
  7.3 2.7 constant_dynamic-slice_fusion.4
  12.6 11.7 %mix_pixels.1 = (bf16[32,128,256]{2,1,0:T(8,128)(2,1)}, bf16[32,128,256]{2,1,0:T(8,128)(2,1)S(1)}, bf16[32,128,256]{2,1,0:T(8,128)(2,1)}, bf16[32,128,256]{2,1,0:T(8,128)(2,1)}) custom-call(bf16[128,202]{1,0:T(8,128)(2,1)S(1)} %copy.147.hyper_ref, bf16[202,128,256]{2,1,0:T(8,128)(2,1)} %bitcast.324), custom_call_target="tpu_custom_call" | custom-call | flops 1 | bytes 1 | tf_op jit(solution)/shard_map/mix_pixels/pallas_call | solution.py:71
  24.4 3.2 collective-permute-start.4
  29.2 4.1 collective-permute-start.1
  33.5 38.0 %collective-permute-done.1 = bf16[3,96,768]{2,1,0:T(8,128)(2,1)S(1)} collective-permute-done((bf16[3,96,768]{2,1,0:T(8,128)(2,1)S(1)}, bf16[3,96,768]{2,1,0:T(8,128)(2,1)S(1)}, u32[]{:S(2)}, u32[]{:S(2)}) %collective-permute-start.1) | collective-permute-done | bytes 442400 | tf_op jit(solution)/shard_map/ppermute | solution.py:465
  74.3 18.6 %collective-permute-done.3 = bf16[3,48,768]{2,1,0:T(8,128)(2,1)S(1)} collective-permute-done((bf16[3,48,768]{2,1,0:T(8,128)(2,1)S(1)}, bf16[3,48,768]{2,1,0:T(8,128)(2,1)S(1)}, u32[]{:S(2)}, u32[]{:S(2)}) %collective-permute-start.3) | collective-permute-done | bytes 221216 | tf_op jit(solution)/shard_map/ppermute | solution.py:476
  92.9 26.7 %collective-permute-done.6.a3.refs_3_ = bf16[32,128,256]{2,1,0:T(8,128)(2,1)} collective-permute-done((bf16[32,128,256]{2,1,0:T(8,128)(2,1)}, bf16[32,128,256]{2,1,0:T(8,128)(2,1)}, u32[]{:S(2)}, u32[]{:S(2)}) %collective-permute-start.6) | collective-permute-done | bytes 2097184 | tf_op jit(solution)/shard_map/ppermute | solution.py:447
  124.1 17.3 %collective-permute-done.7 = bf16[2,3,96,768]{3,2,1,0:T(8,128)(2,1)} collective-permute-done((bf16[2,3,96,768]{3,2,1,0:T(8,128)(2,1)}, bf16[2,3,96,768]{3,2,1,0:T(8,128)(2,1)}, u32[]{:S(2)}, u32[]{:S(2)}) %collective-permute-start.7) | collective-permute-done | bytes 884768 | tf_op jit(solution)/shard_map/ppermute | solution.py:439
  148.1 7.9 %collective-permute-done.8 = bf16[1,384,768]{2,1,0:T(8,128)(2,1)S(1)} collective-permute-done((bf16[1,384,768]{2,1,0:T(8,128)(2,1)S(1)}, bf16[1,384,768]{2,1,0:T(8,128)(2,1)S(1)}, u32[]{:S(2)}, u32[]{:S(2)}) %collective-permute-start.8) | collective-permute-done | bytes 589856 | tf_op jit(solution)/shard_map/ppermute | solution.py:435
  164.4 2.4 slice_bitcast_fusion.4
  168.9 12.4 %project.1 = f32[512,768]{1,0:T(8,128)S(1)} custom-call(bf16[32,128,256]{2,1,0:T(8,128)(2,1)} %get-tuple-element.130.a0.refs_0_, bf16[32,128,256]{2,1,0:T(8,128)(2,1)} %collective-permute-done.4.a1.refs_1_, bf16[32,128,256]{2,1,0:T(8,128)(2,1)} %collective-permute-done.5.a2.refs_2_, bf16[32,128,256]{2,1,0:T(8,128)(2,1)} %collective-permute-done.6.a3.refs_3_, ...), custom_call_target="tpu_custom_call" | custom-call | flops 1 | bytes 1 | tf_op jit(solution)/shard_map/project/pallas_call | solution.py:99
  185.0 4.0 pad_maximum_fusion
  189.1 10.5 %collective-permute-done.11 = bf16[128,768]{1,0:T(8,128)(2,1)S(1)} collective-permute-done((bf16[128,768]{1,0:T(8,128)(2,1)S(1)}, bf16[128,768]{1,0:T(8,128)(2,1)S(1)}, u32[]{:S(2)}, u32[]{:S(2)}) %collective-permute-start.11) | collective-permute-done | bytes 196640 | tf_op jit(solution)/shard_map/ppermute | solution.py:439
  220.6 2.3 collective-permute-done.18
  232.6 3.2 multiply_reduce_fusion
  235.8 3.0 convert_reduce_fusion.2
  243.6 13.4 %convolution_add_fusion.1 = f32[128,768]{1,0:T(8,128)S(1)} fusion(f32[128,768]{1,0:T(8,128)S(1)} %fusion.11, bf16[128,768]{0,1:T(8,128)(2,1)S(1)} %bitcast.354, bf16[4,768,768]{2,1,0:T(8,128)(2,1)} %pad_maximum_fusion, s32[]{:T(128)S(6)} %select_n.319), kind=kOutput, calls=%fused_computation.23 | convolution fusion | flops 151093248 | bytes 2162692 | tf_op jit(solution)/shard_map/dot_general | solution.py:49
  263.9 5.2 collective-permute-done.30.g3.refs_11_
  269.0 3.2 collective-permute-done.29.g2.refs_10_
  272.6 11.0 %back_patches.2 = (bf16[32,96,256]{2,1,0:T(8,128)(2,1)S(1)}, bf16[32,96,256]{2,1,0:T(8,128)(2,1)S(1)}, bf16[32,96,256]{2,1,0:T(8,128)(2,1)S(1)}, bf16[32,96,256]{2,1,0:T(8,128)(2,1)}) custom-call(bf16[128,768]{1,0:T(8,128)(2,1)S(1)} %get-tuple-element.156.g0.refs_8_, bf16[128,768]{1,0:T(8,128)(2,1)S(1)} %collective-permute-done.28.g1.refs_9_, ...), custom_call_target="tpu_custom_call" | custom-call | flops 1 | bytes 1 | tf_op jit(solution)/shard_map/back_patches/pallas_call | solution.py:127
  286.1 2.3 collective-permute-done.34.refs_12_
  288.4 10.1 %gen_grad.1 = (bf16[4,2,256,768]{3,2,1,0:T(8,128)(2,1)}, bf16[4,2,256,768]{3,2,1,0:T(8,128)(2,1)}) custom-call(s32[1]{0:T(128)} %bitcast.97.core_ref, bf16[32,128,256]{2,1,0:T(8,128)(2,1)} %get-tuple-element.130.a0.refs_0_, bf16[32,128,256]{2,1,0:T(8,128)(2,1)} %collective-permute-done.4.a1.refs_1_, bf16[32,128,256]{2,1,0:T(8,128)(2,1)} %collective-permute-done.5.a2.refs_2_, ...), custom_call_target="tpu_custom_call" | custom-call | flops 1 | bytes 1 | tf_op jit(solution)/shard_map/gen_grad/pallas_call | solution.py:155
  309.5 2.2 collective-permute-done.27.late_came
  311.7 6.4 %sum_blocks.1 = (bf16[2,3,2,96,768]{4,3,2,1,0:T(8,128)(2,1)}, bf16[2,3,2,96,768]{4,3,2,1,0:T(8,128)(2,1)}, bf16[3,2,2,96,768]{4,3,2,1,0:T(8,128)(2,1)}, bf16[3,2,2,96,768]{4,3,2,1,0:T(8,128)(2,1)}) custom-call(s32[2]{0:T(128)S(1)} %get-tuple-element.219.left_at, s32[2]{0:T(128)S(1)} %get-tuple-element.220.late_at, s32[1]{0:T(128)} %bitcast.60.y_at, ...), custom_call_target="tpu_custom_call" | custom-call | flops 1 | bytes 1 | tf_op jit(solution)/shard_map/sum_blocks/pallas_call | solution.py:358
  318.2 10.2 %back_patches.3 = (bf16[32,32,256]{2,1,0:T(8,128)(2,1)S(1)}, bf16[32,32,256]{2,1,0:T(8,128)(2,1)}, bf16[32,32,256]{2,1,0:T(8,128)(2,1)}, bf16[32,32,256]{2,1,0:T(8,128)(2,1)}) custom-call(bf16[128,768]{1,0:T(8,128)(2,1)S(1)} %get-tuple-element.156.g0.refs_8_, bf16[128,768]{1,0:T(8,128)(2,1)S(1)} %copy-done.5, bf16[128,768]{1,0:T(8,128)(2,1)S(1)} %copy-done.3, ...), custom_call_target="tpu_custom_call" | custom-call | flops 1 | bytes 1 | tf_op jit(solution)/shard_map/back_patches/pallas_call | solution.py:127
  328.4 7.6 %collective-permute-done.31.g1 = bf16[32,96,256]{2,1,0:T(8,128)(2,1)} collective-permute-done((bf16[32,96,256]{2,1,0:T(8,128)(2,1)}, bf16[32,96,256]{2,1,0:T(8,128)(2,1)}, u32[]{:S(2)}, u32[]{:S(2)}) %collective-permute-start.31) | collective-permute-done | bytes 1572896 | tf_op jit(solution)/shard_map/ppermute | solution.py:439
  337.9 33.0 %collective-permute-done.33.g3 = bf16[32,96,256]{2,1,0:T(8,128)(2,1)} collective-permute-done((bf16[32,96,256]{2,1,0:T(8,128)(2,1)}, bf16[32,96,256]{2,1,0:T(8,128)(2,1)}, u32[]{:S(2)}, u32[]{:S(2)}) %collective-permute-start.33) | collective-permute-done | bytes 1572896 | tf_op jit(solution)/shard_map/ppermute | solution.py:447
  380.5 14.4 %pixel_back.2 = (bf16[202,128,256]{2,1,0:T(8,128)(2,1)}, f32[202,128]{1,0:T(8,128)S(1)}) custom-call(bf16[202,128]{1,0:T(8,128)(2,1)S(1)} %copy-done.13, bf16[202,128,256]{2,1,0:T(8,128)(2,1)} %bitcast.325, bf16[32,96,256]{2,1,0:T(8,128)(2,1)S(1)} %copy-done.7, bf16[32,96,256]{2,1,0:T(8,128)(2,1)} %collective-permute-done.31.g1, ...), custom_call_target="tpu_custom_call" | custom-call | flops 1 | bytes 1 | tf_op jit(solution)/shard_map/pixel_back/pallas_call | solution.py:194
  394.9 42.6 %collective-permute-done.35.g1 = bf16[32,32,256]{2,1,0:T(8,128)(2,1)S(1)} collective-permute-done((bf16[32,32,256]{2,1,0:T(8,128)(2,1)}, bf16[32,32,256]{2,1,0:T(8,128)(2,1)S(1)}, u32[]{:S(2)}, u32[]{:S(2)}) %collective-permute-start.35) | collective-permute-done | bytes 524320 | tf_op jit(solution)/shard_map/ppermute | solution.py:439
  437.6 2.3 fusion.43
  441.1 2.5 fusion.44
  445.9 7.1 %pixel_back.3 = (bf16[202,128,256]{2,1,0:T(8,128)(2,1)}, f32[202,128]{1,0:T(8,128)S(1)}) custom-call(bf16[202,128]{1,0:T(8,128)(2,1)S(1)} %copy-done.13, bf16[202,128,256]{2,1,0:T(8,128)(2,1)} %bitcast.326, bf16[32,32,256]{2,1,0:T(8,128)(2,1)S(1)} %get-tuple-element.175.g0, ...), custom_call_target="tpu_custom_call", output_to_operand_aliasing={{0}: (6, {})} | custom-call | flops 1 | bytes 1 | tf_op jit(solution)/shard_map/pixel_back/pallas_call | solution.py:194
  452.9 6.5 %collective-permute-done.40 = bf16[3,2,96,768]{3,2,0,1:T(8,128)(2,1)S(1)} collective-permute-done((bf16[3,2,96,768]{3,2,0,1:T(8,128)(2,1)}, bf16[3,2,96,768]{3,2,0,1:T(8,128)(2,1)S(1)}, u32[]{:S(2)}, u32[]{:S(2)}) %collective-permute-start.40) | collective-permute-done | bytes 884768 | tf_op jit(solution)/shard_map/ppermute | solution.py:435
  459.4 3.8 collective-permute-done.41
  463.3 2.2 fusion.2
  468.9 3.7 collective-permute-start.47
  474.2 3.6 collective-permute-done.43
  478.7 4.1 collective-permute-start.48
  486.8 7.0 %collective-permute-done.48 = bf16[3,96,768]{2,1,0:T(8,128)(2,1)S(1)} collective-permute-done((bf16[3,96,768]{2,1,0:T(8,128)(2,1)S(1)}, bf16[3,96,768]{2,1,0:T(8,128)(2,1)S(1)}, u32[]{:S(2)}, u32[]{:S(2)}) %collective-permute-start.48) | collective-permute-done | bytes 442400 | tf_op jit(solution)/shard_map/ppermute | solution.py:495
  495.6 7.0 %collective-permute-done.46 = bf16[3,96,768]{2,1,0:T(8,128)(2,1)S(1)} collective-permute-done((bf16[3,96,768]{2,1,0:T(8,128)(2,1)S(1)}, bf16[3,96,768]{2,1,0:T(8,128)(2,1)S(1)}, u32[]{:S(2)}, u32[]{:S(2)}) %collective-permute-start.46) | collective-permute-done | bytes 442400 | tf_op jit(solution)/shard_map/ppermute | solution.py:494
  502.9 2.3 put_parts.4.refs_2_
  505.3 2.3 put_parts.5.refs_2_
  512.4 2.6 collective-permute-start.52
  516.6 6.9 %collective-permute-done.55.refs_0_ = bf16[512,768]{1,0:T(8,128)(2,1)S(1)} collective-permute-done((bf16[512,768]{1,0:T(8,128)(2,1)S(1)}, bf16[512,768]{1,0:T(8,128)(2,1)S(1)}, u32[]{:S(2)}, u32[]{:S(2)}) %collective-permute-start.55) | collective-permute-done | bytes 786464 | tf_op jit(solution)/shard_map/ppermute | solution.py:435
  524.1 6.8 %collective-permute-done.58 = bf16[3,96,768]{2,1,0:T(8,128)(2,1)S(1)} collective-permute-done((bf16[3,96,768]{2,1,0:T(8,128)(2,1)S(1)}, bf16[3,96,768]{2,1,0:T(8,128)(2,1)S(1)}, u32[]{:S(2)}, u32[]{:S(2)}) %collective-permute-start.58) | collective-permute-done | bytes 442400 | tf_op jit(solution)/shard_map/ppermute | solution.py:435
  533.6 3.3 give_pieces.1
  536.9 2.3 put_parts.6.refs_2_
  539.2 2.3 put_parts.7
  (491 shorter events, 123.5 us)
Async XLA Ops:
  7.2 161.7 %all-gather.2.cloned.1.call-start = ((), (), s32[]{:S(2)}) async-start(), calls=%async_computation.2 | async-start | bytes 14155776 | tf_op jit(solution)/shard_map/all_gather | solution.py:600
  10.0 453.2 %reduce-scatter.5.cloned.1.call-start = ((), (), s32[]{:S(2)}) async-start(), calls=%async_computation.4 | async-start | bytes 3932160 | tf_op jit(solution)/shard_map/reduce_scatter | solution.py:736
  24.4 68.5 %collective-permute-start.4 = (bf16[32,128,256]{2,1,0:T(8,128)(2,1)S(1)}, bf16[32,128,256]{2,1,0:T(8,128)(2,1)}, u32[]{:S(2)}, u32[]{:S(2)}) collective-permute-start(bf16[32,128,256]{2,1,0:T(8,128)(2,1)S(1)} %get-tuple-element.109), channel_id=1, source_target_pairs={{0,1},{1,0},{2,3},{3,2},{4,5},{5,4},{6,7},{7,6},{8,9},{9,8},{10,11... | collective-permute-start | bytes 6291464 | tf_op jit(solution)/shard_map/ppermute | solution.py:439
  27.5 65.4 %collective-permute-start.5 = (bf16[32,128,256]{2,1,0:T(8,128)(2,1)}, bf16[32,128,256]{2,1,0:T(8,128)(2,1)}, u32[]{:S(2)}, u32[]{:S(2)}) collective-permute-start(bf16[32,128,256]{2,1,0:T(8,128)(2,1)} %get-tuple-element.110), channel_id=1, source_target_pairs={{0,16},{16,0},{1,17},{17,1},{2,18},{18,2},{3,19},{19,3},{4,20},{20... | collective-permute-start | bytes 6291464 | tf_op jit(solution)/shard_map/ppermute | solution.py:435
  29.0 90.6 %collective-permute-start.6 = (bf16[32,128,256]{2,1,0:T(8,128)(2,1)}, bf16[32,128,256]{2,1,0:T(8,128)(2,1)}, u32[]{:S(2)}, u32[]{:S(2)}) collective-permute-start(bf16[32,128,256]{2,1,0:T(8,128)(2,1)} %get-tuple-element.111), channel_id=1, source_target_pairs={{0,17},{1,16},{16,1},{17,0},{2,19},{3,18},{18,3},{19,2},{4,21},{5,... | collective-permute-start | bytes 6291464 | tf_op jit(solution)/shard_map/ppermute | solution.py:447
  29.2 42.3 %collective-permute-start.1 = (bf16[3,96,768]{2,1,0:T(8,128)(2,1)S(1)}, bf16[3,96,768]{2,1,0:T(8,128)(2,1)S(1)}, u32[]{:S(2)}, u32[]{:S(2)}) collective-permute-start(bf16[3,96,768]{2,1,0:T(8,128)(2,1)S(1)} %take_pieces.1), channel_id=1, source_target_pairs={{0,6},{2,0},{4,2},{6,4},{1,7},{3,1},{5,3},{7,5},{8,14},{10,8},{12,... | collective-permute-start | bytes 1327112 | tf_op jit(solution)/shard_map/ppermute | solution.py:465
  33.3 39.9 %collective-permute-start = (bf16[3,96,768]{2,1,0:T(8,128)(2,1)S(1)}, bf16[3,96,768]{2,1,0:T(8,128)(2,1)S(1)}, u32[]{:S(2)}, u32[]{:S(2)}) collective-permute-start(bf16[3,96,768]{2,1,0:T(8,128)(2,1)S(1)} %take_pieces.1), channel_id=1, source_target_pairs={{0,2},{2,4},{4,6},{6,0},{1,3},{3,5},{5,7},{7,1},{8,10},{10,12},{12... | collective-permute-start | bytes 1327112 | tf_op jit(solution)/shard_map/ppermute | solution.py:465
  71.5 21.3 %collective-permute-start.3 = (bf16[3,48,768]{2,1,0:T(8,128)(2,1)S(1)}, bf16[3,48,768]{2,1,0:T(8,128)(2,1)S(1)}, u32[]{:S(2)}, u32[]{:S(2)}) collective-permute-start(bf16[3,48,768]{2,1,0:T(8,128)(2,1)S(1)} %slice.224), channel_id=1, source_target_pairs={{0,6},{2,0},{4,2},{6,4},{1,7},{3,1},{5,3},{7,5},{8,14},{10,8},{12,... | collective-permute-start | bytes 663560 | tf_op jit(solution)/shard_map/ppermute | solution.py:476
  73.2 19.6 %collective-permute-start.2 = (bf16[3,48,768]{2,1,0:T(8,128)(2,1)S(1)}, bf16[3,48,768]{2,1,0:T(8,128)(2,1)S(1)}, u32[]{:S(2)}, u32[]{:S(2)}) collective-permute-start(bf16[3,48,768]{2,1,0:T(8,128)(2,1)S(1)} %slice.223), channel_id=1, source_target_pairs={{0,2},{2,4},{4,6},{6,0},{1,3},{3,5},{5,7},{7,1},{8,10},{10,12},{12... | collective-permute-start | bytes 663560 | tf_op jit(solution)/shard_map/ppermute | solution.py:475
  120.6 20.8 %collective-permute-start.7 = (bf16[2,3,96,768]{3,2,1,0:T(8,128)(2,1)}, bf16[2,3,96,768]{3,2,1,0:T(8,128)(2,1)}, u32[]{:S(2)}, u32[]{:S(2)}) collective-permute-start(bf16[2,3,96,768]{3,2,1,0:T(8,128)(2,1)} %slice.179), channel_id=1, source_target_pairs={{0,1},{1,0},{2,3},{3,2},{4,5},{5,4},{6,7},{7,6},{8,9},{9,8},{10,11... | collective-permute-start | bytes 2654216 | tf_op jit(solution)/shard_map/ppermute | solution.py:439
  122.5 21.6 %collective-permute-start.9 = (bf16[2,3,96,768]{3,2,0,1:T(8,128)(2,1)S(1)}, bf16[2,3,96,768]{3,2,0,1:T(8,128)(2,1)S(1)}, u32[]{:S(2)}, u32[]{:S(2)}) collective-permute-start(bf16[2,3,96,768]{3,2,0,1:T(8,128)(2,1)S(1)} %slice.226), channel_id=1, source_target_pairs={{0,16},{16,0},{1,17},{17,1},{2,18},{18,2},{3,19},{19,3},{4,20},{20... | collective-permute-start | bytes 2654216 | tf_op jit(solution)/shard_map/ppermute | solution.py:435
  142.7 13.3 %collective-permute-start.8 = (bf16[1,384,768]{2,1,0:T(8,128)(2,1)S(1)}, bf16[1,384,768]{2,1,0:T(8,128)(2,1)S(1)}, u32[]{:S(2)}, u32[]{:S(2)}) collective-permute-start(bf16[1,384,768]{2,1,0:T(8,128)(2,1)S(1)} %bitcast.335), channel_id=1, source_target_pairs={{0,16},{16,0},{1,17},{17,1},{2,18},{18,2},{3,19},{19,3},{4,20},{20... | collective-permute-start | bytes 1769480 | tf_op jit(solution)/shard_map/ppermute | solution.py:435
  144.1 12.7 %collective-permute-start.10 = (bf16[2,2,1,96,768]{4,3,2,1,0:T(8,128)(2,1)S(1)}, bf16[2,2,1,96,768]{4,3,2,1,0:T(8,128)(2,1)S(1)}, u32[]{:S(2)}, u32[]{:S(2)}) collective-permute-start(bf16[2,2,1,96,768]{4,3,2,1,0:T(8,128)(2,1)S(1)} %pad_maximum_fusion.12), channel_id=1, source_target_pairs={{0,1},{1,0},{2,3},{3,2},{4,5},{5,4},{6,7},{7,6},{8,9},{9,8},{10,11... | collective-permute-start | bytes 1769480 | tf_op jit(solution)/shard_map/ppermute | solution.py:439
  158.3 24.2 %collective-permute-start.14 = (bf16[768,768]{1,0:T(8,128)(2,1)}, bf16[768,768]{1,0:T(8,128)(2,1)}, u32[]{:S(2)}, u32[]{:S(2)}) collective-permute-start(bf16[768,768]{1,0:T(8,128)(2,1)} %get-tuple-element.252), channel_id=1, source_target_pairs={{0,8},{8,0},{1,9},{9,1},{2,10},{10,2},{3,11},{11,3},{4,12},{12,4},... | collective-permute-start | bytes 3538952 | tf_op jit(solution)/shard_map/ppermute | solution.py:431
  159.5 25.0 %collective-permute-start.15 = (bf16[768,768]{1,0:T(8,128)(2,1)}, bf16[768,768]{1,0:T(8,128)(2,1)}, u32[]{:S(2)}, u32[]{:S(2)}) collective-permute-start(bf16[768,768]{1,0:T(8,128)(2,1)} %get-tuple-element.254), channel_id=1, source_target_pairs={{0,8},{8,0},{1,9},{9,1},{2,10},{10,2},{3,11},{11,3},{4,12},{12,4},... | collective-permute-start | bytes 3538952 | tf_op jit(solution)/shard_map/ppermute | solution.py:431
  162.3 37.5 %collective-permute-start.16 = (bf16[2,384,768]{2,1,0:T(8,128)(2,1)}, bf16[2,384,768]{2,1,0:T(8,128)(2,1)}, u32[]{:S(2)}, u32[]{:S(2)}) collective-permute-start(bf16[2,384,768]{2,1,0:T(8,128)(2,1)} %pad_maximum_fusion.3), channel_id=1, source_target_pairs={{0,16},{16,0},{1,17},{17,1},{2,18},{18,2},{3,19},{19,3},{4,20},{20... | collective-permute-start | bytes 3538952 | tf_op jit(solution)/shard_map/ppermute | solution.py:435
  163.3 36.5 %collective-permute-start.17 = (bf16[2,2,2,96,768]{4,3,2,1,0:T(8,128)(2,1)}, bf16[2,2,2,96,768]{4,3,2,1,0:T(8,128)(2,1)}, u32[]{:S(2)}, u32[]{:S(2)}) collective-permute-start(bf16[2,2,2,96,768]{4,3,2,1,0:T(8,128)(2,1)} %pad_maximum_fusion.2), channel_id=1, source_target_pairs={{0,1},{1,0},{2,3},{3,2},{4,5},{5,4},{6,7},{7,6},{8,9},{9,8},{10,11... | collective-permute-start | bytes 3538952 | tf_op jit(solution)/shard_map/ppermute | solution.py:439
  181.5 18.1 %collective-permute-start.11 = (bf16[128,768]{1,0:T(8,128)(2,1)S(1)}, bf16[128,768]{1,0:T(8,128)(2,1)S(1)}, u32[]{:S(2)}, u32[]{:S(2)}) collective-permute-start(bf16[128,768]{1,0:T(8,128)(2,1)S(1)} %get-tuple-element.255), channel_id=1, source_target_pairs={{0,1},{1,0},{2,3},{3,2},{4,5},{5,4},{6,7},{7,6},{8,9},{9,8},{10,11... | collective-permute-start | bytes 589832 | tf_op jit(solution)/shard_map/ppermute | solution.py:439
  182.5 17.0 %collective-permute-start.13 = (bf16[128,768]{1,0:T(8,128)(2,1)S(1)}, bf16[128,768]{1,0:T(8,128)(2,1)S(1)}, u32[]{:S(2)}, u32[]{:S(2)}) collective-permute-start(bf16[128,768]{1,0:T(8,128)(2,1)S(1)} %get-tuple-element.256), channel_id=1, source_target_pairs={{0,17},{1,16},{16,1},{17,0},{2,19},{3,18},{18,3},{19,2},{4,21},{5,... | collective-permute-start | bytes 589832 | tf_op jit(solution)/shard_map/ppermute | solution.py:447
  184.5 15.0 %collective-permute-start.12 = (bf16[128,768]{1,0:T(8,128)(2,1)S(1)}, bf16[128,768]{1,0:T(8,128)(2,1)S(1)}, u32[]{:S(2)}, u32[]{:S(2)}) collective-permute-start(bf16[128,768]{1,0:T(8,128)(2,1)S(1)} %get-tuple-element.257), channel_id=1, source_target_pairs={{0,16},{16,0},{1,17},{17,1},{2,18},{18,2},{3,19},{19,3},{4,20},{20... | collective-permute-start | bytes 589832 | tf_op jit(solution)/shard_map/ppermute | solution.py:435
  213.5 12.9 %collective-permute-start.21 = (bf16[768,768]{1,0:T(8,128)(2,1)S(1)}, bf16[768,768]{1,0:T(8,128)(2,1)S(1)}, u32[]{:S(2)}, u32[]{:S(2)}) collective-permute-start(bf16[768,768]{1,0:T(8,128)(2,1)S(1)} %pad_maximum_fusion.9), channel_id=1, source_target_pairs={{0,8},{8,0},{1,9},{9,1},{2,10},{10,2},{3,11},{11,3},{4,12},{12,4},... | collective-permute-start | bytes 3538952 | tf_op jit(solution)/shard_map/ppermute | solution.py:431
  216.9 42.1 %collective-permute-start.23 = (bf16[32,128,256]{2,1,0:T(8,128)(2,1)}, bf16[32,128,256]{2,1,0:T(8,128)(2,1)}, u32[]{:S(2)}, u32[]{:S(2)}) collective-permute-start(bf16[32,128,256]{2,1,0:T(8,128)(2,1)} %get-tuple-element.130.a0.refs_0_), channel_id=1, source_target_pairs={{0,8},{8,0},{1,9},{9,1},{2,10},{10,2},{3,11},{11,3},{4,12},{12,4},... | collective-permute-start | bytes 6291464 | tf_op jit(solution)/shard_map/ppermute | solution.py:431
  222.9 36.1 %collective-permute-start.24 = (bf16[32,128,256]{2,1,0:T(8,128)(2,1)}, bf16[32,128,256]{2,1,0:T(8,128)(2,1)}, u32[]{:S(2)}, u32[]{:S(2)}) collective-permute-start(bf16[32,128,256]{2,1,0:T(8,128)(2,1)} %collective-permute-done.4.a1.refs_1_), channel_id=1, source_target_pairs={{0,8},{8,0},{1,9},{9,1},{2,10},{10,2},{3,11},{11,3},{4,12},{12,4},... | collective-permute-start | bytes 6291464 | tf_op jit(solution)/shard_map/ppermute | solution.py:431
  223.5 35.6 %collective-permute-start.25 = (bf16[32,128,256]{2,1,0:T(8,128)(2,1)}, bf16[32,128,256]{2,1,0:T(8,128)(2,1)}, u32[]{:S(2)}, u32[]{:S(2)}) collective-permute-start(bf16[32,128,256]{2,1,0:T(8,128)(2,1)} %collective-permute-done.5.a2.refs_2_), channel_id=1, source_target_pairs={{0,8},{8,0},{1,9},{9,1},{2,10},{10,2},{3,11},{11,3},{4,12},{12,4},... | collective-permute-start | bytes 6291464 | tf_op jit(solution)/shard_map/ppermute | solution.py:431
  224.3 34.7 %collective-permute-start.26 = (bf16[32,128,256]{2,1,0:T(8,128)(2,1)}, bf16[32,128,256]{2,1,0:T(8,128)(2,1)}, u32[]{:S(2)}, u32[]{:S(2)}) collective-permute-start(bf16[32,128,256]{2,1,0:T(8,128)(2,1)} %collective-permute-done.6.a3.refs_3_), channel_id=1, source_target_pairs={{0,8},{8,0},{1,9},{9,1},{2,10},{10,2},{3,11},{11,3},{4,12},{12,4},... | collective-permute-start | bytes 6291464 | tf_op jit(solution)/shard_map/ppermute | solution.py:431
  232.4 26.7 %collective-permute-start.22 = (bf16[8,128,768]{2,1,0:T(8,128)(2,1)}, bf16[8,128,768]{2,1,0:T(8,128)(2,1)S(1)}, u32[]{:S(2)}, u32[]{:S(2)}) collective-permute-start(bf16[8,128,768]{2,1,0:T(8,128)(2,1)} %copy-done.44), channel_id=1, source_target_pairs={{0,8},{8,0},{1,9},{9,1},{2,10},{10,2},{3,11},{11,3},{4,12},{12,4},... | collective-permute-start | bytes 4718600 | tf_op jit(solution)/shard_map/ppermute | solution.py:431
  298.5 164.7 %reduce-scatter.3.cloned.1.call-start = ((), (), s32[]{:S(2)}) async-start(), calls=%async_computation.3 | async-start | bytes 3932160 | tf_op jit(solution)/shard_map/reduce_scatter | solution.py:736
  299.2 36.8 %collective-permute-start.31 = (bf16[32,96,256]{2,1,0:T(8,128)(2,1)}, bf16[32,96,256]{2,1,0:T(8,128)(2,1)}, u32[]{:S(2)}, u32[]{:S(2)}) collective-permute-start(bf16[32,96,256]{2,1,0:T(8,128)(2,1)} %copy-done.17), channel_id=1, source_target_pairs={{0,1},{1,0},{2,3},{3,2},{4,5},{5,4},{6,7},{7,6},{8,9},{9,8},{10,11... | collective-permute-start | bytes 4718600 | tf_op jit(solution)/shard_map/ppermute | solution.py:439
  300.3 37.6 %collective-permute-start.32 = (bf16[32,96,256]{2,1,0:T(8,128)(2,1)}, bf16[32,96,256]{2,1,0:T(8,128)(2,1)}, u32[]{:S(2)}, u32[]{:S(2)}) collective-permute-start(bf16[32,96,256]{2,1,0:T(8,128)(2,1)} %copy-done.16), channel_id=1, source_target_pairs={{0,16},{16,0},{1,17},{17,1},{2,18},{18,2},{3,19},{19,3},{4,20},{20... | collective-permute-start | bytes 4718600 | tf_op jit(solution)/shard_map/ppermute | solution.py:435
  301.9 69.0 %collective-permute-start.33 = (bf16[32,96,256]{2,1,0:T(8,128)(2,1)}, bf16[32,96,256]{2,1,0:T(8,128)(2,1)}, u32[]{:S(2)}, u32[]{:S(2)}) collective-permute-start(bf16[32,96,256]{2,1,0:T(8,128)(2,1)} %get-tuple-element.145), channel_id=1, source_target_pairs={{0,17},{1,16},{16,1},{17,0},{2,19},{3,18},{18,3},{19,2},{4,21},{5,... | collective-permute-start | bytes 4718600 | tf_op jit(solution)/shard_map/ppermute | solution.py:447
  374.4 63.1 %collective-permute-start.39 = (bf16[3,2,2,96,768]{4,3,0,1,2:T(8,128)(2,1)}, bf16[3,2,2,96,768]{4,3,0,1,2:T(8,128)(2,1)}, u32[]{:S(2)}, u32[]{:S(2)}) collective-permute-start(bf16[3,2,2,96,768]{4,3,0,1,2:T(8,128)(2,1)} %copy.173), channel_id=1, source_target_pairs={{0,16},{16,0},{1,17},{17,1},{2,18},{18,2},{3,19},{19,3},{4,20},{20... | collective-permute-start | bytes 5308424 | tf_op jit(solution)/shard_map/ppermute | solution.py:435
  375.7 61.9 %collective-permute-start.38 = (bf16[2,3,2,96,768]{4,3,1,2,0:T(8,128)(2,1)}, bf16[2,3,2,96,768]{4,3,1,2,0:T(8,128)(2,1)}, u32[]{:S(2)}, u32[]{:S(2)}) collective-permute-start(bf16[2,3,2,96,768]{4,3,1,2,0:T(8,128)(2,1)} %copy.172), channel_id=1, source_target_pairs={{0,1},{1,0},{2,3},{3,2},{4,5},{5,4},{6,7},{7,6},{8,9},{9,8},{10,11... | collective-permute-start | bytes 5308424 | tf_op jit(solution)/shard_map/ppermute | solution.py:439
  377.0 60.5 %collective-permute-start.35 = (bf16[32,32,256]{2,1,0:T(8,128)(2,1)}, bf16[32,32,256]{2,1,0:T(8,128)(2,1)S(1)}, u32[]{:S(2)}, u32[]{:S(2)}) collective-permute-start(bf16[32,32,256]{2,1,0:T(8,128)(2,1)} %get-tuple-element.165), channel_id=1, source_target_pairs={{0,1},{1,0},{2,3},{3,2},{4,5},{5,4},{6,7},{7,6},{8,9},{9,8},{10,11... | collective-permute-start | bytes 1572872 | tf_op jit(solution)/shard_map/ppermute | solution.py:439
  377.7 59.9 %collective-permute-start.36 = (bf16[32,32,256]{2,1,0:T(8,128)(2,1)}, bf16[32,32,256]{2,1,0:T(8,128)(2,1)S(1)}, u32[]{:S(2)}, u32[]{:S(2)}) collective-permute-start(bf16[32,32,256]{2,1,0:T(8,128)(2,1)} %get-tuple-element.166), channel_id=1, source_target_pairs={{0,16},{16,0},{1,17},{17,1},{2,18},{18,2},{3,19},{19,3},{4,20},{20... | collective-permute-start | bytes 1572872 | tf_op jit(solution)/shard_map/ppermute | solution.py:435
  378.5 59.1 %collective-permute-start.37 = (bf16[32,32,256]{2,1,0:T(8,128)(2,1)}, bf16[32,32,256]{2,1,0:T(8,128)(2,1)}, u32[]{:S(2)}, u32[]{:S(2)}) collective-permute-start(bf16[32,32,256]{2,1,0:T(8,128)(2,1)} %get-tuple-element.167), channel_id=1, source_target_pairs={{0,17},{1,16},{16,1},{17,0},{2,19},{3,18},{18,3},{19,2},{4,21},{5,... | collective-permute-start | bytes 1572872 | tf_op jit(solution)/shard_map/ppermute | solution.py:447
  439.9 19.5 %collective-permute-start.40 = (bf16[3,2,96,768]{3,2,0,1:T(8,128)(2,1)}, bf16[3,2,96,768]{3,2,0,1:T(8,128)(2,1)S(1)}, u32[]{:S(2)}, u32[]{:S(2)}) collective-permute-start(bf16[3,2,96,768]{3,2,0,1:T(8,128)(2,1)} %fusion.43), channel_id=1, source_target_pairs={{0,16},{16,0},{1,17},{17,1},{2,18},{18,2},{3,19},{19,3},{4,20},{20... | collective-permute-start | bytes 2654216 | tf_op jit(solution)/shard_map/ppermute | solution.py:435
  443.6 19.6 %collective-permute-start.41 = (bf16[3,2,96,768]{3,2,0,1:T(8,128)(2,1)}, bf16[3,2,96,768]{3,2,0,1:T(8,128)(2,1)}, u32[]{:S(2)}, u32[]{:S(2)}) collective-permute-start(bf16[3,2,96,768]{3,2,0,1:T(8,128)(2,1)} %fusion.44), channel_id=1, source_target_pairs={{0,1},{1,0},{2,3},{3,2},{4,5},{5,4},{6,7},{7,6},{8,9},{9,8},{10,11... | collective-permute-start | bytes 2654216 | tf_op jit(solution)/shard_map/ppermute | solution.py:439
  473.4 31.9 %collective-permute-start.49 = (bf16[512,768]{1,0:T(8,128)(2,1)S(1)}, bf16[512,768]{1,0:T(8,128)(2,1)S(1)}, u32[]{:S(2)}, u32[]{:S(2)}) collective-permute-start(bf16[512,768]{1,0:T(8,128)(2,1)S(1)} %copy-done.8), channel_id=1, source_target_pairs={{0,8},{8,0},{1,9},{9,1},{2,10},{10,2},{3,11},{11,3},{4,12},{12,4},... | collective-permute-start | bytes 2359304 | tf_op jit(solution)/shard_map/ppermute | solution.py:431
  473.4 29.5 %collective-permute-start.50 = (bf16[512,768]{1,0:T(8,128)(2,1)S(1)}, bf16[512,768]{1,0:T(8,128)(2,1)S(1)}, u32[]{:S(2)}, u32[]{:S(2)}) collective-permute-start(bf16[512,768]{1,0:T(8,128)(2,1)S(1)} %copy-done.9), channel_id=1, source_target_pairs={{0,8},{8,0},{1,9},{9,1},{2,10},{10,2},{3,11},{11,3},{4,12},{12,4},... | collective-permute-start | bytes 2359304 | tf_op jit(solution)/shard_map/ppermute | solution.py:431
  478.7 15.1 %collective-permute-start.48 = (bf16[3,96,768]{2,1,0:T(8,128)(2,1)S(1)}, bf16[3,96,768]{2,1,0:T(8,128)(2,1)S(1)}, u32[]{:S(2)}, u32[]{:S(2)}) collective-permute-start(bf16[3,96,768]{2,1,0:T(8,128)(2,1)S(1)} %pad_maximum_fusion.23), channel_id=1, source_target_pairs={{0,6},{2,0},{4,2},{6,4},{1,7},{3,1},{5,3},{7,5},{8,14},{10,8},{12,... | collective-permute-start | bytes 1327112 | tf_op jit(solution)/shard_map/ppermute | solution.py:495
  484.4 18.2 %collective-permute-start.46 = (bf16[3,96,768]{2,1,0:T(8,128)(2,1)S(1)}, bf16[3,96,768]{2,1,0:T(8,128)(2,1)S(1)}, u32[]{:S(2)}, u32[]{:S(2)}) collective-permute-start(bf16[3,96,768]{2,1,0:T(8,128)(2,1)S(1)} %pad_maximum_fusion.22), channel_id=1, source_target_pairs={{0,2},{2,4},{4,6},{6,0},{1,3},{3,5},{5,7},{7,1},{8,10},{10,12},{12... | collective-permute-start | bytes 1327112 | tf_op jit(solution)/shard_map/ppermute | solution.py:494
  486.1 30.0 %collective-permute-start.53 = (bf16[512,768]{1,0:T(8,128)(2,1)S(1)}, bf16[512,768]{1,0:T(8,128)(2,1)S(1)}, u32[]{:S(2)}, u32[]{:S(2)}) collective-permute-start(bf16[512,768]{1,0:T(8,128)(2,1)S(1)} %copy-done.8), channel_id=1, source_target_pairs={{0,16},{16,0},{1,17},{17,1},{2,18},{18,2},{3,19},{19,3},{4,20},{20... | collective-permute-start | bytes 2359304 | tf_op jit(solution)/shard_map/ppermute | solution.py:435
  493.8 29.7 %collective-permute-start.55 = (bf16[512,768]{1,0:T(8,128)(2,1)S(1)}, bf16[512,768]{1,0:T(8,128)(2,1)S(1)}, u32[]{:S(2)}, u32[]{:S(2)}) collective-permute-start(bf16[512,768]{1,0:T(8,128)(2,1)S(1)} %copy-done.9), channel_id=1, source_target_pairs={{0,16},{16,0},{1,17},{17,1},{2,18},{18,2},{3,19},{19,3},{4,20},{20... | collective-permute-start | bytes 2359304 | tf_op jit(solution)/shard_map/ppermute | solution.py:435
  509.6 21.4 %collective-permute-start.58 = (bf16[3,96,768]{2,1,0:T(8,128)(2,1)S(1)}, bf16[3,96,768]{2,1,0:T(8,128)(2,1)S(1)}, u32[]{:S(2)}, u32[]{:S(2)}) collective-permute-start(bf16[3,96,768]{2,1,0:T(8,128)(2,1)S(1)} %fusion.48), channel_id=1, source_target_pairs={{0,16},{16,0},{1,17},{17,1},{2,18},{18,2},{3,19},{19,3},{4,20},{20... | collective-permute-start | bytes 1327112 | tf_op jit(solution)/shard_map/ppermute | solution.py:435
  512.4 11.1 %collective-permute-start.52 = (f32[208,128]{1,0:T(8,128)S(1)}, f32[208,128]{1,0:T(8,128)S(1)}, u32[]{:S(2)}, u32[]{:S(2)}) collective-permute-start(f32[208,128]{1,0:T(8,128)S(1)} %add.531), channel_id=1, source_target_pairs={{0,4},{2,6},{4,0},{6,2},{1,5},{3,7},{5,1},{7,3},{8,12},{10,14},{12... | collective-permute-start | bytes 319496 | tf_op jit(solution)/shard_map/ppermute | solution.py:510
  516.1 16.0 %collective-permute-start.57 = (bf16[3,96,768]{2,1,0:T(8,128)(2,1)S(1)}, bf16[3,96,768]{2,1,0:T(8,128)(2,1)S(1)}, u32[]{:S(2)}, u32[]{:S(2)}) collective-permute-start(bf16[3,96,768]{2,1,0:T(8,128)(2,1)S(1)} %fusion.48), channel_id=1, source_target_pairs={{0,8},{8,0},{1,9},{9,1},{2,10},{10,2},{3,11},{11,3},{4,12},{12,4},... | collective-permute-start | bytes 1327112 | tf_op jit(solution)/shard_map/ppermute | solution.py:431
  516.1 23.1 %collective-permute-start.54 = (bf16[512,768]{1,0:T(8,128)(2,1)S(1)}, bf16[512,768]{1,0:T(8,128)(2,1)S(1)}, u32[]{:S(2)}, u32[]{:S(2)}) collective-permute-start(bf16[512,768]{1,0:T(8,128)(2,1)S(1)} %collective-permute-done.53.refs_0_), channel_id=1, source_target_pairs={{0,8},{8,0},{1,9},{9,1},{2,10},{10,2},{3,11},{11,3},{4,12},{12,4},... | collective-permute-start | bytes 2359304 | tf_op jit(solution)/shard_map/ppermute | solution.py:431
  523.5 13.4 %collective-permute-start.56 = (bf16[512,768]{1,0:T(8,128)(2,1)S(1)}, bf16[512,768]{1,0:T(8,128)(2,1)S(1)}, u32[]{:S(2)}, u32[]{:S(2)}) collective-permute-start(bf16[512,768]{1,0:T(8,128)(2,1)S(1)} %collective-permute-done.55.refs_0_), channel_id=1, source_target_pairs={{0,8},{8,0},{1,9},{9,1},{2,10},{10,2},{3,11},{11,3},{4,12},{12,4},... | collective-permute-start | bytes 2359304 | tf_op jit(solution)/shard_map/ppermute | solution.py:431
  (127 other events, 810.5 us)
Sparse Core Ops, SparseCore 0:
  10.1 147.6 all-gather.1
  298.6 61.1 reduce-scatter.4
  362.6 60.2 reduce-scatter.2
